TPU v7x, 256 devices: a whole 4x4x8 slice. The times are simulated.
256 devices in a mesh: sec: 2 (over core), tile: 32 (over y, z), harm: 4 (over x).
Axes of the slice: x: 4, y: 4, z: 8, core: 2. Of those that a mesh axis runs over, the one named last changes fastest.
Arguments:
- state: float32 [2, 3, 16, 8192, 256], P('sec', None, 'harm', 'tile'), may hold values from -6 to 6
- forcing: float32 [2, 2, 16, 8192, 256], P('sec', None, 'harm', 'tile'), may hold values from -6 to 6
- depth: float32 [2, 8192, 256], P('sec', 'tile'), may hold values from 0.2 to 2
- wet_mask: int32 [2, 8192, 256], P('sec', 'tile'), may hold values 0 or 1
- nest_index: int32 [8192], P('tile'), may hold values from 0 to 65535
- freq_order: int32 [16], replicated, may hold values from 0 to 15, each once
Outputs:
- new_state: float32 [2, 3, 16, 8192, 256], P('sec', None, 'harm', 'tile')
Inputs may be any that keep to these rules, and one draw needn't show every extreme that they name: `freq_order`: each index of the frequency table appears once.
All inputs are finite; a program needn't handle non-finite values. No bound on the sum of `wet_mask` on one device may be relied on, other than what follows from the above.
Results may differ from a plain program's by a relative error of at most 0.00011.
Values sent between devices are 32-bit elements; how exact they have to be, the bound alone decides.
No kernel may reach another device: no remote copies, remote signals or barrier semaphores. Data moves between devices by JAX's collectives and lax.ppermute only.
A program may use at most 320 MiB of HBM per device.

v0:
```python
import math

import jax
import jax.numpy as jnp
from jax import lax
from jax.sharding import PartitionSpec as P

K = 8
H = 16
NT = 64


gravity = 1.0
relax_step = 0.3
drag_coef = 0.5
speed_floor = 0.01
omega_step = 0.1


def shifted(value, axis, steps):
    count = lax.axis_size(axis)
    leading, last = (max(0, -steps), min(count, count - steps))
    return lax.ppermute(value, axis, [(source, source + steps) for source in range(leading, last)])


def padded_2(cells, sides, width):
    for axis, dim in sides:
        count = lax.axis_size(axis)
        ends = count - 1
        head = lax.slice_in_dim(cells, 0, width, axis=dim)
        tail = lax.slice_in_dim(cells, cells.shape[dim] - width, cells.shape[dim], axis=dim)
        cells = jnp.concatenate(
            [
                lax.ppermute(tail, axis, [(i, (i + 1) % count) for i in range(ends)]),
                cells,
                lax.ppermute(head, axis, [((i + 1) % count, i) for i in range(ends)]),
            ],
            axis=dim,
        )
    return cells


def make_basis(freq_order):
    cycles = (freq_order[:K] + 1).astype(jnp.float32)
    samples = jnp.arange(NT).astype(jnp.float32)
    angle = 2.0 * math.pi / NT * samples[:, None] * cycles[None, :]
    basis = jnp.stack([jnp.cos(angle), jnp.sin(angle)], axis=-1).reshape(NT, H)
    return (basis, omega_step * cycles)


def rotate(field, omega):
    pairs = field.reshape((omega.shape[0], 2) + field.shape[1:])
    scale = omega[:, None, None]
    return jnp.stack([scale * pairs[:, 1], -scale * pairs[:, 0]], axis=1).reshape(field.shape)


def diff_cols(field):
    padded = jnp.pad(field, ((0, 0), (0, 0), (1, 1)))
    return 0.5 * (padded[:, :, 2:] - padded[:, :, :-2])


def body(state, forcing, depth, wet_mask, nest_index, freq_order):
    local_ch = state.shape[2]
    rows = state.shape[3]
    cols = state.shape[4]
    cells = rows * cols
    basis, omega = make_basis(freq_order)
    omega_local = lax.dynamic_slice_in_dim(
        omega, lax.axis_index("harm") * (local_ch // 2), local_ch // 2
    )
    fields = state[0]
    flat = fields.reshape(3, local_ch, cells)
    strip = jnp.take(flat, nest_index, axis=2)
    arrived = shifted(strip, "sec", 1)
    edge = jnp.where(lax.axis_index("sec") == 1, arrived, fields[:, :, :, 0])
    fields = fields.at[:, :, :, 0].set(edge)
    eta, east, north = (fields[0], fields[1], fields[2])
    wet = wet_mask[0].astype(jnp.float32)
    height = depth[0]
    coupled = jnp.stack([east, north]).reshape(2, local_ch, cells)
    harms = lax.axis_size("harm")
    basis_split = basis.reshape(NT, harms, local_ch)
    piece = cells // harms
    basis_perm = jnp.transpose(basis_split, (0, 2, 1)).reshape(NT, local_ch * harms)
    received = lax.all_to_all(
        coupled.reshape(2, local_ch, harms, piece), "harm", split_axis=2, concat_axis=2, tiled=True
    )
    received = received.reshape(2, local_ch * harms, piece)
    samples = jnp.einsum("th,fhn->ftn", basis_perm, received, precision=lax.Precision.HIGHEST)
    speed = jnp.sqrt(samples[0] * samples[0] + samples[1] * samples[1] + speed_floor)
    terms = (
        2.0
        / NT
        * jnp.einsum(
            "th,ftn->fhn", basis_perm, speed[None] * samples, precision=lax.Precision.HIGHEST
        )
    )
    returned = lax.all_to_all(
        terms.reshape(2, local_ch, harms, piece), "harm", split_axis=2, concat_axis=2, tiled=True
    )
    friction = returned.reshape(2, local_ch, rows, cols) * (drag_coef / height)[None, None]
    padded_eta = padded_2(eta, (("tile", 1),), 1)
    rows_eta = 0.5 * (padded_eta[:, 2:] - padded_eta[:, :-2])
    res_east = rotate(east, omega_local) + gravity * diff_cols(eta) + friction[0] - forcing[0, 0]
    res_north = rotate(north, omega_local) + gravity * rows_eta + friction[1] - forcing[0, 1]
    east_new = wet * (east - relax_step * res_east)
    north_new = wet * (north - relax_step * res_north)
    padded_flux = padded_2(height * north_new, (("tile", 1),), 1)
    rows_flux = 0.5 * (padded_flux[:, 2:] - padded_flux[:, :-2])
    res_eta = rotate(eta, omega_local) + diff_cols(height * east_new) + rows_flux
    eta_new = wet * (eta - relax_step * res_eta)
    return jnp.stack([eta_new, east_new, north_new])[None]


def solution(mesh):
    in_specs = (
        P("sec", None, "harm", "tile", None),
        P("sec", None, "harm", "tile", None),
        P("sec", "tile", None),
        P("sec", "tile", None),
        P("tile"),
        P(),
    )
    out_specs = P("sec", None, "harm", "tile", None)
    return jax.shard_map(body, mesh=mesh, in_specs=in_specs, out_specs=out_specs, check_vma=False)
```

profile of v0, /device:TPU:24, one launch (start us, length us, event | category | flops | bytes accessed | tf_op | source)
XLA Modules:
  0.0 217.5 jit_solution(17076854317852251852)
XLA Ops:
  0.0 0.0 copy-start.8
  0.0 1.9 copy.212
  1.9 0.0 copy-done.8
  1.9 64.1 %copy.197 = f32[1,3,4,256,256]{2,1,4,3,0:T(4,128)} copy(f32[1,3,4,256,256]{4,3,2,1,0:T(8,128)S(1)} %copy.212) | data formatting | bytes 6291456 | tf_op args[0]
  66.0 3.3 %gather_fusion = f32[256,3,4]{2,1,0:T(4,128)} fusion(f32[3,4,65536]{1,0,2:T(4,128)} %bitcast.2, s32[1024]{0:T(1024)S(1)} %pad_clamp_fusion), kind=kCustom, calls=%fused_computation | custom fusion | bytes 25600 | tf_op jit(solution)/shard_map/jit(_take)/gather | solution.py:73
  69.3 2.2 %select_bitcast_fusion = f32[3,4,256]{1,0,2:T(4,128)} fusion(f32[256,3,4]{2,1,0:T(4,128)} %gather_fusion, pred[256]{0:T(512)(128)(4,1)S(1)} %compare_and_fusion), kind=kLoop, calls=%fused_computation.61 | loop fusion | flops 3072 | bytes 24832 | tf_op jit(solution)/shard_map/jit(_take)/select_n | solution.py:73
  71.5 2.5 %collective-permute-start = (f32[3,4,256]{1,0,2:T(4,128)}, f32[3,4,256]{1,0,2:T(4,128)}, u32[]{:S(2)}, u32[]{:S(2)}) collective-permute-start(f32[3,4,256]{1,0,2:T(4,128)} %select_bitcast_fusion), channel_id=1, source_target_pairs={{0,128},{1,129},{2,130},{3,131},{4,132},{5,133},{6,134},{7,135},{8... | collective-permute-start | bytes 36872 | tf_op jit(solution)/shard_map/ppermute | solution.py:23
  74.0 1.2 slice.150
  75.3 8.3 %copy.207 = f32[3,4,256,1]{1,0,2,3:T(4,128)} copy(f32[3,4,256,1]{3,2,1,0:T(8,128)} %slice.150) | data formatting | bytes 24576 | tf_op jit(solution)/shard_map/squeeze | solution.py:75
  83.6 0.0 collective-permute-done
  83.6 2.0 fusion.33
  85.6 7.6 %copy.200 = f32[3,4,256,1]{3,2,1,0:T(8,128)} copy(f32[3,4,256,1]{1,0,2,3:T(4,128)} %fusion.33) | data formatting | bytes 24576 | tf_op jit(solution)/shard_map/reshape.31
  93.2 4.9 %scatter.4 = f32[3,4,256,256]{3,2,1,0:T(8,128)S(1)} dynamic-update-slice(f32[3,4,256,256]{3,2,1,0:T(8,128)S(1)} %bitcast.88, f32[3,4,256,1]{3,2,1,0:T(8,128)} %copy.200, s32[]{:T(128)} %constant.62.clone.1, s32[]{:T(128)} %constant.62.clone.1, s32[]{:T(128)} %constant.62.clone.1, s32[]{:T(128)} %constant.62.clone.1) | dynamic-update-slice | bytes 24580 | tf_op jit(solution)/shard_map/scatter | solution.py:76
  98.1 1.5 stack.44
  99.6 3.2 %reshape_reshape.6 = f32[2,4,4,16384]{3,2,1,0:T(4,128)} reshape(f32[2,4,256,256]{3,2,1,0:T(8,128)} %stack.44) | data formatting | bytes 4194304 | tf_op jit(solution)/shard_map/reshape;reshape | solution.py:86
  102.8 4.3 %copy.201 = f32[2,4,4,16384]{3,1,0,2:T(4,128)} copy(f32[2,4,4,16384]{3,2,1,0:T(4,128)} %reshape_reshape.6) | data formatting | bytes 4194304 | tf_op jit(solution)/shard_map/reshape;reshape | solution.py:86
  107.1 0.0 copy-start.9
  107.1 4.8 %all-to-all-start = ((f32[2,4,4,16384]{3,1,0,2:T(4,128)}), f32[2,4,4,16384]{3,1,0,2:T(4,128)}, u32[]{:S(2)}, u32[]{:S(2)}) async-start(f32[2,4,4,16384]{3,1,0,2:T(4,128)} %copy.201), calls=%async_computation | async-start | bytes 4194304 | tf_op jit(solution)/shard_map/all_to_all | solution.py:85
  111.9 0.0 copy-done.9
  111.9 0.1 multiply_cosine_fusion
  112.0 25.2 %all-to-all-done = f32[2,4,4,16384]{3,1,0,2:T(4,128)} async-done(((f32[2,4,4,16384]{3,1,0,2:T(4,128)}), f32[2,4,4,16384]{3,1,0,2:T(4,128)}, u32[]{:S(2)}, u32[]{:S(2)}) %all-to-all-start) | async-done | bytes 2097184 | tf_op jit(solution)/shard_map/all_to_all | solution.py:85
  137.2 8.9 %convolution_bitcast_fusion = f32[2,64,16384]{2,1,0:T(8,128)S(1)} fusion(f32[2,4,4,16384]{3,1,0,2:T(4,128)} %all-to-all-done, f32[64,4,4,1]{0,1,3,2:T(4,128)S(1)} %bitcast.96), kind=kOutput, calls=%fused_computation.1 | convolution fusion | flops 402653184 | bytes 10489856 | tf_op jit(solution)/shard_map/th,fhn->ftn/dot_general | solution.py:89
  146.2 1.5 fusion.5
  147.7 6.2 %fusion = f32[2,16,16384]{2,1,0:T(8,128)} fusion(f32[64,16,1]{0,1,2:T(8,128)S(1)} %bitcast.97, f32[2,64,16384]{2,1,0:T(8,128)S(1)} %convolution_bitcast_fusion, f32[64,16384]{1,0:T(8,128)S(1)} %fusion.5), kind=kOutput, calls=%fused_computation.3 | convolution fusion | flops 405274624 | bytes 14684160 | tf_op jit(solution)/shard_map/th,ftn->fhn/dot_general | solution.py:94
  153.9 2.9 %reshape.166 = f32[2,4,4,16384]{3,2,1,0:T(4,128)} reshape(f32[2,16,16384]{2,1,0:T(8,128)} %fusion) | data formatting | bytes 4194304 | tf_op jit(solution)/shard_map/reshape | solution.py:99
  156.7 4.3 %copy.204 = f32[2,4,4,16384]{3,1,0,2:T(4,128)} copy(f32[2,4,4,16384]{3,2,1,0:T(4,128)} %reshape.166) | data formatting | bytes 4194304 | tf_op jit(solution)/shard_map/reshape | solution.py:99
  161.0 0.0 copy-start.6
  161.0 4.6 %all-to-all-start.1 = ((f32[2,4,4,16384]{3,1,0,2:T(4,128)}), f32[2,4,4,16384]{3,1,0,2:T(4,128)}, u32[]{:S(2)}, u32[]{:S(2)}) async-start(f32[2,4,4,16384]{3,1,0,2:T(4,128)} %copy.204), calls=%async_computation.1 | async-start | bytes 4194304 | tf_op jit(solution)/shard_map/all_to_all | solution.py:98
  165.6 0.1 fusion.36
  165.6 0.0 copy-done.6
  165.6 0.8 broadcast_divide_fusion
  166.4 1.0 convert_bitcast_fusion
  167.4 0.4 fusion.37
  167.8 0.0 copy-start
  167.8 3.8 %collective-permute-start.2 = (f32[4,1,256]{2,1,0:T(1,128)S(1)}, f32[4,1,256]{2,1,0:T(1,128)S(1)}, u32[]{:S(2)}, u32[]{:S(2)}) collective-permute-start(f32[4,1,256]{2,1,0:T(1,128)S(1)} %get-tuple-element.38), channel_id=1, source_target_pairs={{0,4},{4,8},{8,12},{12,16},{16,20},{20,24},{24,28},{28,32},{32,36}... | collective-permute-start | bytes 12296 | tf_op jit(solution)/shard_map/ppermute | solution.py:34
  171.6 6.0 %collective-permute-start.1 = (f32[4,1,256]{2,1,0:T(1,128)S(1)}, f32[4,1,256]{2,1,0:T(1,128)S(1)}, u32[]{:S(2)}, u32[]{:S(2)}) collective-permute-start(f32[4,1,256]{2,1,0:T(1,128)S(1)} %get-tuple-element.37), channel_id=1, source_target_pairs={{4,0},{8,4},{12,8},{16,12},{20,16},{24,20},{28,24},{32,28},{36,32}... | collective-permute-start | bytes 12296 | tf_op jit(solution)/shard_map/ppermute | solution.py:36
  177.7 1.3 slice_multiply_fusion.3
  179.0 0.0 copy-done
  179.0 1.6 pad_maximum_fusion.5
  180.6 9.6 %all-to-all-done.1 = f32[2,4,4,16384]{3,1,0,2:T(4,128)} async-done(((f32[2,4,4,16384]{3,1,0,2:T(4,128)}), f32[2,4,4,16384]{3,1,0,2:T(4,128)}, u32[]{:S(2)}, u32[]{:S(2)}) %all-to-all-start.1) | async-done | bytes 2097184 | tf_op jit(solution)/shard_map/all_to_all | solution.py:98
  190.2 4.3 %copy.205 = f32[2,4,4,16384]{3,2,1,0:T(4,128)} copy(f32[2,4,4,16384]{3,1,0,2:T(4,128)} %all-to-all-done.1) | data formatting | bytes 4194304 | tf_op jit(solution)/shard_map/all_to_all | solution.py:98
  194.5 3.6 %reshape.167 = f32[2,4,256,256]{3,2,1,0:T(8,128)} reshape(f32[2,4,4,16384]{3,2,1,0:T(4,128)} %copy.205) | data formatting | bytes 4194304 | tf_op jit(solution)/shard_map/reshape | solution.py:101
  198.1 0.0 copy-start.1
  198.1 0.0 copy-start.2
  198.1 0.0 copy-start.3
  198.1 0.0 copy-start.7
  198.1 1.9 broadcast_multiply_fusion
  200.1 0.0 collective-permute-done.2
  200.1 0.0 collective-permute-done.1
  200.1 0.0 copy-done.1
  200.1 0.3 copy-done.2
  200.4 0.3 copy-done.3
  200.7 0.0 copy-done.7
  200.7 0.0 copy-start.4
  200.7 2.9 %broadcast_multiply_fusion.2 = (f32[4,256,256]{2,1,0:T(8,128)S(1)}, f32[4,256,256]{2,1,0:T(8,128)S(1)}, f32[4,256,256]{2,1,0:T(8,128)S(1)}, f32[4,256,256]{2,1,0:T(8,128)S(1)}) fusion(f32[256,256]{1,0:T(8,128)S(1)} %bitcast.94, f32[1,2,4,256,256]{4,3,2,1,0:T(8,128)} %param.9, f32[2,4,256,256]{3,2,1,0:T(8,128)S(1)} %broadcast_multiply_fusion, ...), kind=kLoop, calls=%fused_computation.63 | loop fusion | flops 5242880 | bytes 14163968 | tf_op jit(solution)/shard_map/mul | solution.py:110
  203.6 3.8 %collective-permute-start.4 = (f32[4,1,256]{2,1,0:T(1,128)S(1)}, f32[4,1,256]{2,1,0:T(1,128)S(1)}, u32[]{:S(2)}, u32[]{:S(2)}) collective-permute-start(f32[4,1,256]{2,1,0:T(1,128)S(1)} %get-tuple-element.32), channel_id=1, source_target_pairs={{0,4},{4,8},{8,12},{12,16},{16,20},{20,24},{24,28},{28,32},{32,36}... | collective-permute-start | bytes 12296 | tf_op jit(solution)/shard_map/ppermute | solution.py:34
  207.5 6.0 %collective-permute-start.3 = (f32[4,1,256]{2,1,0:T(1,128)S(1)}, f32[4,1,256]{2,1,0:T(1,128)S(1)}, u32[]{:S(2)}, u32[]{:S(2)}) collective-permute-start(f32[4,1,256]{2,1,0:T(1,128)S(1)} %get-tuple-element.31), channel_id=1, source_target_pairs={{4,0},{8,4},{12,8},{16,12},{20,16},{24,20},{28,24},{32,28},{36,32}... | collective-permute-start | bytes 12296 | tf_op jit(solution)/shard_map/ppermute | solution.py:36
  213.5 0.0 copy-done.4
  213.5 0.0 copy-done.5
  213.5 0.1 pad_maximum_fusion.4
  213.6 0.0 collective-permute-done.4
  213.6 1.2 collective-permute-done.3
  214.8 0.7 fusion.22
  215.5 2.0 maximum_bitcast_fusion
  (12 shorter events, 0.1 us)
Async XLA Ops:
  0.0 1.9 copy-start.8
  71.5 12.1 %collective-permute-start = (f32[3,4,256]{1,0,2:T(4,128)}, f32[3,4,256]{1,0,2:T(4,128)}, u32[]{:S(2)}, u32[]{:S(2)}) collective-permute-start(f32[3,4,256]{1,0,2:T(4,128)} %select_bitcast_fusion), channel_id=1, source_target_pairs={{0,128},{1,129},{2,130},{3,131},{4,132},{5,133},{6,134},{7,135},{8... | collective-permute-start | bytes 36872 | tf_op jit(solution)/shard_map/ppermute | solution.py:23
  107.1 4.8 %copy-start.9 = (s32[16]{0:T(128)S(1)}, s32[16]{0:T(128)}, u32[]{:S(2)}) copy-start(s32[16]{0:T(128)} %param.13) | copy-start | bytes 196
  107.1 30.2 %all-to-all-start = ((f32[2,4,4,16384]{3,1,0,2:T(4,128)}), f32[2,4,4,16384]{3,1,0,2:T(4,128)}, u32[]{:S(2)}, u32[]{:S(2)}) async-start(f32[2,4,4,16384]{3,1,0,2:T(4,128)} %copy.201), calls=%async_computation | async-start | bytes 4194304 | tf_op jit(solution)/shard_map/all_to_all | solution.py:85
  161.0 4.7 %copy-start.6 = (f32[1,256,256]{2,1,0:T(8,128)S(1)}, f32[1,256,256]{2,1,0:T(8,128)}, u32[]{:S(2)}) copy-start(f32[1,256,256]{2,1,0:T(8,128)} %param.10) | copy-start | bytes 786436
  161.0 29.3 %all-to-all-start.1 = ((f32[2,4,4,16384]{3,1,0,2:T(4,128)}), f32[2,4,4,16384]{3,1,0,2:T(4,128)}, u32[]{:S(2)}, u32[]{:S(2)}) async-start(f32[2,4,4,16384]{3,1,0,2:T(4,128)} %copy.204), calls=%async_computation.1 | async-start | bytes 4194304 | tf_op jit(solution)/shard_map/all_to_all | solution.py:98
  167.8 11.2 %copy-start = (f32[4,256,256]{2,1,0:T(8,128)}, f32[4,256,256]{2,1,0:T(8,128)S(1)}, u32[]{:S(2)}) copy-start(f32[4,256,256]{2,1,0:T(8,128)S(1)} %get-tuple-element.26) | copy-start | bytes 3145732
  167.8 32.3 %collective-permute-start.2 = (f32[4,1,256]{2,1,0:T(1,128)S(1)}, f32[4,1,256]{2,1,0:T(1,128)S(1)}, u32[]{:S(2)}, u32[]{:S(2)}) collective-permute-start(f32[4,1,256]{2,1,0:T(1,128)S(1)} %get-tuple-element.38), channel_id=1, source_target_pairs={{0,4},{4,8},{8,12},{12,16},{16,20},{20,24},{24,28},{28,32},{32,36}... | collective-permute-start | bytes 12296 | tf_op jit(solution)/shard_map/ppermute | solution.py:34
  171.6 28.4 %collective-permute-start.1 = (f32[4,1,256]{2,1,0:T(1,128)S(1)}, f32[4,1,256]{2,1,0:T(1,128)S(1)}, u32[]{:S(2)}, u32[]{:S(2)}) collective-permute-start(f32[4,1,256]{2,1,0:T(1,128)S(1)} %get-tuple-element.37), channel_id=1, source_target_pairs={{4,0},{8,4},{12,8},{16,12},{20,16},{24,20},{28,24},{32,28},{36,32}... | collective-permute-start | bytes 12296 | tf_op jit(solution)/shard_map/ppermute | solution.py:36
  198.1 2.0 copy-start.1
  198.1 2.2 %copy-start.2 = (f32[2,2,256,256]{3,2,1,0:T(8,128)S(1)}, f32[2,2,256,256]{3,2,1,0:T(8,128)}, u32[]{:S(2)}) copy-start(f32[2,2,256,256]{3,2,1,0:T(8,128)} %get-tuple-element.45) | copy-start | bytes 3145732
  198.1 2.6 %copy-start.3 = (f32[2,2,256,256]{3,2,1,0:T(8,128)S(1)}, f32[2,2,256,256]{3,2,1,0:T(8,128)}, u32[]{:S(2)}) copy-start(f32[2,2,256,256]{3,2,1,0:T(8,128)} %get-tuple-element.46) | copy-start | bytes 3145732
  198.1 2.6 %copy-start.7 = (f32[1,256,256]{2,1,0:T(8,128)S(1)}, f32[1,256,256]{2,1,0:T(8,128)}, u32[]{:S(2)}) copy-start(f32[1,256,256]{2,1,0:T(8,128)} %param.10) | copy-start | bytes 786436
  200.7 12.8 %copy-start.4 = (f32[2,1,256,256]{3,2,1,0:T(8,128)S(1)}, f32[2,1,256,256]{3,2,1,0:T(8,128)}, u32[]{:S(2)}) copy-start(f32[2,1,256,256]{3,2,1,0:T(8,128)} %get-tuple-element.39) | copy-start | bytes 1572868
  200.7 12.8 %copy-start.5 = (f32[2,1,256,256]{3,2,1,0:T(8,128)S(1)}, f32[2,1,256,256]{3,2,1,0:T(8,128)}, u32[]{:S(2)}) copy-start(f32[2,1,256,256]{3,2,1,0:T(8,128)} %get-tuple-element.40) | copy-start | bytes 1572868
  203.6 10.0 %collective-permute-start.4 = (f32[4,1,256]{2,1,0:T(1,128)S(1)}, f32[4,1,256]{2,1,0:T(1,128)S(1)}, u32[]{:S(2)}, u32[]{:S(2)}) collective-permute-start(f32[4,1,256]{2,1,0:T(1,128)S(1)} %get-tuple-element.32), channel_id=1, source_target_pairs={{0,4},{4,8},{8,12},{12,16},{16,20},{20,24},{24,28},{28,32},{32,36}... | collective-permute-start | bytes 12296 | tf_op jit(solution)/shard_map/ppermute | solution.py:34
  207.5 7.4 %collective-permute-start.3 = (f32[4,1,256]{2,1,0:T(1,128)S(1)}, f32[4,1,256]{2,1,0:T(1,128)S(1)}, u32[]{:S(2)}, u32[]{:S(2)}) collective-permute-start(f32[4,1,256]{2,1,0:T(1,128)S(1)} %get-tuple-element.31), channel_id=1, source_target_pairs={{4,0},{8,4},{12,8},{16,12},{20,16},{24,20},{28,24},{32,28},{36,32}... | collective-permute-start | bytes 12296 | tf_op jit(solution)/shard_map/ppermute | solution.py:36
where the time goes:
time: 219 us; the launch traced here: 218 us
  local copies, waits for them, and re-layouts  116 us (53%)
  waiting for transfers between devices  36 us (16%)
  starting transfers between devices  31.6 us (14%)
  other arithmetic  18.1 us (8%)
  matrix products  15.1 us (7%)
    unnamed x22, local copies, waits for them, and re-layouts  66.7 us
    all_to_all x1, waiting for transfers between devices, body(): lax.all_to_all(coupled.reshape(2, local_ch, harms, piece), 'harm', split_...  25.2 us
    ppermute x2, starting transfers between devices, padded_2(): lax.ppermute(head, axis, [((i + 1) % count, i) for i in range(ends)])  12.1 us
    all_to_all x1, waiting for transfers between devices, body(): lax.all_to_all(terms.reshape(2, local_ch, harms, piece), 'harm', split_ax...  9.63 us
    dot_general x1, matrix products, body(): jnp.einsum('th,fhn->ftn', basis_perm, received, precision=lax.Precision.H...  8.94 us
    squeeze x1, local copies, waits for them, and re-layouts, body(): edge = jnp.where(lax.axis_index('sec') == 1, arrived, fields[:, :, :, 0])  8.27 us
    ppermute x2, starting transfers between devices, padded_2(): lax.ppermute(tail, axis, [(i, (i + 1) % count) for i in range(ends)])  7.67 us
    another operation x1, local copies, waits for them, and re-layouts  7.64 us
  transfers between devices with their start and end apart: 7, of which 3 were waited for; matrix products, arithmetic and copies ran while one was open for 11% of the time, Pallas kernels for 0%

commit v1 on v0

v1 whole, which is shorter than its diff:
```python
import functools

import jax
import jax.numpy as jnp
from jax import lax
from jax.experimental import pallas as pl
from jax.experimental.pallas import tpu as pltpu
from jax.sharding import PartitionSpec as P

K = 8
NT = 64
CELLS = 256
RING = 4
HALF = 128
PIECE = 32
LANES = 128
BLOCK = 8 * PIECE
relax_step = 0.3
speed_floor = 0.01
omega_step = 0.1
TURN = 6.283185307179586 / NT
F32 = jnp.float32
BF16 = jnp.bfloat16
I32 = jnp.int32
MIB = 1 << 20


def params(mib=48):
    return pltpu.CompilerParams(vmem_limit_bytes=mib * MIB)


def cost(us):
    return pl.CostEstimate(flops=0, bytes_accessed=int(us * 3.0e6), transcendentals=0)


def vmem(count):
    return [pl.BlockSpec(memory_space=pltpu.VMEM)] * count


def dot(a, b):
    return jnp.dot(a, b, preferred_element_type=F32)


def pair(x):
    high = x.astype(BF16)
    return high, (x - high.astype(F32)).astype(BF16)


def iota(shape, dim):
    return lax.broadcasted_iota(I32, shape, dim)


def trig(freq_ref, me, time, slot, channel):
    owner = (me - slot + RING) & (RING - 1)
    constituent = owner * 2 + (channel >> 1)
    cycles = jnp.zeros(time.shape, I32)
    for k in range(K):
        cycles = jnp.where(constituent == k, freq_ref[k] + 1, cycles)
    angle = ((time * cycles) & (NT - 1)).astype(F32) * TURN
    return jnp.where((channel & 1) == 0, jnp.cos(angle), jnp.sin(angle))


def prepare(freq_ref, index_ref, fields_ref, strip_ref, forward_ref, backward_ref):
    me = lax.axis_index("harm")
    index = index_ref[...]
    row_of, col_of = index >> 8, index & (CELLS - 1)
    pick = jnp.where(iota((CELLS, CELLS), 0) == col_of, 1.0, 0.0).astype(BF16)
    picks = jnp.concatenate([pick, pick, pick], 0)
    at_row = iota((CELLS, CELLS), 0) == row_of
    for k in range(12):
        plane = fields_ref[k]
        high, rest = plane.astype(BF16), None
        rest = plane - high.astype(F32)
        mid, low = pair(rest)
        column = dot(jnp.concatenate([high, mid, low], 1), picks)
        strip_ref[k : k + 1, :] = jnp.sum(jnp.where(at_row, column, 0.0), axis=0, keepdims=True)
    shape = (128, 96)
    row, col = iota(shape, 0), iota(shape, 1)
    part, lane = col >> 5, col & 31
    value = trig(freq_ref, me, row & 63, lane >> 3, lane & 3)
    value = jnp.where((row >> 6) == ((lane >> 2) & 1), value, 0.0)
    high = value.astype(BF16).astype(F32)
    forward_ref[...] = jnp.where(part == 1, value - high, high).astype(BF16)
    shape = (64, 256)
    row, col = iota(shape, 0), iota(shape, 1)
    lane = row & 31
    value = trig(freq_ref, me, col & 63, lane >> 3, lane & 3) * (1.0 / NT)
    value = jnp.where(((col >> 6) & 1) == ((lane >> 2) & 1), value, 0.0)
    high = value.astype(BF16).astype(F32)
    low = jnp.where(col < 128, value - high, 0.0)
    backward_ref[...] = jnp.where(row < 32, high, low).astype(BF16)


def pieces(state_ref, outs, sems, start):
    me = lax.axis_index("harm")
    copies = []
    for slot in range(RING):
        row = pl.multiple_of(start + ((me + slot) & (RING - 1)) * PIECE, PIECE)
        for j in range(2):
            copies.append(
                pltpu.make_async_copy(
                    state_ref.at[0, pl.ds(1, 2), :, pl.ds(row, PIECE), pl.ds(j * LANES, LANES)],
                    outs[slot].at[pl.ds(j * BLOCK, BLOCK), :].reshape(2, 4, PIECE, LANES),
                    sems.at[slot, j],
                )
            )
    for copy in copies:
        copy.start()
    return copies


def pack_upper(state_ref, *refs):
    for copy in pieces(state_ref, refs[:4], refs[4], 0):
        copy.wait()


def pack_lower(strip_ref, state_ref, *refs):
    outs, (first_ref, last_ref, edges, sems, edge_sems) = refs[:4], refs[4:]
    shelf = lax.axis_index("sec") == 1
    looks = [
        pltpu.make_async_copy(state_ref.at[0, :, :, pl.ds(row, 8), :], edges.at[e], edge_sems.at[e])
        for e, row in enumerate((0, CELLS - 8))
    ]
    for look in looks:
        look.start()
    copies = pieces(state_ref, outs, sems, HALF)
    for look in looks:
        look.wait()
    strip = strip_ref[...]
    take = jnp.logical_and(iota((12, CELLS), 1) == 0, shelf)
    first = edges[0].reshape(12, 8, CELLS)[:, 0, :]
    last = edges[1].reshape(12, 8, CELLS)[:, 7, :]
    first = jnp.where(take, strip[:, 0:1], first)
    last = jnp.where(take, strip[:, CELLS - 1 : CELLS], last)
    first_ref[...] = first[0:4]
    last_ref[...] = last[0:4]
    for e, values in enumerate((strip, first, last)):
        for j in range(2):
            row = 2 * BLOCK + 24 * j + 8 * e
            for slot in range(RING):
                outs[slot][row : row + 8, :] = values[4:12, j * LANES : (j + 1) * LANES]
    for copy in copies:
        copy.wait()


def friction(more, forward_ref, backward_ref, *refs):
    xs, outs = refs[:RING], refs[RING : 2 * RING]
    forward, backward = forward_ref[...], backward_ref[...]

    def terms(x):
        high, low = pair(x)
        samples = dot(forward, jnp.concatenate([high, high, low], 0))
        east, north = samples[:NT], samples[NT:]
        square = east * east + north * north + speed_floor
        speed = square * lax.rsqrt(square)
        high, low = pair(jnp.concatenate([speed * east, speed * north], 0))
        both = dot(backward, jnp.concatenate([high, low], 0))
        return both[:32] + both[32:]

    def step(r, carry):
        x = jnp.concatenate(
            [
                jnp.concatenate([ref[pl.ds(j * BLOCK + r, 8, stride=PIECE), :] for ref in xs], 0)
                for j in range(2)
            ],
            1,
        )
        out = terms(x)
        for slot in range(RING):
            for j in range(2):
                outs[slot][pl.ds(j * BLOCK + r, 8, stride=PIECE), :] = out[
                    8 * slot : 8 * slot + 8, j * LANES : (j + 1) * LANES
                ]
        return carry

    lax.fori_loop(0, PIECE, step, 0, unroll=4)
    if more:
        for e in range(3):
            rows = [pl.ds(2 * BLOCK + 24 * j + 8 * e, 8) for j in range(2)]
            x = jnp.concatenate(
                [jnp.concatenate([ref[rows[j], :] for ref in xs], 0) for j in range(2)], 1
            )
            refs[2 * RING][8 * e : 8 * e + 8, :] = terms(x)[:8]


def left_right(x):
    lane = iota(x.shape, 1)
    right = jnp.where(lane == CELLS - 1, 0.0, pltpu.roll(x, CELLS - 1, 1))
    left = jnp.where(lane == 0, 0.0, pltpu.roll(x, 1, 1))
    return right - left


def up_down(x, before, after):
    row = iota(x.shape, 0)
    down = jnp.where(row == CELLS - 1, after, pltpu.roll(x, CELLS - 1, 0))
    up = jnp.where(row == 0, before, pltpu.roll(x, 1, 0))
    return down - up


def known(freq_ref, strip_ref, before_ref, after_ref, state_ref, forcing_ref, east_ref, north_ref, eta_ref, edge_ref):
    me = lax.axis_index("harm")
    shelf = lax.axis_index("sec") == 1
    take = jnp.logical_and(iota((CELLS, CELLS), 1) == 0, shelf)
    columns = jnp.concatenate([strip_ref[...], jnp.zeros((4, CELLS), F32)], 0).T

    def field(f, ch):
        k = 4 * f + ch
        return jnp.where(take, columns[:, k : k + 1], state_ref[0, f, ch])

    for i in range(2):
        omega = omega_step * (freq_ref[2 * me + i] + 1).astype(F32)
        eta = [field(0, 2 * i + p) for p in range(2)]
        for p in range(2):
            ch = 2 * i + p
            turn = -omega if p else omega
            eta_ref[ch] = eta[p] - relax_step * (turn * eta[1 - p])
        east = [field(1, 2 * i + p) for p in range(2)]
        for p in range(2):
            ch = 2 * i + p
            turn = -omega if p else omega
            rest = turn * east[1 - p] + 0.5 * left_right(eta[p]) - forcing_ref[0, 0, ch]
            east_ref[ch] = east[p] - relax_step * rest
        north = [field(2, 2 * i + p) for p in range(2)]
        for p in range(2):
            ch = 2 * i + p
            turn = -omega if p else omega
            slope = up_down(eta[p], before_ref[ch : ch + 1, :], after_ref[ch : ch + 1, :])
            rest = turn * north[1 - p] + 0.5 * slope - forcing_ref[0, 1, ch]
            value = north[p] - relax_step * rest
            north_ref[ch] = value
            edge_ref[ch : ch + 1, :] = value[0:1, :]
            edge_ref[4 + ch : 5 + ch, :] = value[CELLS - 1 : CELLS, :]


def edge_flux(edge_ref, extra_ref, depth_ref, wet_ref, first_ref, last_ref):
    for out_ref, at, row in ((first_ref, 0, 0), (last_ref, 1, CELLS - 1)):
        height = depth_ref[0, row : row + 1, :]
        wet = wet_ref[0, row : row + 1, :].astype(F32)
        drag = extra_ref[8 + 8 * at + 4 : 8 + 8 * at + 8, :]
        north = wet * (edge_ref[4 * at : 4 * at + 4, :] - (relax_step / height) * drag)
        out_ref[...] = height * north


def finish(extra_ref, before_ref, after_ref, depth_ref, wet_ref, east_ref, north_ref, eta_ref, *refs):
    drags, out_ref = refs[:-1], refs[-1]
    me = lax.axis_index("harm")
    shelf = lax.axis_index("sec") == 1
    columns = extra_ref[0:8, :].T
    for c in range(2):
        for slot in range(RING):
            row = pl.multiple_of(c * HALF + ((me + slot) & (RING - 1)) * PIECE, PIECE)
            rows = pl.ds(row, PIECE)
            wet = wet_ref[0, rows, :].astype(F32)
            factor = relax_step / depth_ref[0, rows, :]
            drag_ref = drags[4 * c + slot]
            for k in range(8):
                drag = jnp.concatenate(
                    [drag_ref[pl.ds(j * BLOCK + k * PIECE, PIECE), :] for j in range(2)], 1
                )
                source = (east_ref, north_ref)[k // 4]
                out_ref[0, 1 + k // 4, k % 4, rows, :] = wet * (source[k % 4, rows, :] - factor * drag)
    height = depth_ref[0]
    wet = wet_ref[0].astype(F32)
    factor = relax_step / height
    first = jnp.logical_and(iota((CELLS, CELLS), 1) == 0, shelf)
    for k in range(8):
        source = (east_ref, north_ref)[k // 4]
        fixed = wet * (source[k % 4] - factor * columns[:, k : k + 1])
        lanes = pl.ds(0, 128)
        out_ref[0, 1 + k // 4, k % 4, :, lanes] = jnp.where(
            first[:, :128], fixed[:, :128], out_ref[0, 1 + k // 4, k % 4, :, lanes]
        )
    for ch in range(4):
        slope = left_right(height * out_ref[0, 1, ch])
        slope = slope + up_down(
            height * out_ref[0, 2, ch], before_ref[ch : ch + 1, :], after_ref[ch : ch + 1, :]
        )
        out_ref[0, 0, ch] = wet * (eta_ref[ch] - (0.5 * relax_step) * slope)


def around(value, steps):
    return lax.ppermute(value, "harm", [(i, (i + steps) % RING) for i in range(RING)])


def body(state, forcing, depth, wet_mask, nest_index, freq_order):
    me = lax.axis_index("harm")
    tiles = lax.axis_size("tile")
    smem = pl.BlockSpec(memory_space=pltpu.SMEM)
    hbm = pl.BlockSpec(memory_space=pl.ANY)
    array = jax.ShapeDtypeStruct

    half = array((2 * BLOCK, LANES), F32)
    parts = pl.pallas_call(
        pack_upper,
        name="pack_upper",
        in_specs=[hbm],
        out_specs=vmem(RING),
        out_shape=(half,) * RING,
        scratch_shapes=[pltpu.SemaphoreType.DMA((RING, 2))],
        compiler_params=params(),
        cost_estimate=cost(2),
    )(state)
    upper = [parts[0]] + [around(parts[slot], slot) for slot in (1, 2, 3)]

    strip, forward, backward = pl.pallas_call(
        prepare,
        name="prepare",
        in_specs=[smem] + vmem(2),
        out_specs=vmem(3),
        out_shape=(array((12, CELLS), F32), array((128, 96), BF16), array((64, 256), BF16)),
        compiler_params=params(),
        cost_estimate=cost(4),
    )(freq_order, nest_index.reshape(1, CELLS), state.reshape(12, CELLS, CELLS))
    strip = lax.ppermute(strip, "sec", [(0, 1)])

    packed = pl.pallas_call(
        pack_lower,
        name="pack_lower",
        in_specs=vmem(1) + [hbm],
        out_specs=vmem(6),
        out_shape=(array((2 * BLOCK + 48, LANES), F32),) * RING + (array((4, CELLS), F32),) * 2,
        scratch_shapes=[
            pltpu.VMEM((2, 3, 4, 8, CELLS), F32),
            pltpu.SemaphoreType.DMA((RING, 2)),
            pltpu.SemaphoreType.DMA((2,)),
        ],
        compiler_params=params(),
        cost_estimate=cost(2),
    )(strip, state)
    lower = [packed[0]] + [around(packed[slot], slot) for slot in (1, 2, 3)]
    to_next = [(i, i + 1) for i in range(tiles - 1)]
    to_last = [(i + 1, i) for i in range(tiles - 1)]
    after = lax.ppermute(packed[4], "tile", to_last)
    before = lax.ppermute(packed[5], "tile", to_next)

    def drag(xs, more):
        outs = (half,) * RING + (array((24, CELLS), F32),) * more
        return pl.pallas_call(
            functools.partial(friction, more),
            name="friction",
            in_specs=vmem(2 + RING),
            out_specs=vmem(len(outs)),
            out_shape=outs,
            compiler_params=params(),
            cost_estimate=cost(10),
        )(forward, backward, *xs)

    upper_terms = drag(upper, 0)
    upper_back = [upper_terms[0]] + [around(upper_terms[slot], -slot) for slot in (1, 2, 3)]
    lower_terms = drag(lower, 1)
    lower_back = [lower_terms[0]] + [around(lower_terms[slot], -slot) for slot in (1, 2, 3)]
    extra = lower_terms[RING]

    plane = array((4, CELLS, CELLS), F32)
    east, north, eta, edge = pl.pallas_call(
        known,
        name="known",
        in_specs=[smem] + vmem(5),
        out_specs=vmem(4),
        out_shape=(plane, plane, plane, array((8, CELLS), F32)),
        compiler_params=params(),
        cost_estimate=cost(5),
    )(freq_order, strip, before, after, state, forcing)

    first, last = pl.pallas_call(
        edge_flux,
        name="edge_flux",
        in_specs=vmem(4),
        out_specs=vmem(2),
        out_shape=(array((4, CELLS), F32),) * 2,
        compiler_params=params(),
        cost_estimate=cost(1),
    )(edge, extra, depth, wet_mask)
    after_flux = lax.ppermute(first, "tile", to_last)
    before_flux = lax.ppermute(last, "tile", to_next)

    return pl.pallas_call(
        finish,
        name="finish",
        in_specs=vmem(8 + 2 * RING),
        out_specs=vmem(1)[0],
        out_shape=array((1, 3, 4, CELLS, CELLS), F32),
        compiler_params=params(),
        cost_estimate=cost(5),
    )(extra, before_flux, after_flux, depth, wet_mask, east, north, eta, *upper_back, *lower_back)


def solution(mesh):
    in_specs = (
        P("sec", None, "harm", "tile", None),
        P("sec", None, "harm", "tile", None),
        P("sec", "tile", None),
        P("sec", "tile", None),
        P("tile"),
        P(),
    )
    out_specs = P("sec", None, "harm", "tile", None)
    return jax.shard_map(body, mesh=mesh, in_specs=in_specs, out_specs=out_specs, check_vma=False)
```

time: 219 us -> 83.3 us (0.38)
  local copies, waits for them, and re-layouts: 116 us -> 1.93 us
  Pallas kernels: 0 us -> 18.5 us
  other arithmetic: 18.1 us -> 0 us
  matrix products: 15.1 us -> 0 us
  waiting for transfers between devices: 36 us -> 28.1 us
  starting transfers between devices: 31.6 us -> 34.3 us
    unnamed x22 -> x14, local copies, waits for them, and re-layouts: 66.7 us -> 1.93 us
    all_to_all x2 -> x0, waiting for transfers between devices: 34.8 us -> none  [the longest x1 25.2 us: body(): lax.all_to_all(coupled.reshape(2, local_ch, harms, piece), 'harm', split_...]
    ppermute x5 -> x17, waiting for transfers between devices: 1.2 us -> 28.1 us  [the longest x12 20 us: around(): lax.ppermute(value, 'harm', [(i, (i + steps) % RING) for i in range(RING)])]
    pallas_call x0 -> x8, Pallas kernels: none -> 18.5 us  [the longest x2 8.55 us: drag(): pl.pallas_call(functools.partial(friction, more), name='friction', in_spe...]
    another operation x5 -> x0, local copies, waits for them, and re-layouts: 16.6 us -> none
    dot_general x2 -> x0, matrix products: 15.1 us -> none  [the longest x1 8.94 us: body(): jnp.einsum('th,fhn->ftn', basis_perm, received, precision=lax.Precision.H...]
    ppermute x5 -> x17, starting transfers between devices: 22.3 us -> 34.3 us  [the longest x12 17.2 us: around(): lax.ppermute(value, 'harm', [(i, (i + steps) % RING) for i in range(RING)])]
    reshape x3 -> x0, local copies, waits for them, and re-layouts: 10.8 us -> none  [the longest x2 7.12 us: body(): terms.reshape(2, local_ch, harms, piece)]
  transfers between devices with their start and end apart: 7 -> 17, of which waited for: 3 -> 8; matrix products, arithmetic and copies ran while one was open for 11% -> 0% of each run, Pallas kernels for 0% -> 18%
where the time goes in v1:
time: 83.3 us; the launch traced here: 83 us
  starting transfers between devices  34.3 us (41%)
  waiting for transfers between devices  28.1 us (34%)
  Pallas kernels  18.5 us (22%)
  local copies, waits for them, and re-layouts  1.93 us (2%)
    ppermute x12, waiting for transfers between devices, around(): lax.ppermute(value, 'harm', [(i, (i + steps) % RING) for i in range(RING)])  20 us
    ppermute x12, starting transfers between devices, around(): lax.ppermute(value, 'harm', [(i, (i + steps) % RING) for i in range(RING)])  17.2 us
    pallas_call x2, Pallas kernels, drag(): pl.pallas_call(functools.partial(friction, more), name='friction', in_spe...  8.55 us
    ppermute x1, starting transfers between devices, body(): after_flux = lax.ppermute(first, 'tile', to_last)  6.03 us
    ppermute x1, waiting for transfers between devices, body(): before = lax.ppermute(packed[5], 'tile', to_next)  5.69 us
    ppermute x1, starting transfers between devices, body(): after = lax.ppermute(packed[4], 'tile', to_last)  4.04 us
    ppermute x1, starting transfers between devices, body(): before = lax.ppermute(packed[5], 'tile', to_next)  3.81 us
    pallas_call x1, Pallas kernels, body(): pl.pallas_call(finish, name='finish', in_specs=vmem(8 + 2 * RING), out_sp...  3.66 us
  transfers between devices with their start and end apart: 17, of which 8 were waited for; matrix products, arithmetic and copies ran while one was open for 0% of the time, Pallas kernels for 18%

profile of v1, /device:TPU:24, one launch (start us, length us, event | category | flops | bytes accessed | tf_op | source)
XLA Modules:
  0.0 83.0 jit_solution(6776200677122739749)
XLA Ops:
  0.0 0.0 copy-start
  0.0 1.9 %copy-done = f32[1,3,4,256,256]{4,3,2,1,0:T(8,128)S(1)} copy-done((f32[1,3,4,256,256]{4,3,2,1,0:T(8,128)S(1)}, f32[1,3,4,256,256]{4,3,2,1,0:T(8,128)}, u32[]{:S(2)}) %copy-start) | copy-done | bytes 3145752
  1.9 0.0 copy-start.1
  1.9 0.0 copy-start.5
  1.9 0.0 copy-start.6
  1.9 0.2 pack_upper.1
  2.1 1.6 %collective-permute-start.8 = (f32[512,128]{1,0:T(8,128)S(1)}, f32[512,128]{1,0:T(8,128)S(1)}, u32[]{:S(2)}, u32[]{:S(2)}) collective-permute-start(f32[512,128]{1,0:T(8,128)S(1)} %get-tuple-element.50), channel_id=1, source_target_pairs={{0,1},{1,2},{2,3},{3,0},{4,5},{5,6},{6,7},{7,4},{8,9},{9,10},{10,1... | collective-permute-start | bytes 786440 | tf_op jit(solution)/shard_map/ppermute | solution.py:282
  3.6 2.7 %collective-permute-start.9 = (f32[512,128]{1,0:T(8,128)S(1)}, f32[512,128]{1,0:T(8,128)S(1)}, u32[]{:S(2)}, u32[]{:S(2)}) collective-permute-start(f32[512,128]{1,0:T(8,128)S(1)} %get-tuple-element.51), channel_id=1, source_target_pairs={{0,2},{1,3},{2,0},{3,1},{4,6},{5,7},{6,4},{7,5},{8,10},{9,11},{10,... | collective-permute-start | bytes 786440 | tf_op jit(solution)/shard_map/ppermute | solution.py:282
  6.4 1.4 %collective-permute-start.10 = (f32[512,128]{1,0:T(8,128)S(1)}, f32[512,128]{1,0:T(8,128)S(1)}, u32[]{:S(2)}, u32[]{:S(2)}) collective-permute-start(f32[512,128]{1,0:T(8,128)S(1)} %get-tuple-element.52), channel_id=1, source_target_pairs={{0,3},{1,0},{2,1},{3,2},{4,7},{5,4},{6,5},{7,6},{8,11},{9,8},{10,9... | collective-permute-start | bytes 786440 | tf_op jit(solution)/shard_map/ppermute | solution.py:282
  7.8 0.0 copy-done.1
  7.8 0.0 copy-done.5
  7.8 0.0 copy-done.6
  7.8 0.0 copy-start.2
  7.8 2.5 %prepare.1 = (f32[12,256]{1,0:T(8,128)S(1)}, bf16[128,96]{1,0:T(8,128)(2,1)S(1)}, bf16[64,256]{1,0:T(8,128)(2,1)S(1)}) custom-call(s32[16]{0:T(128)S(1)} %copy-done.5, s32[1,256]{1,0:T(1,128)S(1)} %bitcast.3, f32[12,256,256]{2,1,0:T(8,128)S(1)} %bitcast.2), custom_call_target="tpu_custom_call" | custom-call | bytes 12000000 | tf_op jit(solution)/shard_map/prepare/pallas_call | solution.py:305
  10.4 1.3 %collective-permute-start = (f32[12,256]{1,0:T(8,128)S(1)}, f32[12,256]{1,0:T(8,128)S(1)}, u32[]{:S(2)}, u32[]{:S(2)}) collective-permute-start(f32[12,256]{1,0:T(8,128)S(1)} %get-tuple-element.35), channel_id=1, source_target_pairs={{0,128},{1,129},{2,130},{3,131},{4,132},{5,133},{6,134},{7,135},{8... | collective-permute-start | bytes 36872 | tf_op jit(solution)/shard_map/ppermute | solution.py:314
  11.7 0.8 collective-permute-done.strip_ref
  12.5 0.3 pack_lower.1
  12.8 0.7 collective-permute-start.1
  13.5 0.9 %collective-permute-start.2 = (f32[560,128]{1,0:T(8,128)S(1)}, f32[560,128]{1,0:T(8,128)S(1)}, u32[]{:S(2)}, u32[]{:S(2)}) collective-permute-start(f32[560,128]{1,0:T(8,128)S(1)} %get-tuple-element.38), channel_id=1, source_target_pairs={{0,2},{1,3},{2,0},{3,1},{4,6},{5,7},{6,4},{7,5},{8,10},{9,11},{10,... | collective-permute-start | bytes 860168 | tf_op jit(solution)/shard_map/ppermute | solution.py:282
  14.3 0.0 collective-permute-done.8.refs_1_
  14.3 1.9 %collective-permute-start.3 = (f32[560,128]{1,0:T(8,128)S(1)}, f32[560,128]{1,0:T(8,128)S(1)}, u32[]{:S(2)}, u32[]{:S(2)}) collective-permute-start(f32[560,128]{1,0:T(8,128)S(1)} %get-tuple-element.39), channel_id=1, source_target_pairs={{0,3},{1,0},{2,1},{3,2},{4,7},{5,4},{6,5},{7,6},{8,11},{9,8},{10,9... | collective-permute-start | bytes 860168 | tf_op jit(solution)/shard_map/ppermute | solution.py:282
  16.2 2.9 %collective-permute-done.9.refs_2_ = f32[512,128]{1,0:T(8,128)S(1)} collective-permute-done((f32[512,128]{1,0:T(8,128)S(1)}, f32[512,128]{1,0:T(8,128)S(1)}, u32[]{:S(2)}, u32[]{:S(2)}) %collective-permute-start.9) | collective-permute-done | bytes 262176 | tf_op jit(solution)/shard_map/ppermute | solution.py:282
  19.2 0.0 collective-permute-done.10.refs_3_
  19.2 4.1 %friction.3 = (f32[512,128]{1,0:T(8,128)S(1)}, f32[512,128]{1,0:T(8,128)S(1)}, f32[512,128]{1,0:T(8,128)S(1)}, f32[512,128]{1,0:T(8,128)S(1)}) custom-call(bf16[128,96]{1,0:T(8,128)(2,1)S(1)} %get-tuple-element.33.forward_ref, bf16[64,256]{1,0:T(8,128)(2,1)S(1)} %get-tuple-element.34.backward_ref, f32[512,128]{1,0:T(8,128)S(1)} %get-tuple-element.49.refs_0_, ...), custom_call_target="tpu_custom_call" | custom-call | bytes 30000000 | tf_op jit(solution)/shard_map/friction/pallas_call | solution.py:338
  23.3 1.3 %collective-permute-start.11 = (f32[512,128]{1,0:T(8,128)S(1)}, f32[512,128]{1,0:T(8,128)S(1)}, u32[]{:S(2)}, u32[]{:S(2)}) collective-permute-start(f32[512,128]{1,0:T(8,128)S(1)} %get-tuple-element.54), channel_id=1, source_target_pairs={{0,3},{1,0},{2,1},{3,2},{4,7},{5,4},{6,5},{7,6},{8,11},{9,8},{10,9... | collective-permute-start | bytes 786440 | tf_op jit(solution)/shard_map/ppermute | solution.py:282
  24.6 3.8 %collective-permute-start.4 = (f32[4,256]{1,0:T(4,128)S(1)}, f32[4,256]{1,0:T(4,128)S(1)}, u32[]{:S(2)}, u32[]{:S(2)}) collective-permute-start(f32[4,256]{1,0:T(4,128)S(1)} %get-tuple-element.41), channel_id=1, source_target_pairs={{0,4},{4,8},{8,12},{12,16},{16,20},{20,24},{24,28},{28,32},{32,36}... | collective-permute-start | bytes 12296 | tf_op jit(solution)/shard_map/ppermute | solution.py:334
  28.4 5.7 %collective-permute-done.4.before_ref = f32[4,256]{1,0:T(4,128)S(1)} collective-permute-done((f32[4,256]{1,0:T(4,128)S(1)}, f32[4,256]{1,0:T(4,128)S(1)}, u32[]{:S(2)}, u32[]{:S(2)}) %collective-permute-start.4) | collective-permute-done | bytes 4128 | tf_op jit(solution)/shard_map/ppermute | solution.py:334
  34.1 0.0 copy-start.3
  34.1 0.0 copy-start.4
  34.1 4.0 %collective-permute-start.5 = (f32[4,256]{1,0:T(4,128)S(1)}, f32[4,256]{1,0:T(4,128)S(1)}, u32[]{:S(2)}, u32[]{:S(2)}) collective-permute-start(f32[4,256]{1,0:T(4,128)S(1)} %get-tuple-element.42), channel_id=1, source_target_pairs={{4,0},{8,4},{12,8},{16,12},{20,16},{24,20},{28,24},{32,28},{36,32}... | collective-permute-start | bytes 12296 | tf_op jit(solution)/shard_map/ppermute | solution.py:333
  38.1 1.6 %collective-permute-done.5.after_ref = f32[4,256]{1,0:T(4,128)S(1)} collective-permute-done((f32[4,256]{1,0:T(4,128)S(1)}, f32[4,256]{1,0:T(4,128)S(1)}, u32[]{:S(2)}, u32[]{:S(2)}) %collective-permute-start.5) | collective-permute-done | bytes 4128 | tf_op jit(solution)/shard_map/ppermute | solution.py:333
  39.7 0.0 copy-done.2
  39.7 3.3 %known.1 = (f32[4,256,256]{2,1,0:T(8,128)S(1)}, f32[4,256,256]{2,1,0:T(8,128)S(1)}, f32[4,256,256]{2,1,0:T(8,128)S(1)}, f32[8,256]{1,0:T(8,128)S(1)}) custom-call(s32[16]{0:T(128)S(1)} %copy-done.5, f32[12,256]{1,0:T(8,128)S(1)} %collective-permute-done.strip_ref, f32[4,256]{1,0:T(4,128)S(1)} %collective-permute-done.4.before_ref, ...), custom_call_target="tpu_custom_call" | custom-call | bytes 15000000 | tf_op jit(solution)/shard_map/known/pallas_call | solution.py:355
  43.0 0.0 collective-permute-done.1.refs_1_
  43.0 0.0 collective-permute-done.2.refs_2_
  43.0 0.0 collective-permute-done.3.refs_3_
  43.0 4.4 %friction.2 = (f32[512,128]{1,0:T(8,128)S(1)}, f32[512,128]{1,0:T(8,128)S(1)}, f32[512,128]{1,0:T(8,128)S(1)}, f32[512,128]{1,0:T(8,128)S(1)}, f32[24,256]{1,0:T(8,128)S(1)}) custom-call(bf16[128,96]{1,0:T(8,128)(2,1)S(1)} %get-tuple-element.33.forward_ref, bf16[64,256]{1,0:T(8,128)(2,1)S(1)} %get-tuple-element.34.backward_ref, ...), custom_call_target="tpu_custom_call" | custom-call | bytes 30000000 | tf_op jit(solution)/shard_map/friction/pallas_call | solution.py:338
  47.5 0.0 copy-done.3
  47.5 0.0 copy-done.4
  47.6 1.9 %collective-permute-start.6 = (f32[4,256]{1,0:T(4,128)S(1)}, f32[4,256]{1,0:T(4,128)S(1)}, u32[]{:S(2)}, u32[]{:S(2)}) collective-permute-start(f32[4,256]{1,0:T(4,128)S(1)} %get-tuple-element.44), channel_id=1, source_target_pairs={{0,4},{4,8},{8,12},{12,16},{16,20},{20,24},{24,28},{28,32},{32,36}... | collective-permute-start | bytes 12296 | tf_op jit(solution)/shard_map/ppermute | solution.py:375
  49.5 6.0 %collective-permute-start.7 = (f32[4,256]{1,0:T(4,128)S(1)}, f32[4,256]{1,0:T(4,128)S(1)}, u32[]{:S(2)}, u32[]{:S(2)}) collective-permute-start(f32[4,256]{1,0:T(4,128)S(1)} %get-tuple-element.45), channel_id=1, source_target_pairs={{4,0},{8,4},{12,8},{16,12},{20,16},{24,20},{28,24},{32,28},{36,32}... | collective-permute-start | bytes 12296 | tf_op jit(solution)/shard_map/ppermute | solution.py:374
  55.5 2.4 %collective-permute-start.12 = (f32[512,128]{1,0:T(8,128)S(1)}, f32[512,128]{1,0:T(8,128)S(1)}, u32[]{:S(2)}, u32[]{:S(2)}) collective-permute-start(f32[512,128]{1,0:T(8,128)S(1)} %get-tuple-element.55), channel_id=1, source_target_pairs={{0,2},{1,3},{2,0},{3,1},{4,6},{5,7},{6,4},{7,5},{8,10},{9,11},{10,... | collective-permute-start | bytes 786440 | tf_op jit(solution)/shard_map/ppermute | solution.py:282
  57.9 0.8 collective-permute-start.13
  58.7 0.0 collective-permute-done.6.before_ref
  58.7 2.4 %collective-permute-start.14 = (f32[512,128]{1,0:T(8,128)S(1)}, f32[512,128]{1,0:T(8,128)S(1)}, u32[]{:S(2)}, u32[]{:S(2)}) collective-permute-start(f32[512,128]{1,0:T(8,128)S(1)} %get-tuple-element.58), channel_id=1, source_target_pairs={{0,3},{1,0},{2,1},{3,2},{4,7},{5,4},{6,5},{7,6},{8,11},{9,8},{10,9... | collective-permute-start | bytes 786440 | tf_op jit(solution)/shard_map/ppermute | solution.py:282
  61.2 0.0 collective-permute-done.7.after_ref
  61.2 0.0 collective-permute-start.15
  61.2 0.0 collective-permute-done.11.refs_1_
  61.2 1.1 %collective-permute-start.16 = (f32[512,128]{1,0:T(8,128)S(1)}, f32[512,128]{1,0:T(8,128)S(1)}, u32[]{:S(2)}, u32[]{:S(2)}) collective-permute-start(f32[512,128]{1,0:T(8,128)S(1)} %get-tuple-element.60), channel_id=1, source_target_pairs={{0,1},{1,2},{2,3},{3,0},{4,5},{5,6},{6,7},{7,4},{8,9},{9,10},{10,1... | collective-permute-start | bytes 786440 | tf_op jit(solution)/shard_map/ppermute | solution.py:282
  62.3 4.1 %collective-permute-done.12.refs_2_ = f32[512,128]{1,0:T(8,128)S(1)} collective-permute-done((f32[512,128]{1,0:T(8,128)S(1)}, f32[512,128]{1,0:T(8,128)S(1)}, u32[]{:S(2)}, u32[]{:S(2)}) %collective-permute-start.12) | collective-permute-done | bytes 262176 | tf_op jit(solution)/shard_map/ppermute | solution.py:282
  66.4 7.7 %collective-permute-done.13.refs_3_ = f32[512,128]{1,0:T(8,128)S(1)} collective-permute-done((f32[512,128]{1,0:T(8,128)S(1)}, f32[512,128]{1,0:T(8,128)S(1)}, u32[]{:S(2)}, u32[]{:S(2)}) %collective-permute-start.13) | collective-permute-done | bytes 262176 | tf_op jit(solution)/shard_map/ppermute | solution.py:282
  74.1 0.0 collective-permute-done.14.refs_5_
  74.1 2.8 %collective-permute-done.15.refs_6_ = f32[512,128]{1,0:T(8,128)S(1)} collective-permute-done((f32[512,128]{1,0:T(8,128)S(1)}, f32[512,128]{1,0:T(8,128)S(1)}, u32[]{:S(2)}, u32[]{:S(2)}) %collective-permute-start.15) | collective-permute-done | bytes 262176 | tf_op jit(solution)/shard_map/ppermute | solution.py:282
  76.9 2.5 %collective-permute-done.16.refs_7_ = f32[512,128]{1,0:T(8,128)S(1)} collective-permute-done((f32[512,128]{1,0:T(8,128)S(1)}, f32[512,128]{1,0:T(8,128)S(1)}, u32[]{:S(2)}, u32[]{:S(2)}) %collective-permute-start.16) | collective-permute-done | bytes 262176 | tf_op jit(solution)/shard_map/ppermute | solution.py:282
  79.4 3.7 %finish.1 = f32[1,3,4,256,256]{4,3,2,1,0:T(8,128)} custom-call(f32[24,256]{1,0:T(8,128)S(1)} %get-tuple-element.40.extra_ref, f32[4,256]{1,0:T(4,128)S(1)} %collective-permute-done.6.before_ref, f32[4,256]{1,0:T(4,128)S(1)} %collective-permute-done.7.after_ref, f32[1,256,256]{2,1,0:T(8,128)S(1)} %copy-done.3, s32[1,256,256]{2,1,0:T(8,128)S(1)} %copy-done.4, ...), custom_call_target="tpu_custom_call" | custom-call | bytes 15000000 | tf_op jit(solution)/shard_map/finish/pallas_call | solution.py:377
  (1 shorter events, 0.0 us)
Async XLA Ops:
  0.0 1.9 %copy-start = (f32[1,3,4,256,256]{4,3,2,1,0:T(8,128)S(1)}, f32[1,3,4,256,256]{4,3,2,1,0:T(8,128)}, u32[]{:S(2)}) copy-start(f32[1,3,4,256,256]{4,3,2,1,0:T(8,128)} %state_ref.5) | copy-start | bytes 9437188
  1.9 5.9 %copy-start.1 = (f32[1,3,4,256,256]{4,3,2,1,0:T(8,128)S(1)}, f32[1,3,4,256,256]{4,3,2,1,0:T(8,128)}, u32[]{:S(2)}) copy-start(f32[1,3,4,256,256]{4,3,2,1,0:T(8,128)} %state_ref.5) | copy-start | bytes 9437188
  1.9 5.9 %copy-start.5 = (s32[16]{0:T(128)S(1)}, s32[16]{0:T(128)}, u32[]{:S(2)}) copy-start(s32[16]{0:T(128)} %freq_ref.3) | copy-start | bytes 196
  1.9 5.9 %copy-start.6 = (s32[256]{0:T(256)S(1)}, s32[256]{0:T(256)}, u32[]{:S(2)}) copy-start(s32[256]{0:T(256)} %param.10) | copy-start | bytes 3076
  2.1 12.3 %collective-permute-start.8 = (f32[512,128]{1,0:T(8,128)S(1)}, f32[512,128]{1,0:T(8,128)S(1)}, u32[]{:S(2)}, u32[]{:S(2)}) collective-permute-start(f32[512,128]{1,0:T(8,128)S(1)} %get-tuple-element.50), channel_id=1, source_target_pairs={{0,1},{1,2},{2,3},{3,0},{4,5},{5,6},{6,7},{7,4},{8,9},{9,10},{10,1... | collective-permute-start | bytes 786440 | tf_op jit(solution)/shard_map/ppermute | solution.py:282
  3.6 15.5 %collective-permute-start.9 = (f32[512,128]{1,0:T(8,128)S(1)}, f32[512,128]{1,0:T(8,128)S(1)}, u32[]{:S(2)}, u32[]{:S(2)}) collective-permute-start(f32[512,128]{1,0:T(8,128)S(1)} %get-tuple-element.51), channel_id=1, source_target_pairs={{0,2},{1,3},{2,0},{3,1},{4,6},{5,7},{6,4},{7,5},{8,10},{9,11},{10,... | collective-permute-start | bytes 786440 | tf_op jit(solution)/shard_map/ppermute | solution.py:282
  6.4 12.8 %collective-permute-start.10 = (f32[512,128]{1,0:T(8,128)S(1)}, f32[512,128]{1,0:T(8,128)S(1)}, u32[]{:S(2)}, u32[]{:S(2)}) collective-permute-start(f32[512,128]{1,0:T(8,128)S(1)} %get-tuple-element.52), channel_id=1, source_target_pairs={{0,3},{1,0},{2,1},{3,2},{4,7},{5,4},{6,5},{7,6},{8,11},{9,8},{10,9... | collective-permute-start | bytes 786440 | tf_op jit(solution)/shard_map/ppermute | solution.py:282
  7.8 31.9 %copy-start.2 = (f32[1,2,4,256,256]{4,3,2,1,0:T(8,128)S(1)}, f32[1,2,4,256,256]{4,3,2,1,0:T(8,128)}, u32[]{:S(2)}) copy-start(f32[1,2,4,256,256]{4,3,2,1,0:T(8,128)} %forcing_ref.1) | copy-start | bytes 6291460
  10.4 2.1 %collective-permute-start = (f32[12,256]{1,0:T(8,128)S(1)}, f32[12,256]{1,0:T(8,128)S(1)}, u32[]{:S(2)}, u32[]{:S(2)}) collective-permute-start(f32[12,256]{1,0:T(8,128)S(1)} %get-tuple-element.35), channel_id=1, source_target_pairs={{0,128},{1,129},{2,130},{3,131},{4,132},{5,133},{6,134},{7,135},{8... | collective-permute-start | bytes 36872 | tf_op jit(solution)/shard_map/ppermute | solution.py:314
  12.8 30.2 %collective-permute-start.1 = (f32[560,128]{1,0:T(8,128)S(1)}, f32[560,128]{1,0:T(8,128)S(1)}, u32[]{:S(2)}, u32[]{:S(2)}) collective-permute-start(f32[560,128]{1,0:T(8,128)S(1)} %get-tuple-element.37), channel_id=1, source_target_pairs={{0,1},{1,2},{2,3},{3,0},{4,5},{5,6},{6,7},{7,4},{8,9},{9,10},{10,1... | collective-permute-start | bytes 860168 | tf_op jit(solution)/shard_map/ppermute | solution.py:282
  13.5 29.6 %collective-permute-start.2 = (f32[560,128]{1,0:T(8,128)S(1)}, f32[560,128]{1,0:T(8,128)S(1)}, u32[]{:S(2)}, u32[]{:S(2)}) collective-permute-start(f32[560,128]{1,0:T(8,128)S(1)} %get-tuple-element.38), channel_id=1, source_target_pairs={{0,2},{1,3},{2,0},{3,1},{4,6},{5,7},{6,4},{7,5},{8,10},{9,11},{10,... | collective-permute-start | bytes 860168 | tf_op jit(solution)/shard_map/ppermute | solution.py:282
  14.3 28.7 %collective-permute-start.3 = (f32[560,128]{1,0:T(8,128)S(1)}, f32[560,128]{1,0:T(8,128)S(1)}, u32[]{:S(2)}, u32[]{:S(2)}) collective-permute-start(f32[560,128]{1,0:T(8,128)S(1)} %get-tuple-element.39), channel_id=1, source_target_pairs={{0,3},{1,0},{2,1},{3,2},{4,7},{5,4},{6,5},{7,6},{8,11},{9,8},{10,9... | collective-permute-start | bytes 860168 | tf_op jit(solution)/shard_map/ppermute | solution.py:282
  23.3 37.9 %collective-permute-start.11 = (f32[512,128]{1,0:T(8,128)S(1)}, f32[512,128]{1,0:T(8,128)S(1)}, u32[]{:S(2)}, u32[]{:S(2)}) collective-permute-start(f32[512,128]{1,0:T(8,128)S(1)} %get-tuple-element.54), channel_id=1, source_target_pairs={{0,3},{1,0},{2,1},{3,2},{4,7},{5,4},{6,5},{7,6},{8,11},{9,8},{10,9... | collective-permute-start | bytes 786440 | tf_op jit(solution)/shard_map/ppermute | solution.py:282
  24.6 9.5 %collective-permute-start.4 = (f32[4,256]{1,0:T(4,128)S(1)}, f32[4,256]{1,0:T(4,128)S(1)}, u32[]{:S(2)}, u32[]{:S(2)}) collective-permute-start(f32[4,256]{1,0:T(4,128)S(1)} %get-tuple-element.41), channel_id=1, source_target_pairs={{0,4},{4,8},{8,12},{12,16},{16,20},{20,24},{24,28},{28,32},{32,36}... | collective-permute-start | bytes 12296 | tf_op jit(solution)/shard_map/ppermute | solution.py:334
  34.1 13.4 %copy-start.3 = (f32[1,256,256]{2,1,0:T(8,128)S(1)}, f32[1,256,256]{2,1,0:T(8,128)}, u32[]{:S(2)}) copy-start(f32[1,256,256]{2,1,0:T(8,128)} %depth_ref.3) | copy-start | bytes 786436
  34.1 13.4 %copy-start.4 = (s32[1,256,256]{2,1,0:T(8,128)S(1)}, s32[1,256,256]{2,1,0:T(8,128)}, u32[]{:S(2)}) copy-start(s32[1,256,256]{2,1,0:T(8,128)} %wet_ref.3) | copy-start | bytes 786436
  34.1 5.6 %collective-permute-start.5 = (f32[4,256]{1,0:T(4,128)S(1)}, f32[4,256]{1,0:T(4,128)S(1)}, u32[]{:S(2)}, u32[]{:S(2)}) collective-permute-start(f32[4,256]{1,0:T(4,128)S(1)} %get-tuple-element.42), channel_id=1, source_target_pairs={{4,0},{8,4},{12,8},{16,12},{20,16},{24,20},{28,24},{32,28},{36,32}... | collective-permute-start | bytes 12296 | tf_op jit(solution)/shard_map/ppermute | solution.py:333
  47.6 11.2 %collective-permute-start.6 = (f32[4,256]{1,0:T(4,128)S(1)}, f32[4,256]{1,0:T(4,128)S(1)}, u32[]{:S(2)}, u32[]{:S(2)}) collective-permute-start(f32[4,256]{1,0:T(4,128)S(1)} %get-tuple-element.44), channel_id=1, source_target_pairs={{0,4},{4,8},{8,12},{12,16},{16,20},{20,24},{24,28},{28,32},{32,36}... | collective-permute-start | bytes 12296 | tf_op jit(solution)/shard_map/ppermute | solution.py:375
  49.5 11.7 %collective-permute-start.7 = (f32[4,256]{1,0:T(4,128)S(1)}, f32[4,256]{1,0:T(4,128)S(1)}, u32[]{:S(2)}, u32[]{:S(2)}) collective-permute-start(f32[4,256]{1,0:T(4,128)S(1)} %get-tuple-element.45), channel_id=1, source_target_pairs={{4,0},{8,4},{12,8},{16,12},{20,16},{24,20},{28,24},{32,28},{36,32}... | collective-permute-start | bytes 12296 | tf_op jit(solution)/shard_map/ppermute | solution.py:374
  55.5 10.9 %collective-permute-start.12 = (f32[512,128]{1,0:T(8,128)S(1)}, f32[512,128]{1,0:T(8,128)S(1)}, u32[]{:S(2)}, u32[]{:S(2)}) collective-permute-start(f32[512,128]{1,0:T(8,128)S(1)} %get-tuple-element.55), channel_id=1, source_target_pairs={{0,2},{1,3},{2,0},{3,1},{4,6},{5,7},{6,4},{7,5},{8,10},{9,11},{10,... | collective-permute-start | bytes 786440 | tf_op jit(solution)/shard_map/ppermute | solution.py:282
  57.9 16.1 %collective-permute-start.13 = (f32[512,128]{1,0:T(8,128)S(1)}, f32[512,128]{1,0:T(8,128)S(1)}, u32[]{:S(2)}, u32[]{:S(2)}) collective-permute-start(f32[512,128]{1,0:T(8,128)S(1)} %get-tuple-element.56), channel_id=1, source_target_pairs={{0,1},{1,2},{2,3},{3,0},{4,5},{5,6},{6,7},{7,4},{8,9},{9,10},{10,1... | collective-permute-start | bytes 786440 | tf_op jit(solution)/shard_map/ppermute | solution.py:282
  58.7 15.3 %collective-permute-start.14 = (f32[512,128]{1,0:T(8,128)S(1)}, f32[512,128]{1,0:T(8,128)S(1)}, u32[]{:S(2)}, u32[]{:S(2)}) collective-permute-start(f32[512,128]{1,0:T(8,128)S(1)} %get-tuple-element.58), channel_id=1, source_target_pairs={{0,3},{1,0},{2,1},{3,2},{4,7},{5,4},{6,5},{7,6},{8,11},{9,8},{10,9... | collective-permute-start | bytes 786440 | tf_op jit(solution)/shard_map/ppermute | solution.py:282
  61.2 15.7 %collective-permute-start.15 = (f32[512,128]{1,0:T(8,128)S(1)}, f32[512,128]{1,0:T(8,128)S(1)}, u32[]{:S(2)}, u32[]{:S(2)}) collective-permute-start(f32[512,128]{1,0:T(8,128)S(1)} %get-tuple-element.59), channel_id=1, source_target_pairs={{0,2},{1,3},{2,0},{3,1},{4,6},{5,7},{6,4},{7,5},{8,10},{9,11},{10,... | collective-permute-start | bytes 786440 | tf_op jit(solution)/shard_map/ppermute | solution.py:282
  61.2 18.2 %collective-permute-start.16 = (f32[512,128]{1,0:T(8,128)S(1)}, f32[512,128]{1,0:T(8,128)S(1)}, u32[]{:S(2)}, u32[]{:S(2)}) collective-permute-start(f32[512,128]{1,0:T(8,128)S(1)} %get-tuple-element.60), channel_id=1, source_target_pairs={{0,1},{1,2},{2,3},{3,0},{4,5},{5,6},{6,7},{7,4},{8,9},{9,10},{10,1... | collective-permute-start | bytes 786440 | tf_op jit(solution)/shard_map/ppermute | solution.py:282

commit v2 on v1

v2 whole, which is shorter than its diff:
```python
import functools

import jax
import jax.numpy as jnp
from jax import lax
from jax.experimental import pallas as pl
from jax.experimental.pallas import tpu as pltpu
from jax.sharding import PartitionSpec as P

K = 8
NT = 64
CELLS = 256
RING = 4
LANES = 128
UPPER = 32
LOWER = 32
ROWS_UP = RING * UPPER
ROWS_LOW = RING * LOWER
REACH = 16
relax_step = 0.3
speed_floor = 0.01
omega_step = 0.1
TURN = 6.283185307179586 / NT
F32 = jnp.float32
BF16 = jnp.bfloat16
I32 = jnp.int32
MIB = 1 << 20


def params(mib=48):
    return pltpu.CompilerParams(vmem_limit_bytes=mib * MIB)


def cost(us):
    return pl.CostEstimate(flops=0, bytes_accessed=int(us * 3.0e6), transcendentals=0)


def vmem(count):
    return [pl.BlockSpec(memory_space=pltpu.VMEM)] * count


def dot(a, b):
    return jnp.dot(a, b, preferred_element_type=F32)


def pair(x):
    high = x.astype(BF16)
    return high, (x - high.astype(F32)).astype(BF16)


def iota(shape, dim):
    return lax.broadcasted_iota(I32, shape, dim)


def trig(freq_ref, me, time, slot, channel):
    owner = (me - slot + RING) & (RING - 1)
    constituent = owner * 2 + (channel >> 1)
    cycles = jnp.zeros(time.shape, I32)
    for k in range(K):
        cycles = jnp.where(constituent == k, freq_ref[k] + 1, cycles)
    angle = ((time * cycles) & (NT - 1)).astype(F32) * TURN
    return jnp.where((channel & 1) == 0, jnp.cos(angle), jnp.sin(angle))


def prepare(freq_ref, index_ref, fields_ref, strip_ref, forward_ref, backward_ref):
    me = lax.axis_index("harm")
    index = index_ref[...]
    row_of, col_of = index >> 8, index & (CELLS - 1)
    pick = jnp.where(iota((CELLS, CELLS), 0) == col_of, 1.0, 0.0).astype(BF16)
    picks = jnp.concatenate([pick, pick, pick], 0)
    at_row = iota((CELLS, CELLS), 0) == row_of
    for k in range(12):
        plane = fields_ref[k]
        high, rest = plane.astype(BF16), None
        rest = plane - high.astype(F32)
        mid, low = pair(rest)
        column = dot(jnp.concatenate([high, mid, low], 1), picks)
        strip_ref[k : k + 1, :] = jnp.sum(jnp.where(at_row, column, 0.0), axis=0, keepdims=True)
    shape = (128, 96)
    row, col = iota(shape, 0), iota(shape, 1)
    part, lane = col >> 5, col & 31
    value = trig(freq_ref, me, row & 63, lane >> 3, lane & 3)
    value = jnp.where((row >> 6) == ((lane >> 2) & 1), value, 0.0)
    high = value.astype(BF16).astype(F32)
    forward_ref[...] = jnp.where(part == 1, value - high, high).astype(BF16)
    shape = (64, 256)
    row, col = iota(shape, 0), iota(shape, 1)
    lane = row & 31
    value = trig(freq_ref, me, col & 63, lane >> 3, lane & 3) * (1.0 / NT)
    value = jnp.where(((col >> 6) & 1) == ((lane >> 2) & 1), value, 0.0)
    high = value.astype(BF16).astype(F32)
    low = jnp.where(col < 128, value - high, 0.0)
    backward_ref[...] = jnp.where(row < 32, high, low).astype(BF16)


def piece(state_ref, out_ref, sem, row, size, j):
    return pltpu.make_async_copy(
        state_ref.at[0, pl.ds(1, 2), :, pl.ds(row, size), pl.ds(j * LANES, LANES)],
        out_ref.reshape(2, 4, size, LANES),
        sem,
    )


def pack_upper(state_ref, *refs):
    outs, sems = refs[:RING], refs[RING]
    me = lax.axis_index("harm")
    copies = []
    for slot in (1, 3, 2, 0):
        row = pl.multiple_of(((me + slot) & (RING - 1)) * UPPER, UPPER)
        for j in range(2):
            out_ref = outs[slot].at[pl.ds(8 * UPPER * j, 8 * UPPER), :]
            copies.append(piece(state_ref, out_ref, sems.at[slot, j], row, UPPER, j))
    for copy in copies:
        copy.start()
    for copy in copies:
        copy.wait()


def pack_lower(strip_ref, state_ref, *refs):
    outs, (first_ref, last_ref, edges, sems, edge_sems) = refs[:RING], refs[RING:]
    me = lax.axis_index("harm")
    shelf = lax.axis_index("sec") == 1
    copies = []
    for e, row in enumerate((0, CELLS - 8)):
        copies.append(
            pltpu.make_async_copy(state_ref.at[0, :, :, pl.ds(row, 8), :], edges.at[e], edge_sems.at[e])
        )
    for slot in range(RING):
        row = pl.multiple_of(ROWS_UP + ((me + slot) & (RING - 1)) * LOWER, 8)
        for j in range(2):
            out_ref = outs[slot].at[pl.ds(8 * LOWER * j, 8 * LOWER), :]
            copies.append(piece(state_ref, out_ref, sems.at[slot, j], row, LOWER, j))
    for copy in copies:
        copy.start()
    for copy in copies[:2]:
        copy.wait()
    strip = strip_ref[...]
    take = jnp.logical_and(iota((12, CELLS), 1) == 0, shelf)
    first = edges[0].reshape(12, 8, CELLS)[:, 0, :]
    last = edges[1].reshape(12, 8, CELLS)[:, 7, :]
    first = jnp.where(take, strip[:, 0:1], first)
    last = jnp.where(take, strip[:, CELLS - 1 : CELLS], last)
    first_ref[...] = first[0:4]
    last_ref[...] = last[0:4]
    for e, values in enumerate((strip, first, last)):
        for j in range(2):
            row = 16 * LOWER + 24 * j + 8 * e
            for out_ref in outs:
                out_ref[row : row + 8, :] = values[4:12, j * LANES : (j + 1) * LANES]
    for copy in copies[2:]:
        copy.wait()


def terms(forward, backward, x):
    high, low = pair(x)
    samples = dot(forward, jnp.concatenate([high, high, low], 0))
    east, north = samples[:NT], samples[NT:]
    square = east * east + north * north + speed_floor
    speed = square * lax.rsqrt(square)
    high, low = pair(jnp.concatenate([speed * east, speed * north], 0))
    both = dot(backward, jnp.concatenate([high, low], 0))
    return both[:32] + both[32:]


def rows_terms(size, forward, backward, xs, outs):
    def step(r, carry):
        rows = [pl.ds(8 * size * j + r, 8, stride=size) for j in range(2)]
        halves = [jnp.concatenate([ref[rows[j], :] for ref in xs], 0) for j in range(2)]
        out = terms(forward, backward, jnp.concatenate(halves, 1))
        for slot in range(RING):
            for j in range(2):
                outs[slot][rows[j], :] = out[8 * slot : 8 * slot + 8, j * LANES : (j + 1) * LANES]
        return carry

    lax.fori_loop(0, size, step, 0, unroll=4)


def friction_upper(forward_ref, backward_ref, behind_ref, *refs):
    rows_terms(UPPER, forward_ref[...], backward_ref[...], refs[:RING], refs[RING:])


def friction_lower(forward_ref, backward_ref, behind_ref, *refs):
    xs, outs, extra_ref = refs[:RING], refs[RING : 2 * RING], refs[2 * RING]
    forward, backward = forward_ref[...], backward_ref[...]
    rows_terms(LOWER, forward, backward, xs, outs)
    for e in range(3):
        rows = [pl.ds(16 * LOWER + 24 * j + 8 * e, 8) for j in range(2)]
        halves = [jnp.concatenate([ref[rows[j], :] for ref in xs], 0) for j in range(2)]
        extra_ref[8 * e : 8 * e + 8, :] = terms(forward, backward, jnp.concatenate(halves, 1))[:8]


def left_right(x):
    lane = iota(x.shape, 1)
    right = jnp.where(lane == CELLS - 1, 0.0, pltpu.roll(x, CELLS - 1, 1))
    left = jnp.where(lane == 0, 0.0, pltpu.roll(x, 1, 1))
    return right - left


def up_down(x, before, after):
    count = x.shape[0]
    row = iota(x.shape, 0)
    down = jnp.where(row == count - 1, after, pltpu.roll(x, count - 1, 0))
    up = jnp.where(row == 0, before, pltpu.roll(x, 1, 0))
    return down - up


def known(freq_ref, strip_ref, before_ref, after_ref, state_ref, forcing_ref, east_ref, north_ref, eta_ref, edge_ref):
    me = lax.axis_index("harm")
    shelf = lax.axis_index("sec") == 1
    take = jnp.logical_and(iota((CELLS, CELLS), 1) == 0, shelf)
    columns = jnp.concatenate([strip_ref[...], jnp.zeros((4, CELLS), F32)], 0).T

    def field(f, ch):
        k = 4 * f + ch
        return jnp.where(take, columns[:, k : k + 1], state_ref[0, f, ch])

    for i in range(2):
        omega = omega_step * (freq_ref[2 * me + i] + 1).astype(F32)
        eta = [field(0, 2 * i + p) for p in range(2)]
        for p in range(2):
            ch = 2 * i + p
            turn = -omega if p else omega
            eta_ref[ch] = eta[p] - relax_step * (turn * eta[1 - p])
        east = [field(1, 2 * i + p) for p in range(2)]
        for p in range(2):
            ch = 2 * i + p
            turn = -omega if p else omega
            rest = turn * east[1 - p] + 0.5 * left_right(eta[p]) - forcing_ref[0, 0, ch]
            east_ref[ch] = east[p] - relax_step * rest
        north = [field(2, 2 * i + p) for p in range(2)]
        for p in range(2):
            ch = 2 * i + p
            turn = -omega if p else omega
            slope = up_down(eta[p], before_ref[ch : ch + 1, :], after_ref[ch : ch + 1, :])
            rest = turn * north[1 - p] + 0.5 * slope - forcing_ref[0, 1, ch]
            value = north[p] - relax_step * rest
            north_ref[ch] = value
            edge_ref[ch : ch + 1, :] = value[0:1, :]
            edge_ref[4 + ch : 5 + ch, :] = value[CELLS - 1 : CELLS, :]


def edge_flux(edge_ref, extra_ref, depth_ref, wet_ref, first_ref, last_ref):
    for out_ref, at, row in ((first_ref, 0, 0), (last_ref, 1, CELLS - 1)):
        height = depth_ref[0, row : row + 1, :]
        wet = wet_ref[0, row : row + 1, :].astype(F32)
        drag = extra_ref[8 + 8 * at + 4 : 8 + 8 * at + 8, :]
        north = wet * (edge_ref[4 * at : 4 * at + 4, :] - (relax_step / height) * drag)
        out_ref[...] = height * north


def transports(start, size, turned, extra_ref, depth_ref, wet_ref, sources, drags, store):
    me = lax.axis_index("harm")
    shelf = lax.axis_index("sec") == 1
    take = jnp.logical_and(iota((size, LANES), 1) == 0, shelf)
    turned[...] = extra_ref[0:8, :].T
    for slot in range(RING):
        at = pl.multiple_of(((me + slot) & (RING - 1)) * size, 8)
        rows = pl.ds(start + at, size)
        columns = turned[rows, :]
        wet = wet_ref[0, rows, :].astype(F32)
        factor = relax_step / depth_ref[0, rows, :]
        for k in range(8):
            left, right = (
                drags[slot][pl.ds((8 * j + k) * size, size), :] for j in range(2)
            )
            left = jnp.where(take, columns[:, k : k + 1], left)
            drag = jnp.concatenate([left, right], 1)
            store(1 + k // 4, k % 4, at, wet * (sources[k // 4][k % 4, rows, :] - factor * drag))


def new_eta(east, north, before, after, height, wet, eta):
    slope = left_right(height * east) + up_down(height * north, before, after)
    return wet * (eta - (0.5 * relax_step) * slope)


def finish_upper(extra_ref, depth_ref, wet_ref, east_ref, north_ref, eta_ref, *refs):
    slots, (out_ref, carry_ref, made, turned, sems) = refs[:RING], refs[RING:]

    def store(f, ch, row, value):
        made[f, ch, pl.ds(row, UPPER), :] = value

    transports(0, UPPER, turned, extra_ref, depth_ref, wet_ref, (east_ref, north_ref), slots, store)
    copies = []
    for f in (1, 2, 0):
        if f == 0:
            height = depth_ref[0, :ROWS_UP, :]
            wet = wet_ref[0, :ROWS_UP, :].astype(F32)
            for ch in range(4):
                made[0, ch] = new_eta(made[1, ch], made[2, ch], 0.0, 0.0, height, wet, eta_ref[ch, :ROWS_UP, :])
        copy = pltpu.make_async_copy(made.at[f], out_ref.at[0, f, :, pl.ds(0, ROWS_UP), :], sems.at[f])
        copy.start()
        copies.append(copy)
    for f in range(2):
        for ch in range(4):
            carry_ref[f, ch, :REACH, :] = made[1 + f, ch, :REACH, :]
            carry_ref[f, ch, REACH:, :] = made[1 + f, ch, ROWS_UP - REACH :, :]
    for copy in copies:
        copy.wait()


def finish_lower(
    extra_ref, before_ref, after_ref, depth_ref, wet_ref, east_ref, north_ref, eta_ref, carry_ref, begun_ref, *refs
):
    slots, (out_ref, made, level, top, turned, sems, level_sems) = refs[:RING], refs[RING:]
    top_row = ROWS_UP - REACH
    for f in range(2):
        for ch in range(4):
            made[f, ch, :REACH, :] = carry_ref[f, ch, REACH:, :]

    def store(f, ch, row, value):
        made[f - 1, ch, pl.ds(REACH + row, LOWER), :] = value

    transports(ROWS_UP, LOWER, turned, extra_ref, depth_ref, wet_ref, (east_ref, north_ref), slots, store)
    copies = []

    def send(source, target, sem):
        copy = pltpu.make_async_copy(source, target, sem)
        copy.start()
        copies.append(copy)

    for f in range(2):
        send(
            made.at[f, :, pl.ds(REACH, ROWS_LOW), :],
            out_ref.at[0, 1 + f, :, pl.ds(ROWS_UP, ROWS_LOW), :],
            sems.at[f],
        )
    height = depth_ref[0, :REACH, :]
    wet = wet_ref[0, :REACH, :].astype(F32)
    for ch in range(4):
        value = new_eta(
            carry_ref[0, ch, :REACH, :], carry_ref[1, ch, :REACH, :], before_ref[ch : ch + 1, :], 0.0,
            height, wet, eta_ref[ch, :REACH, :],
        )
        top[ch] = value[:8]
    send(top, out_ref.at[0, 0, :, pl.ds(0, 8), :], sems.at[2])
    height = depth_ref[0, top_row:, :]
    wet = wet_ref[0, top_row:, :].astype(F32)
    for ch in range(4):
        level[ch] = new_eta(
            made[0, ch], made[1, ch], 0.0, after_ref[ch : ch + 1, :], height, wet, eta_ref[ch, top_row:, :]
        )
        send(
            level.at[ch, pl.ds(8, ROWS_LOW + REACH - 8), :],
            out_ref.at[0, 0, ch, pl.ds(top_row + 8, ROWS_LOW + REACH - 8), :],
            level_sems.at[ch],
        )
    for copy in copies:
        copy.wait()


def around(value, steps):
    return lax.ppermute(value, "harm", [(i, (i + steps) % RING) for i in range(RING)])


def body(state, forcing, depth, wet_mask, nest_index, freq_order):
    me = lax.axis_index("harm")
    tiles = lax.axis_size("tile")
    smem = pl.BlockSpec(memory_space=pltpu.SMEM)
    hbm = pl.BlockSpec(memory_space=pl.ANY)
    main = pl.BlockSpec(memory_space=pltpu.HBM)
    array = jax.ShapeDtypeStruct

    upper = array((16 * UPPER, LANES), F32)
    parts = pl.pallas_call(
        pack_upper,
        name="pack_upper",
        in_specs=[hbm],
        out_specs=vmem(RING),
        out_shape=(upper,) * RING,
        scratch_shapes=[pltpu.SemaphoreType.DMA((RING, 2))],
        compiler_params=params(),
        cost_estimate=cost(2),
    )(state)
    raw = [parts[0]] + [around(parts[slot], slot) for slot in (1, 2, 3)]

    strip, forward, backward = pl.pallas_call(
        prepare,
        name="prepare",
        in_specs=[smem] + vmem(2),
        out_specs=vmem(3),
        out_shape=(array((12, CELLS), F32), array((128, 96), BF16), array((64, 256), BF16)),
        compiler_params=params(),
        cost_estimate=cost(4),
    )(freq_order, nest_index.reshape(1, CELLS), state.reshape(12, CELLS, CELLS))
    strip = lax.ppermute(strip, "sec", [(0, 1)])

    edge_eta = array((4, CELLS), F32)
    packed = pl.pallas_call(
        pack_lower,
        name="pack_lower",
        in_specs=vmem(1) + [hbm],
        out_specs=vmem(RING + 2),
        out_shape=(array((16 * LOWER + 48, LANES), F32),) * RING + (edge_eta, edge_eta),
        scratch_shapes=[
            pltpu.VMEM((2, 3, 4, 8, CELLS), F32),
            pltpu.SemaphoreType.DMA((RING, 2)),
            pltpu.SemaphoreType.DMA((2,)),
        ],
        compiler_params=params(),
        cost_estimate=cost(2),
    )(strip, state)
    first, last = packed[RING:]
    raw_lower = [packed[0]] + [around(packed[slot], slot) for slot in (1, 2, 3)]
    to_next = [(i, i + 1) for i in range(tiles - 1)]
    to_last = [(i + 1, i) for i in range(tiles - 1)]
    after = lax.ppermute(first, "tile", to_last)
    before = lax.ppermute(last, "tile", to_next)

    plane = array((4, CELLS, CELLS), F32)
    east, north, eta, edge = pl.pallas_call(
        known,
        name="known",
        in_specs=[smem] + vmem(5),
        out_specs=vmem(4),
        out_shape=(plane, plane, plane, array((8, CELLS), F32)),
        compiler_params=params(),
        cost_estimate=cost(5),
    )(freq_order, strip, before, after, state, forcing)

    made = pl.pallas_call(
        friction_upper,
        name="friction_upper",
        in_specs=vmem(2) + [hbm] + vmem(RING),
        out_specs=vmem(RING),
        out_shape=(upper,) * RING,
        compiler_params=params(),
        cost_estimate=cost(4),
    )(forward, backward, edge, *raw)
    drags = [made[0]] + [around(made[slot], -slot) for slot in (1, 2, 3)]
    made = pl.pallas_call(
        friction_lower,
        name="friction_lower",
        in_specs=vmem(2) + [hbm] + vmem(RING),
        out_specs=vmem(RING + 1),
        out_shape=(array((16 * LOWER, LANES), F32),) * RING + (array((24, CELLS), F32),),
        compiler_params=params(),
        cost_estimate=cost(4),
    )(forward, backward, made[0], *raw_lower)
    extra = made[RING]
    drags_lower = [made[0]] + [around(made[slot], -slot) for slot in (1, 2, 3)]

    first, last = pl.pallas_call(
        edge_flux,
        name="edge_flux",
        in_specs=vmem(4),
        out_specs=vmem(2),
        out_shape=(edge_eta, edge_eta),
        compiler_params=params(),
        cost_estimate=cost(1),
    )(edge, extra, depth, wet_mask)
    after_flux = lax.ppermute(first, "tile", to_last)
    before_flux = lax.ppermute(last, "tile", to_next)

    whole = array((1, 3, 4, CELLS, CELLS), F32)
    begun, carry = pl.pallas_call(
        finish_upper,
        name="finish_upper",
        in_specs=vmem(6 + RING),
        out_specs=[hbm, vmem(1)[0]],
        out_shape=(whole, array((2, 4, 2 * REACH, CELLS), F32)),
        scratch_shapes=[
            pltpu.VMEM((3, 4, ROWS_UP, CELLS), F32),
            pltpu.VMEM((CELLS, 8), F32),
            pltpu.SemaphoreType.DMA((3,)),
        ],
        compiler_params=params(),
        cost_estimate=cost(3),
    )(extra, depth, wet_mask, east, north, eta, *drags)
    return pl.pallas_call(
        finish_lower,
        name="finish_lower",
        in_specs=vmem(9) + [hbm] + vmem(RING),
        out_specs=hbm,
        out_shape=whole,
        input_output_aliases={9: 0},
        scratch_shapes=[
            pltpu.VMEM((2, 4, REACH + ROWS_LOW, CELLS), F32),
            pltpu.VMEM((4, REACH + ROWS_LOW, CELLS), F32),
            pltpu.VMEM((4, 8, CELLS), F32),
            pltpu.VMEM((CELLS, 8), F32),
            pltpu.SemaphoreType.DMA((3,)),
            pltpu.SemaphoreType.DMA((4,)),
        ],
        compiler_params=params(),
        cost_estimate=cost(3),
    )(extra, before_flux, after_flux, depth, wet_mask, east, north, eta, carry, begun, *drags_lower)


def solution(mesh):
    in_specs = (
        P("sec", None, "harm", "tile", None),
        P("sec", None, "harm", "tile", None),
        P("sec", "tile", None),
        P("sec", "tile", None),
        P("tile"),
        P(),
    )
    out_specs = P("sec", None, "harm", "tile", None)
    return jax.shard_map(body, mesh=mesh, in_specs=in_specs, out_specs=out_specs, check_vma=False)
```

time: 83.3 us -> 65.4 us (0.79); the launches traced: 83 us -> 64.3 us
  waiting for transfers between devices: 28.1 us -> 8.43 us
    ppermute x12, waiting for transfers between devices: 20 us -> 6.98 us  [around(): lax.ppermute(value, 'harm', [(i, (i + steps) % RING) for i in range(RING)])]
    ppermute x2, waiting for transfers between devices: 7.26 us -> 0.62 us  [the longest x1 0.62 us: body(): after = lax.ppermute(first, 'tile', to_last)]
    ppermute x2, starting transfers between devices: 7.85 us -> 9.86 us  [the longest x1 6.04 us: body(): after = lax.ppermute(first, 'tile', to_last)]
    ppermute x12, starting transfers between devices: 17.2 us -> 16 us  [around(): lax.ppermute(value, 'harm', [(i, (i + steps) % RING) for i in range(RING)])]
    pallas_call x3 -> x4, Pallas kernels: 12.2 us -> 12.3 us  [the longest x1 4.43 us: body(): pl.pallas_call(friction_lower, name='friction_lower', in_specs=vmem(2) +...]
  transfers between devices with their start and end apart: 17 -> 17, of which waited for: 8 -> 5; matrix products, arithmetic and copies ran while one was open for 0% -> 0% of each run, Pallas kernels for 18% -> 26%
where the time goes in v2:
time: 65.4 us; the launch traced here: 64.3 us
  starting transfers between devices  35 us (54%)
  Pallas kernels  18.6 us (28%)
  waiting for transfers between devices  8.43 us (13%)
  local copies, waits for them, and re-layouts  1.91 us (3%)
    ppermute x12, starting transfers between devices, around(): lax.ppermute(value, 'harm', [(i, (i + steps) % RING) for i in range(RING)])  16 us
    ppermute x12, waiting for transfers between devices, around(): lax.ppermute(value, 'harm', [(i, (i + steps) % RING) for i in range(RING)])  6.98 us
    ppermute x1, starting transfers between devices, body(): after = lax.ppermute(first, 'tile', to_last)  6.04 us
    ppermute x1, starting transfers between devices, body(): after_flux = lax.ppermute(first, 'tile', to_last)  5.94 us
    pallas_call x1, Pallas kernels, body(): pl.pallas_call(friction_lower, name='friction_lower', in_specs=vmem(2) +...  4.43 us
    pallas_call x1, Pallas kernels, body(): pl.pallas_call(friction_upper, name='friction_upper', in_specs=vmem(2) +...  4.09 us
    ppermute x1, starting transfers between devices, body(): before = lax.ppermute(last, 'tile', to_next)  3.83 us
    pallas_call x1, Pallas kernels, body(): pl.pallas_call(known, name='known', in_specs=[smem] + vmem(5), out_specs=...  3.3 us
  transfers between devices with their start and end apart: 17, of which 5 were waited for; matrix products, arithmetic and copies ran while one was open for 0% of the time, Pallas kernels for 26%

profile of v2, /device:TPU:24, one launch (start us, length us, event | category | flops | bytes accessed | tf_op | source)
XLA Modules:
  0.0 64.3 jit_solution(4622707090991465170)
XLA Ops:
  0.0 0.0 copy-start
  0.0 1.9 %copy-done = f32[1,3,4,256,256]{4,3,2,1,0:T(8,128)S(1)} copy-done((f32[1,3,4,256,256]{4,3,2,1,0:T(8,128)S(1)}, f32[1,3,4,256,256]{4,3,2,1,0:T(8,128)}, u32[]{:S(2)}) %copy-start) | copy-done | bytes 3145752
  1.9 0.0 copy-start.1
  1.9 0.0 copy-start.5
  1.9 0.0 copy-start.6
  1.9 0.2 pack_upper.1
  2.1 1.6 %collective-permute-start.3 = (f32[512,128]{1,0:T(8,128)S(1)}, f32[512,128]{1,0:T(8,128)S(1)}, u32[]{:S(2)}, u32[]{:S(2)}) collective-permute-start(f32[512,128]{1,0:T(8,128)S(1)} %get-tuple-element.42), channel_id=1, source_target_pairs={{0,1},{1,2},{2,3},{3,0},{4,5},{5,6},{6,7},{7,4},{8,9},{9,10},{10,1... | collective-permute-start | bytes 786440 | tf_op jit(solution)/shard_map/ppermute | solution.py:352
  3.6 2.7 %collective-permute-start.4 = (f32[512,128]{1,0:T(8,128)S(1)}, f32[512,128]{1,0:T(8,128)S(1)}, u32[]{:S(2)}, u32[]{:S(2)}) collective-permute-start(f32[512,128]{1,0:T(8,128)S(1)} %get-tuple-element.43), channel_id=1, source_target_pairs={{0,2},{1,3},{2,0},{3,1},{4,6},{5,7},{6,4},{7,5},{8,10},{9,11},{10,... | collective-permute-start | bytes 786440 | tf_op jit(solution)/shard_map/ppermute | solution.py:352
  6.4 1.4 %collective-permute-start.5 = (f32[512,128]{1,0:T(8,128)S(1)}, f32[512,128]{1,0:T(8,128)S(1)}, u32[]{:S(2)}, u32[]{:S(2)}) collective-permute-start(f32[512,128]{1,0:T(8,128)S(1)} %get-tuple-element.44), channel_id=1, source_target_pairs={{0,3},{1,0},{2,1},{3,2},{4,7},{5,4},{6,5},{7,6},{8,11},{9,8},{10,9... | collective-permute-start | bytes 786440 | tf_op jit(solution)/shard_map/ppermute | solution.py:352
  7.8 0.0 copy-done.1
  7.8 0.0 copy-done.5
  7.8 0.0 copy-done.6
  7.8 0.0 copy-start.4
  7.8 2.5 %prepare.1 = (f32[12,256]{1,0:T(8,128)S(1)}, bf16[128,96]{1,0:T(8,128)(2,1)S(1)}, bf16[64,256]{1,0:T(8,128)(2,1)S(1)}) custom-call(s32[16]{0:T(128)S(1)} %copy-done.5, s32[1,256]{1,0:T(1,128)S(1)} %bitcast.3, f32[12,256,256]{2,1,0:T(8,128)S(1)} %bitcast.2), custom_call_target="tpu_custom_call" | custom-call | bytes 12000000 | tf_op jit(solution)/shard_map/prepare/pallas_call | solution.py:376
  10.4 1.3 %collective-permute-start = (f32[12,256]{1,0:T(8,128)S(1)}, f32[12,256]{1,0:T(8,128)S(1)}, u32[]{:S(2)}, u32[]{:S(2)}) collective-permute-start(f32[12,256]{1,0:T(8,128)S(1)} %get-tuple-element.37), channel_id=1, source_target_pairs={{0,128},{1,129},{2,130},{3,131},{4,132},{5,133},{6,134},{7,135},{8... | collective-permute-start | bytes 36872 | tf_op jit(solution)/shard_map/ppermute | solution.py:385
  11.7 0.8 %collective-permute-done.strip_ref = f32[12,256]{1,0:T(8,128)S(1)} collective-permute-done((f32[12,256]{1,0:T(8,128)S(1)}, f32[12,256]{1,0:T(8,128)S(1)}, u32[]{:S(2)}, u32[]{:S(2)}) %collective-permute-start) | collective-permute-done | bytes 12320 | tf_op jit(solution)/shard_map/ppermute | solution.py:385
  12.5 0.3 pack_lower.1
  12.8 3.8 %collective-permute-start.1 = (f32[4,256]{1,0:T(4,128)S(1)}, f32[4,256]{1,0:T(4,128)S(1)}, u32[]{:S(2)}, u32[]{:S(2)}) collective-permute-start(f32[4,256]{1,0:T(4,128)S(1)} %get-tuple-element.38), channel_id=1, source_target_pairs={{0,4},{4,8},{8,12},{12,16},{16,20},{20,24},{24,28},{28,32},{32,36}... | collective-permute-start | bytes 12296 | tf_op jit(solution)/shard_map/ppermute | solution.py:407
  16.6 6.0 %collective-permute-start.2 = (f32[4,256]{1,0:T(4,128)S(1)}, f32[4,256]{1,0:T(4,128)S(1)}, u32[]{:S(2)}, u32[]{:S(2)}) collective-permute-start(f32[4,256]{1,0:T(4,128)S(1)} %get-tuple-element.39), channel_id=1, source_target_pairs={{4,0},{8,4},{12,8},{16,12},{20,16},{24,20},{28,24},{32,28},{36,32}... | collective-permute-start | bytes 12296 | tf_op jit(solution)/shard_map/ppermute | solution.py:406
  22.7 0.0 collective-permute-done.1.before_ref
  22.7 0.7 %collective-permute-start.6 = (f32[560,128]{1,0:T(8,128)S(1)}, f32[560,128]{1,0:T(8,128)S(1)}, u32[]{:S(2)}, u32[]{:S(2)}) collective-permute-start(f32[560,128]{1,0:T(8,128)S(1)} %get-tuple-element.47), channel_id=1, source_target_pairs={{0,1},{1,2},{2,3},{3,0},{4,5},{5,6},{6,7},{7,4},{8,9},{9,10},{10,1... | collective-permute-start | bytes 860168 | tf_op jit(solution)/shard_map/ppermute | solution.py:352
  23.3 0.6 collective-permute-done.2.after_ref
  24.0 0.5 collective-permute-start.7
  24.5 0.0 collective-permute-done.3.refs_1_
  24.5 0.0 copy-start.2
  24.5 0.0 copy-start.3
  24.5 2.8 %collective-permute-start.8 = (f32[560,128]{1,0:T(8,128)S(1)}, f32[560,128]{1,0:T(8,128)S(1)}, u32[]{:S(2)}, u32[]{:S(2)}) collective-permute-start(f32[560,128]{1,0:T(8,128)S(1)} %get-tuple-element.49), channel_id=1, source_target_pairs={{0,3},{1,0},{2,1},{3,2},{4,7},{5,4},{6,5},{7,6},{8,11},{9,8},{10,9... | collective-permute-start | bytes 860168 | tf_op jit(solution)/shard_map/ppermute | solution.py:352
  27.2 0.0 copy-done.4
  27.2 3.3 %known.1 = (f32[4,256,256]{2,1,0:T(8,128)S(1)}, f32[4,256,256]{2,1,0:T(8,128)S(1)}, f32[4,256,256]{2,1,0:T(8,128)S(1)}, f32[8,256]{1,0:T(8,128)S(1)}) custom-call(s32[16]{0:T(128)S(1)} %copy-done.5, f32[12,256]{1,0:T(8,128)S(1)} %collective-permute-done.strip_ref, f32[4,256]{1,0:T(4,128)S(1)} %collective-permute-done.1.before_ref, ...), custom_call_target="tpu_custom_call" | custom-call | bytes 15000000 | tf_op jit(solution)/shard_map/known/pallas_call | solution.py:410
  30.6 0.0 collective-permute-done.4.refs_2_
  30.6 0.0 collective-permute-done.5.refs_3_
  30.6 4.1 %friction_upper.1 = (f32[512,128]{1,0:T(8,128)S(1)}, f32[512,128]{1,0:T(8,128)S(1)}, f32[512,128]{1,0:T(8,128)S(1)}, f32[512,128]{1,0:T(8,128)S(1)}) custom-call(bf16[128,96]{1,0:T(8,128)(2,1)S(1)} %get-tuple-element.35.forward_ref, bf16[64,256]{1,0:T(8,128)(2,1)S(1)} %get-tuple-element.36.backward_ref, f32[8,256]{1,0:T(8,128)S(1)} %get-tuple-element.40.behind_ref.edge_ref, ...), custom_call_target="tpu_custom_call" | custom-call | bytes 12000000 | tf_op jit(solution)/shard_map/friction_upper/pallas_call | solution.py:420
  34.7 0.9 %collective-permute-start.11 = (f32[512,128]{1,0:T(8,128)S(1)}, f32[512,128]{1,0:T(8,128)S(1)}, u32[]{:S(2)}, u32[]{:S(2)}) collective-permute-start(f32[512,128]{1,0:T(8,128)S(1)} %get-tuple-element.56), channel_id=1, source_target_pairs={{0,3},{1,0},{2,1},{3,2},{4,7},{5,4},{6,5},{7,6},{8,11},{9,8},{10,9... | collective-permute-start | bytes 786440 | tf_op jit(solution)/shard_map/ppermute | solution.py:352
  35.6 1.0 %collective-permute-start.12 = (f32[512,128]{1,0:T(8,128)S(1)}, f32[512,128]{1,0:T(8,128)S(1)}, u32[]{:S(2)}, u32[]{:S(2)}) collective-permute-start(f32[512,128]{1,0:T(8,128)S(1)} %get-tuple-element.57), channel_id=1, source_target_pairs={{0,2},{1,3},{2,0},{3,1},{4,6},{5,7},{6,4},{7,5},{8,10},{9,11},{10,... | collective-permute-start | bytes 786440 | tf_op jit(solution)/shard_map/ppermute | solution.py:352
  36.5 6.8 %collective-permute-done.6.refs_1_ = f32[560,128]{1,0:T(8,128)S(1)} collective-permute-done((f32[560,128]{1,0:T(8,128)S(1)}, f32[560,128]{1,0:T(8,128)S(1)}, u32[]{:S(2)}, u32[]{:S(2)}) %collective-permute-start.6) | collective-permute-done | bytes 286752 | tf_op jit(solution)/shard_map/ppermute | solution.py:352
  43.3 0.0 collective-permute-start.13
  43.3 0.0 collective-permute-done.7.refs_2_
  43.3 0.0 collective-permute-done.8.refs_3_
  43.4 4.4 %friction_lower.1 = (f32[512,128]{1,0:T(8,128)S(1)}, f32[512,128]{1,0:T(8,128)S(1)}, f32[512,128]{1,0:T(8,128)S(1)}, f32[512,128]{1,0:T(8,128)S(1)}, f32[24,256]{1,0:T(8,128)S(1)}) custom-call(bf16[128,96]{1,0:T(8,128)(2,1)S(1)} %get-tuple-element.35.forward_ref, bf16[64,256]{1,0:T(8,128)(2,1)S(1)} %get-tuple-element.36.backward_ref, ...), custom_call_target="tpu_custom_call" | custom-call | bytes 12000000 | tf_op jit(solution)/shard_map/friction_lower/pallas_call | solution.py:430
  47.8 3.3 %collective-permute-start.14 = (f32[512,128]{1,0:T(8,128)S(1)}, f32[512,128]{1,0:T(8,128)S(1)}, u32[]{:S(2)}, u32[]{:S(2)}) collective-permute-start(f32[512,128]{1,0:T(8,128)S(1)} %get-tuple-element.62), channel_id=1, source_target_pairs={{0,3},{1,0},{2,1},{3,2},{4,7},{5,4},{6,5},{7,6},{8,11},{9,8},{10,9... | collective-permute-start | bytes 786440 | tf_op jit(solution)/shard_map/ppermute | solution.py:352
  51.1 0.0 collective-permute-start.15
  51.1 0.0 collective-permute-done.11.refs_1_
  51.1 1.1 %collective-permute-start.16 = (f32[512,128]{1,0:T(8,128)S(1)}, f32[512,128]{1,0:T(8,128)S(1)}, u32[]{:S(2)}, u32[]{:S(2)}) collective-permute-start(f32[512,128]{1,0:T(8,128)S(1)} %get-tuple-element.64), channel_id=1, source_target_pairs={{0,1},{1,2},{2,3},{3,0},{4,5},{5,6},{6,7},{7,4},{8,9},{9,10},{10,1... | collective-permute-start | bytes 786440 | tf_op jit(solution)/shard_map/ppermute | solution.py:352
  52.2 0.0 copy-done.2
  52.2 0.0 copy-done.3
  52.3 0.0 collective-permute-done.12.refs_2_
  52.3 1.9 %collective-permute-start.9 = (f32[4,256]{1,0:T(4,128)S(1)}, f32[4,256]{1,0:T(4,128)S(1)}, u32[]{:S(2)}, u32[]{:S(2)}) collective-permute-start(f32[4,256]{1,0:T(4,128)S(1)} %get-tuple-element.51), channel_id=1, source_target_pairs={{0,4},{4,8},{8,12},{12,16},{16,20},{20,24},{24,28},{28,32},{32,36}... | collective-permute-start | bytes 12296 | tf_op jit(solution)/shard_map/ppermute | solution.py:452
  54.2 0.1 collective-permute-done.13.refs_3_
  54.3 5.9 %collective-permute-start.10 = (f32[4,256]{1,0:T(4,128)S(1)}, f32[4,256]{1,0:T(4,128)S(1)}, u32[]{:S(2)}, u32[]{:S(2)}) collective-permute-start(f32[4,256]{1,0:T(4,128)S(1)} %get-tuple-element.52), channel_id=1, source_target_pairs={{4,0},{8,4},{12,8},{16,12},{20,16},{24,20},{28,24},{32,28},{36,32}... | collective-permute-start | bytes 12296 | tf_op jit(solution)/shard_map/ppermute | solution.py:451
  60.3 1.8 %finish_upper.1 = (f32[1,3,4,256,256]{4,3,2,1,0:T(8,128)}, f32[2,4,32,256]{3,2,1,0:T(8,128)S(1)}) custom-call(f32[24,256]{1,0:T(8,128)S(1)} %get-tuple-element.50.extra_ref, f32[1,256,256]{2,1,0:T(8,128)S(1)} %copy-done.2, s32[1,256,256]{2,1,0:T(8,128)S(1)} %copy-done.3, f32[4,256,256]{2,1,0:T(8,128)S(1)} %get-tuple-element.53.east_ref, ...), custom_call_target="tpu_custom_call" | custom-call | bytes 9000000 | tf_op jit(solution)/shard_map/finish_upper/pallas_call | solution.py:455
  62.1 0.0 collective-permute-done.9.before_ref
  62.1 0.0 collective-permute-done.10.after_ref
  62.1 0.0 collective-permute-done.14.refs_1_
  62.1 0.0 collective-permute-done.15.refs_2_
  62.1 0.1 collective-permute-done.16.refs_3_
  62.2 2.0 %finish_lower.1 = f32[1,3,4,256,256]{4,3,2,1,0:T(8,128)} custom-call(f32[24,256]{1,0:T(8,128)S(1)} %get-tuple-element.50.extra_ref, f32[4,256]{1,0:T(4,128)S(1)} %collective-permute-done.9.before_ref, f32[4,256]{1,0:T(4,128)S(1)} %collective-permute-done.10.after_ref, f32[1,256,256]{2,1,0:T(8,128)S(1)} %copy-done.2, ...), custom_call_target="tpu_custom_call", output_to_operand_aliasing={{}: (9, {})} | custom-call | bytes 9000000 | tf_op jit(solution)/shard_map/finish_lower/pallas_call | solution.py:469
  (1 shorter events, 0.0 us)
Async XLA Ops:
  0.0 1.9 %copy-start = (f32[1,3,4,256,256]{4,3,2,1,0:T(8,128)S(1)}, f32[1,3,4,256,256]{4,3,2,1,0:T(8,128)}, u32[]{:S(2)}) copy-start(f32[1,3,4,256,256]{4,3,2,1,0:T(8,128)} %state_ref.5) | copy-start | bytes 9437188
  1.9 5.9 %copy-start.1 = (f32[1,3,4,256,256]{4,3,2,1,0:T(8,128)S(1)}, f32[1,3,4,256,256]{4,3,2,1,0:T(8,128)}, u32[]{:S(2)}) copy-start(f32[1,3,4,256,256]{4,3,2,1,0:T(8,128)} %state_ref.5) | copy-start | bytes 9437188
  1.9 5.9 %copy-start.5 = (s32[16]{0:T(128)S(1)}, s32[16]{0:T(128)}, u32[]{:S(2)}) copy-start(s32[16]{0:T(128)} %freq_ref.3) | copy-start | bytes 196
  1.9 5.9 %copy-start.6 = (s32[256]{0:T(256)S(1)}, s32[256]{0:T(256)}, u32[]{:S(2)}) copy-start(s32[256]{0:T(256)} %param.10) | copy-start | bytes 3076
  2.1 22.4 %collective-permute-start.3 = (f32[512,128]{1,0:T(8,128)S(1)}, f32[512,128]{1,0:T(8,128)S(1)}, u32[]{:S(2)}, u32[]{:S(2)}) collective-permute-start(f32[512,128]{1,0:T(8,128)S(1)} %get-tuple-element.42), channel_id=1, source_target_pairs={{0,1},{1,2},{2,3},{3,0},{4,5},{5,6},{6,7},{7,4},{8,9},{9,10},{10,1... | collective-permute-start | bytes 786440 | tf_op jit(solution)/shard_map/ppermute | solution.py:352
  3.6 26.9 %collective-permute-start.4 = (f32[512,128]{1,0:T(8,128)S(1)}, f32[512,128]{1,0:T(8,128)S(1)}, u32[]{:S(2)}, u32[]{:S(2)}) collective-permute-start(f32[512,128]{1,0:T(8,128)S(1)} %get-tuple-element.43), channel_id=1, source_target_pairs={{0,2},{1,3},{2,0},{3,1},{4,6},{5,7},{6,4},{7,5},{8,10},{9,11},{10,... | collective-permute-start | bytes 786440 | tf_op jit(solution)/shard_map/ppermute | solution.py:352
  6.4 24.2 %collective-permute-start.5 = (f32[512,128]{1,0:T(8,128)S(1)}, f32[512,128]{1,0:T(8,128)S(1)}, u32[]{:S(2)}, u32[]{:S(2)}) collective-permute-start(f32[512,128]{1,0:T(8,128)S(1)} %get-tuple-element.44), channel_id=1, source_target_pairs={{0,3},{1,0},{2,1},{3,2},{4,7},{5,4},{6,5},{7,6},{8,11},{9,8},{10,9... | collective-permute-start | bytes 786440 | tf_op jit(solution)/shard_map/ppermute | solution.py:352
  7.8 19.4 %copy-start.4 = (f32[1,2,4,256,256]{4,3,2,1,0:T(8,128)S(1)}, f32[1,2,4,256,256]{4,3,2,1,0:T(8,128)}, u32[]{:S(2)}) copy-start(f32[1,2,4,256,256]{4,3,2,1,0:T(8,128)} %forcing_ref.1) | copy-start | bytes 6291460
  10.4 2.1 %collective-permute-start = (f32[12,256]{1,0:T(8,128)S(1)}, f32[12,256]{1,0:T(8,128)S(1)}, u32[]{:S(2)}, u32[]{:S(2)}) collective-permute-start(f32[12,256]{1,0:T(8,128)S(1)} %get-tuple-element.37), channel_id=1, source_target_pairs={{0,128},{1,129},{2,130},{3,131},{4,132},{5,133},{6,134},{7,135},{8... | collective-permute-start | bytes 36872 | tf_op jit(solution)/shard_map/ppermute | solution.py:385
  12.8 9.9 %collective-permute-start.1 = (f32[4,256]{1,0:T(4,128)S(1)}, f32[4,256]{1,0:T(4,128)S(1)}, u32[]{:S(2)}, u32[]{:S(2)}) collective-permute-start(f32[4,256]{1,0:T(4,128)S(1)} %get-tuple-element.38), channel_id=1, source_target_pairs={{0,4},{4,8},{8,12},{12,16},{16,20},{20,24},{24,28},{28,32},{32,36}... | collective-permute-start | bytes 12296 | tf_op jit(solution)/shard_map/ppermute | solution.py:407
  16.6 7.4 %collective-permute-start.2 = (f32[4,256]{1,0:T(4,128)S(1)}, f32[4,256]{1,0:T(4,128)S(1)}, u32[]{:S(2)}, u32[]{:S(2)}) collective-permute-start(f32[4,256]{1,0:T(4,128)S(1)} %get-tuple-element.39), channel_id=1, source_target_pairs={{4,0},{8,4},{12,8},{16,12},{20,16},{24,20},{28,24},{32,28},{36,32}... | collective-permute-start | bytes 12296 | tf_op jit(solution)/shard_map/ppermute | solution.py:406
  22.7 20.7 %collective-permute-start.6 = (f32[560,128]{1,0:T(8,128)S(1)}, f32[560,128]{1,0:T(8,128)S(1)}, u32[]{:S(2)}, u32[]{:S(2)}) collective-permute-start(f32[560,128]{1,0:T(8,128)S(1)} %get-tuple-element.47), channel_id=1, source_target_pairs={{0,1},{1,2},{2,3},{3,0},{4,5},{5,6},{6,7},{7,4},{8,9},{9,10},{10,1... | collective-permute-start | bytes 860168 | tf_op jit(solution)/shard_map/ppermute | solution.py:352
  24.0 19.4 %collective-permute-start.7 = (f32[560,128]{1,0:T(8,128)S(1)}, f32[560,128]{1,0:T(8,128)S(1)}, u32[]{:S(2)}, u32[]{:S(2)}) collective-permute-start(f32[560,128]{1,0:T(8,128)S(1)} %get-tuple-element.48), channel_id=1, source_target_pairs={{0,2},{1,3},{2,0},{3,1},{4,6},{5,7},{6,4},{7,5},{8,10},{9,11},{10,... | collective-permute-start | bytes 860168 | tf_op jit(solution)/shard_map/ppermute | solution.py:352
  24.5 27.8 %copy-start.2 = (f32[1,256,256]{2,1,0:T(8,128)S(1)}, f32[1,256,256]{2,1,0:T(8,128)}, u32[]{:S(2)}) copy-start(f32[1,256,256]{2,1,0:T(8,128)} %depth_ref.5) | copy-start | bytes 786436
  24.5 27.8 %copy-start.3 = (s32[1,256,256]{2,1,0:T(8,128)S(1)}, s32[1,256,256]{2,1,0:T(8,128)}, u32[]{:S(2)}) copy-start(s32[1,256,256]{2,1,0:T(8,128)} %wet_ref.5) | copy-start | bytes 786436
  24.5 18.9 %collective-permute-start.8 = (f32[560,128]{1,0:T(8,128)S(1)}, f32[560,128]{1,0:T(8,128)S(1)}, u32[]{:S(2)}, u32[]{:S(2)}) collective-permute-start(f32[560,128]{1,0:T(8,128)S(1)} %get-tuple-element.49), channel_id=1, source_target_pairs={{0,3},{1,0},{2,1},{3,2},{4,7},{5,4},{6,5},{7,6},{8,11},{9,8},{10,9... | collective-permute-start | bytes 860168 | tf_op jit(solution)/shard_map/ppermute | solution.py:352
  34.7 16.4 %collective-permute-start.11 = (f32[512,128]{1,0:T(8,128)S(1)}, f32[512,128]{1,0:T(8,128)S(1)}, u32[]{:S(2)}, u32[]{:S(2)}) collective-permute-start(f32[512,128]{1,0:T(8,128)S(1)} %get-tuple-element.56), channel_id=1, source_target_pairs={{0,3},{1,0},{2,1},{3,2},{4,7},{5,4},{6,5},{7,6},{8,11},{9,8},{10,9... | collective-permute-start | bytes 786440 | tf_op jit(solution)/shard_map/ppermute | solution.py:352
  35.6 16.7 %collective-permute-start.12 = (f32[512,128]{1,0:T(8,128)S(1)}, f32[512,128]{1,0:T(8,128)S(1)}, u32[]{:S(2)}, u32[]{:S(2)}) collective-permute-start(f32[512,128]{1,0:T(8,128)S(1)} %get-tuple-element.57), channel_id=1, source_target_pairs={{0,2},{1,3},{2,0},{3,1},{4,6},{5,7},{6,4},{7,5},{8,10},{9,11},{10,... | collective-permute-start | bytes 786440 | tf_op jit(solution)/shard_map/ppermute | solution.py:352
  43.3 11.0 %collective-permute-start.13 = (f32[512,128]{1,0:T(8,128)S(1)}, f32[512,128]{1,0:T(8,128)S(1)}, u32[]{:S(2)}, u32[]{:S(2)}) collective-permute-start(f32[512,128]{1,0:T(8,128)S(1)} %get-tuple-element.58), channel_id=1, source_target_pairs={{0,1},{1,2},{2,3},{3,0},{4,5},{5,6},{6,7},{7,4},{8,9},{9,10},{10,1... | collective-permute-start | bytes 786440 | tf_op jit(solution)/shard_map/ppermute | solution.py:352
  47.8 14.3 %collective-permute-start.14 = (f32[512,128]{1,0:T(8,128)S(1)}, f32[512,128]{1,0:T(8,128)S(1)}, u32[]{:S(2)}, u32[]{:S(2)}) collective-permute-start(f32[512,128]{1,0:T(8,128)S(1)} %get-tuple-element.62), channel_id=1, source_target_pairs={{0,3},{1,0},{2,1},{3,2},{4,7},{5,4},{6,5},{7,6},{8,11},{9,8},{10,9... | collective-permute-start | bytes 786440 | tf_op jit(solution)/shard_map/ppermute | solution.py:352
  51.1 11.0 %collective-permute-start.15 = (f32[512,128]{1,0:T(8,128)S(1)}, f32[512,128]{1,0:T(8,128)S(1)}, u32[]{:S(2)}, u32[]{:S(2)}) collective-permute-start(f32[512,128]{1,0:T(8,128)S(1)} %get-tuple-element.63), channel_id=1, source_target_pairs={{0,2},{1,3},{2,0},{3,1},{4,6},{5,7},{6,4},{7,5},{8,10},{9,11},{10,... | collective-permute-start | bytes 786440 | tf_op jit(solution)/shard_map/ppermute | solution.py:352
  51.1 11.1 %collective-permute-start.16 = (f32[512,128]{1,0:T(8,128)S(1)}, f32[512,128]{1,0:T(8,128)S(1)}, u32[]{:S(2)}, u32[]{:S(2)}) collective-permute-start(f32[512,128]{1,0:T(8,128)S(1)} %get-tuple-element.64), channel_id=1, source_target_pairs={{0,1},{1,2},{2,3},{3,0},{4,5},{5,6},{6,7},{7,4},{8,9},{9,10},{10,1... | collective-permute-start | bytes 786440 | tf_op jit(solution)/shard_map/ppermute | solution.py:352
  52.3 9.8 %collective-permute-start.9 = (f32[4,256]{1,0:T(4,128)S(1)}, f32[4,256]{1,0:T(4,128)S(1)}, u32[]{:S(2)}, u32[]{:S(2)}) collective-permute-start(f32[4,256]{1,0:T(4,128)S(1)} %get-tuple-element.51), channel_id=1, source_target_pairs={{0,4},{4,8},{8,12},{12,16},{16,20},{20,24},{24,28},{28,32},{32,36}... | collective-permute-start | bytes 12296 | tf_op jit(solution)/shard_map/ppermute | solution.py:452
  54.3 7.8 %collective-permute-start.10 = (f32[4,256]{1,0:T(4,128)S(1)}, f32[4,256]{1,0:T(4,128)S(1)}, u32[]{:S(2)}, u32[]{:S(2)}) collective-permute-start(f32[4,256]{1,0:T(4,128)S(1)} %get-tuple-element.52), channel_id=1, source_target_pairs={{4,0},{8,4},{12,8},{16,12},{20,16},{24,20},{28,24},{32,28},{36,32}... | collective-permute-start | bytes 12296 | tf_op jit(solution)/shard_map/ppermute | solution.py:451

commit v3 on v2

--- a/solution.py
+++ b/solution.py
@@ -93,9 +93,9 @@
     backward_ref[...] = jnp.where(row < 32, high, low).astype(BF16)
 
 
-def piece(state_ref, out_ref, sem, row, size, j):
+def piece(state_ref, field, out_ref, sem, row, size, j):
     return pltpu.make_async_copy(
-        state_ref.at[0, pl.ds(1, 2), :, pl.ds(row, size), pl.ds(j * LANES, LANES)],
+        state_ref.at[0, pl.ds(field, 2), :, pl.ds(row, size), pl.ds(j * LANES, LANES)],
         out_ref.reshape(2, 4, size, LANES),
         sem,
     )
@@ -109,7 +109,7 @@
         row = pl.multiple_of(((me + slot) & (RING - 1)) * UPPER, UPPER)
         for j in range(2):
             out_ref = outs[slot].at[pl.ds(8 * UPPER * j, 8 * UPPER), :]
-            copies.append(piece(state_ref, out_ref, sems.at[slot, j], row, UPPER, j))
+            copies.append(piece(state_ref, 0, out_ref, sems.at[slot, j], row, UPPER, j))
     for copy in copies:
         copy.start()
     for copy in copies:
@@ -129,7 +129,7 @@
         row = pl.multiple_of(ROWS_UP + ((me + slot) & (RING - 1)) * LOWER, 8)
         for j in range(2):
             out_ref = outs[slot].at[pl.ds(8 * LOWER * j, 8 * LOWER), :]
-            copies.append(piece(state_ref, out_ref, sems.at[slot, j], row, LOWER, j))
+            copies.append(piece(state_ref, 1, out_ref, sems.at[slot, j], row, LOWER, j))
     for copy in copies:
         copy.start()
     for copy in copies[:2]:
@@ -175,8 +175,10 @@
     lax.fori_loop(0, size, step, 0, unroll=4)
 
 
-def friction_upper(forward_ref, backward_ref, behind_ref, *refs):
-    rows_terms(UPPER, forward_ref[...], backward_ref[...], refs[:RING], refs[RING:])
+def friction_upper(forward_ref, backward_ref, first_ref, last_ref, *refs):
+    rows_terms(UPPER, forward_ref[...], backward_ref[...], refs[:RING], refs[RING : 2 * RING])
+    refs[2 * RING][...] = first_ref[...]
+    refs[2 * RING + 1][...] = last_ref[...]
 
 
 def friction_lower(forward_ref, backward_ref, behind_ref, *refs):
@@ -204,7 +206,7 @@
     return down - up
 
 
-def known(freq_ref, strip_ref, before_ref, after_ref, state_ref, forcing_ref, east_ref, north_ref, eta_ref, edge_ref):
+def known(freq_ref, behind_ref, strip_ref, state_ref, forcing_ref, east_ref, north_ref, eta_ref, edge_ref):
     me = lax.axis_index("harm")
     shelf = lax.axis_index("sec") == 1
     take = jnp.logical_and(iota((CELLS, CELLS), 1) == 0, shelf)
@@ -231,7 +233,7 @@
         for p in range(2):
             ch = 2 * i + p
             turn = -omega if p else omega
-            slope = up_down(eta[p], before_ref[ch : ch + 1, :], after_ref[ch : ch + 1, :])
+            slope = up_down(eta[p], 0.0, 0.0)
             rest = turn * north[1 - p] + 0.5 * slope - forcing_ref[0, 1, ch]
             value = north[p] - relax_step * rest
             north_ref[ch] = value
@@ -239,13 +241,18 @@
             edge_ref[4 + ch : 5 + ch, :] = value[CELLS - 1 : CELLS, :]
 
 
-def edge_flux(edge_ref, extra_ref, depth_ref, wet_ref, first_ref, last_ref):
-    for out_ref, at, row in ((first_ref, 0, 0), (last_ref, 1, CELLS - 1)):
+def edge_flux(edge_ref, before_ref, after_ref, extra_ref, depth_ref, wet_ref, first_ref, last_ref, north_ref):
+    half = 0.5 * relax_step
+    for out_ref, at, row, beside in (
+        (first_ref, 0, 0, half * before_ref[...]),
+        (last_ref, 1, CELLS - 1, -half * after_ref[...]),
+    ):
         height = depth_ref[0, row : row + 1, :]
         wet = wet_ref[0, row : row + 1, :].astype(F32)
         drag = extra_ref[8 + 8 * at + 4 : 8 + 8 * at + 8, :]
-        north = wet * (edge_ref[4 * at : 4 * at + 4, :] - (relax_step / height) * drag)
+        north = wet * (edge_ref[4 * at : 4 * at + 4, :] + beside - (relax_step / height) * drag)
         out_ref[...] = height * north
+        north_ref[4 * at : 4 * at + 4, :] = north
 
 
 def transports(start, size, turned, extra_ref, depth_ref, wet_ref, sources, drags, store):
@@ -299,7 +306,7 @@
 
 
 def finish_lower(
-    extra_ref, before_ref, after_ref, depth_ref, wet_ref, east_ref, north_ref, eta_ref, carry_ref, begun_ref, *refs
+    extra_ref, edge_ref, before_ref, after_ref, depth_ref, wet_ref, east_ref, north_ref, eta_ref, carry_ref, begun_ref, *refs
 ):
     slots, (out_ref, made, level, top, turned, sems, level_sems) = refs[:RING], refs[RING:]
     top_row = ROWS_UP - REACH
@@ -311,6 +318,8 @@
         made[f - 1, ch, pl.ds(REACH + row, LOWER), :] = value
 
     transports(ROWS_UP, LOWER, turned, extra_ref, depth_ref, wet_ref, (east_ref, north_ref), slots, store)
+    for ch in range(4):
+        made[1, ch, REACH + ROWS_LOW - 1 : REACH + ROWS_LOW, :] = edge_ref[4 + ch : 5 + ch, :]
     copies = []
 
     def send(source, target, sem):
@@ -327,12 +336,15 @@
     height = depth_ref[0, :REACH, :]
     wet = wet_ref[0, :REACH, :].astype(F32)
     for ch in range(4):
+        north = carry_ref[1, ch, :REACH, :]
+        north = jnp.where(iota((REACH, CELLS), 0) == 0, edge_ref[ch : ch + 1, :], north)
         value = new_eta(
-            carry_ref[0, ch, :REACH, :], carry_ref[1, ch, :REACH, :], before_ref[ch : ch + 1, :], 0.0,
-            height, wet, eta_ref[ch, :REACH, :],
+            carry_ref[0, ch, :REACH, :], north, before_ref[ch : ch + 1, :], 0.0, height, wet, eta_ref[ch, :REACH, :]
         )
-        top[ch] = value[:8]
-    send(top, out_ref.at[0, 0, :, pl.ds(0, 8), :], sems.at[2])
+        top[0, ch] = value[:8]
+        top[1, ch] = north[:8]
+    for i in range(2):
+        send(top.at[i], out_ref.at[0, 2 * i, :, pl.ds(0, 8), :], sems.at[2 + i])
     height = depth_ref[0, top_row:, :]
     wet = wet_ref[0, top_row:, :].astype(F32)
     for ch in range(4):
@@ -370,7 +382,7 @@
         scratch_shapes=[pltpu.SemaphoreType.DMA((RING, 2))],
         compiler_params=params(),
         cost_estimate=cost(2),
-    )(state)
+    )(lax.slice(state, (0, 1, 0, 0, 0), (1, 3, 4, ROWS_UP, CELLS)))
     raw = [parts[0]] + [around(parts[slot], slot) for slot in (1, 2, 3)]
 
     strip, forward, backward = pl.pallas_call(
@@ -403,30 +415,29 @@
     raw_lower = [packed[0]] + [around(packed[slot], slot) for slot in (1, 2, 3)]
     to_next = [(i, i + 1) for i in range(tiles - 1)]
     to_last = [(i + 1, i) for i in range(tiles - 1)]
-    after = lax.ppermute(first, "tile", to_last)
-    before = lax.ppermute(last, "tile", to_next)
-
+    made = pl.pallas_call(
+        friction_upper,
+        name="friction_upper",
+        in_specs=vmem(4 + RING),
+        out_specs=vmem(RING + 2),
+        out_shape=(upper,) * RING + (edge_eta, edge_eta),
+        compiler_params=params(),
+        cost_estimate=cost(4),
+    )(forward, backward, first, last, *raw)
+    after = lax.ppermute(made[RING], "tile", to_last)
+    before = lax.ppermute(made[RING + 1], "tile", to_next)
+    drags = [made[0]] + [around(made[slot], -slot) for slot in (1, 2, 3)]
     plane = array((4, CELLS, CELLS), F32)
     east, north, eta, edge = pl.pallas_call(
         known,
         name="known",
-        in_specs=[smem] + vmem(5),
+        in_specs=[smem, hbm] + vmem(3),
         out_specs=vmem(4),
         out_shape=(plane, plane, plane, array((8, CELLS), F32)),
         compiler_params=params(),
         cost_estimate=cost(5),
-    )(freq_order, strip, before, after, state, forcing)
-
-    made = pl.pallas_call(
-        friction_upper,
-        name="friction_upper",
-        in_specs=vmem(2) + [hbm] + vmem(RING),
-        out_specs=vmem(RING),
-        out_shape=(upper,) * RING,
-        compiler_params=params(),
-        cost_estimate=cost(4),
-    )(forward, backward, edge, *raw)
-    drags = [made[0]] + [around(made[slot], -slot) for slot in (1, 2, 3)]
+    )(freq_order, made[0], strip, state, forcing)
+
     made = pl.pallas_call(
         friction_lower,
         name="friction_lower",
@@ -435,19 +446,19 @@
         out_shape=(array((16 * LOWER, LANES), F32),) * RING + (array((24, CELLS), F32),),
         compiler_params=params(),
         cost_estimate=cost(4),
-    )(forward, backward, made[0], *raw_lower)
+    )(forward, backward, edge, *raw_lower)
     extra = made[RING]
     drags_lower = [made[0]] + [around(made[slot], -slot) for slot in (1, 2, 3)]
 
-    first, last = pl.pallas_call(
+    first, last, edge = pl.pallas_call(
         edge_flux,
         name="edge_flux",
-        in_specs=vmem(4),
-        out_specs=vmem(2),
-        out_shape=(edge_eta, edge_eta),
+        in_specs=vmem(6),
+        out_specs=vmem(3),
+        out_shape=(edge_eta, edge_eta, array((8, CELLS), F32)),
         compiler_params=params(),
         cost_estimate=cost(1),
-    )(edge, extra, depth, wet_mask)
+    )(edge, before, after, extra, depth, wet_mask)
     after_flux = lax.ppermute(first, "tile", to_last)
     before_flux = lax.ppermute(last, "tile", to_next)
 
@@ -469,21 +480,21 @@
     return pl.pallas_call(
         finish_lower,
         name="finish_lower",
-        in_specs=vmem(9) + [hbm] + vmem(RING),
+        in_specs=vmem(10) + [hbm] + vmem(RING),
         out_specs=hbm,
         out_shape=whole,
-        input_output_aliases={9: 0},
+        input_output_aliases={10: 0},
         scratch_shapes=[
             pltpu.VMEM((2, 4, REACH + ROWS_LOW, CELLS), F32),
             pltpu.VMEM((4, REACH + ROWS_LOW, CELLS), F32),
-            pltpu.VMEM((4, 8, CELLS), F32),
+            pltpu.VMEM((2, 4, 8, CELLS), F32),
             pltpu.VMEM((CELLS, 8), F32),
-            pltpu.SemaphoreType.DMA((3,)),
+            pltpu.SemaphoreType.DMA((4,)),
             pltpu.SemaphoreType.DMA((4,)),
         ],
         compiler_params=params(),
         cost_estimate=cost(3),
-    )(extra, before_flux, after_flux, depth, wet_mask, east, north, eta, carry, begun, *drags_lower)
+    )(extra, edge, before_flux, after_flux, depth, wet_mask, east, north, eta, carry, begun, *drags_lower)
 
 
 def solution(mesh):

time: 65.4 us -> 62.4 us (0.954); the launches traced: 64.3 us -> 62.2 us
  waiting for transfers between devices: 8.43 us -> 5.27 us
  starting transfers between devices: 35 us -> 36.4 us
    ppermute x12, waiting for transfers between devices: 6.98 us -> 4.44 us  [around(): lax.ppermute(value, 'harm', [(i, (i + steps) % RING) for i in range(RING)])]
    unnamed x14 -> x12, local copies, waits for them, and re-layouts: 1.91 us -> 0.02 us
    slice x0 -> x1, local copies, waits for them, and re-layouts: none -> 1.45 us  [body(): lax.slice(state, (0, 1, 0, 0, 0), (1, 3, 4, ROWS_UP, CELLS))]
    ppermute x12, starting transfers between devices: 16 us -> 17.3 us  [around(): lax.ppermute(value, 'harm', [(i, (i + steps) % RING) for i in range(RING)])]
  transfers between devices with their start and end apart: 17 -> 17, of which waited for: 5 -> 3; matrix products, arithmetic and copies ran while one was open for 0% -> 0% of each run, Pallas kernels for 26% -> 27%
where the time goes in v3:
time: 62.4 us; the launch traced here: 62.2 us
  starting transfers between devices  36.4 us (58%)
  Pallas kernels  18.7 us (30%)
  waiting for transfers between devices  5.27 us (8%)
  local copies, waits for them, and re-layouts  1.47 us (2%)
    ppermute x12, starting transfers between devices, around(): lax.ppermute(value, 'harm', [(i, (i + steps) % RING) for i in range(RING)])  17.3 us
    ppermute x1, starting transfers between devices, body(): after = lax.ppermute(made[RING], 'tile', to_last)  6.04 us
    ppermute x1, starting transfers between devices, body(): after_flux = lax.ppermute(first, 'tile', to_last)  6.03 us
    ppermute x12, waiting for transfers between devices, around(): lax.ppermute(value, 'harm', [(i, (i + steps) % RING) for i in range(RING)])  4.44 us
    pallas_call x1, Pallas kernels, body(): pl.pallas_call(friction_lower, name='friction_lower', in_specs=vmem(2) +...  4.43 us
    pallas_call x1, Pallas kernels, body(): pl.pallas_call(friction_upper, name='friction_upper', in_specs=vmem(4 + R...  4.09 us
    ppermute x1, starting transfers between devices, body(): before = lax.ppermute(made[RING + 1], 'tile', to_next)  3.81 us
    pallas_call x1, Pallas kernels, body(): pl.pallas_call(known, name='known', in_specs=[smem, hbm] + vmem(3), out_s...  3.36 us
  transfers between devices with their start and end apart: 17, of which 3 were waited for; matrix products, arithmetic and copies ran while one was open for 0% of the time, Pallas kernels for 27%

profile of v3, /device:TPU:24, one launch (start us, length us, event | category | flops | bytes accessed | tf_op | source)
XLA Modules:
  0.0 62.2 jit_solution(14941517759873286960)
XLA Ops:
  0.0 0.0 copy-start
  0.0 0.0 copy-start.4
  0.0 0.0 copy-start.5
  0.0 1.4 %slice.3.state_ref = f32[1,2,4,128,256]{4,3,2,1,0:T(8,128)S(1)} slice(f32[1,3,4,256,256]{4,3,2,1,0:T(8,128)} %state_ref.3), slice={[0:1], [1:3], [0:4], [0:128], [0:256]} | slice | bytes 2097152 | tf_op jit(solution)/shard_map/slice | solution.py:385
  1.5 0.2 pack_upper.1
  1.7 1.6 %collective-permute-start.1 = (f32[512,128]{1,0:T(8,128)S(1)}, f32[512,128]{1,0:T(8,128)S(1)}, u32[]{:S(2)}, u32[]{:S(2)}) collective-permute-start(f32[512,128]{1,0:T(8,128)S(1)} %get-tuple-element.44), channel_id=1, source_target_pairs={{0,1},{1,2},{2,3},{3,0},{4,5},{5,6},{6,7},{7,4},{8,9},{9,10},{10,1... | collective-permute-start | bytes 786440 | tf_op jit(solution)/shard_map/ppermute | solution.py:364
  3.2 2.7 %collective-permute-start.2 = (f32[512,128]{1,0:T(8,128)S(1)}, f32[512,128]{1,0:T(8,128)S(1)}, u32[]{:S(2)}, u32[]{:S(2)}) collective-permute-start(f32[512,128]{1,0:T(8,128)S(1)} %get-tuple-element.45), channel_id=1, source_target_pairs={{0,2},{1,3},{2,0},{3,1},{4,6},{5,7},{6,4},{7,5},{8,10},{9,11},{10,... | collective-permute-start | bytes 786440 | tf_op jit(solution)/shard_map/ppermute | solution.py:364
  6.0 1.4 %collective-permute-start.3 = (f32[512,128]{1,0:T(8,128)S(1)}, f32[512,128]{1,0:T(8,128)S(1)}, u32[]{:S(2)}, u32[]{:S(2)}) collective-permute-start(f32[512,128]{1,0:T(8,128)S(1)} %get-tuple-element.46), channel_id=1, source_target_pairs={{0,3},{1,0},{2,1},{3,2},{4,7},{5,4},{6,5},{7,6},{8,11},{9,8},{10,9... | collective-permute-start | bytes 786440 | tf_op jit(solution)/shard_map/ppermute | solution.py:364
  7.4 0.0 copy-done
  7.4 0.0 copy-done.4
  7.4 0.0 copy-done.5
  7.4 0.0 copy-start.3
  7.4 2.5 %prepare.1 = (f32[12,256]{1,0:T(8,128)S(1)}, bf16[128,96]{1,0:T(8,128)(2,1)S(1)}, bf16[64,256]{1,0:T(8,128)(2,1)S(1)}) custom-call(s32[16]{0:T(128)S(1)} %copy-done.4, s32[1,256]{1,0:T(1,128)S(1)} %bitcast.3, f32[12,256,256]{2,1,0:T(8,128)S(1)} %bitcast.2), custom_call_target="tpu_custom_call" | custom-call | bytes 12000000 | tf_op jit(solution)/shard_map/prepare/pallas_call | solution.py:388
  9.9 1.3 %collective-permute-start = (f32[12,256]{1,0:T(8,128)S(1)}, f32[12,256]{1,0:T(8,128)S(1)}, u32[]{:S(2)}, u32[]{:S(2)}) collective-permute-start(f32[12,256]{1,0:T(8,128)S(1)} %get-tuple-element.40), channel_id=1, source_target_pairs={{0,128},{1,129},{2,130},{3,131},{4,132},{5,133},{6,134},{7,135},{8... | collective-permute-start | bytes 36872 | tf_op jit(solution)/shard_map/ppermute | solution.py:397
  11.2 0.8 %collective-permute-done.strip_ref = f32[12,256]{1,0:T(8,128)S(1)} collective-permute-done((f32[12,256]{1,0:T(8,128)S(1)}, f32[12,256]{1,0:T(8,128)S(1)}, u32[]{:S(2)}, u32[]{:S(2)}) %collective-permute-start) | collective-permute-done | bytes 12320 | tf_op jit(solution)/shard_map/ppermute | solution.py:397
  12.1 0.3 pack_lower.1
  12.4 0.7 %collective-permute-start.4 = (f32[560,128]{1,0:T(8,128)S(1)}, f32[560,128]{1,0:T(8,128)S(1)}, u32[]{:S(2)}, u32[]{:S(2)}) collective-permute-start(f32[560,128]{1,0:T(8,128)S(1)} %get-tuple-element.50), channel_id=1, source_target_pairs={{0,1},{1,2},{2,3},{3,0},{4,5},{5,6},{6,7},{7,4},{8,9},{9,10},{10,1... | collective-permute-start | bytes 860168 | tf_op jit(solution)/shard_map/ppermute | solution.py:364
  13.0 0.9 %collective-permute-start.5 = (f32[560,128]{1,0:T(8,128)S(1)}, f32[560,128]{1,0:T(8,128)S(1)}, u32[]{:S(2)}, u32[]{:S(2)}) collective-permute-start(f32[560,128]{1,0:T(8,128)S(1)} %get-tuple-element.51), channel_id=1, source_target_pairs={{0,2},{1,3},{2,0},{3,1},{4,6},{5,7},{6,4},{7,5},{8,10},{9,11},{10,... | collective-permute-start | bytes 860168 | tf_op jit(solution)/shard_map/ppermute | solution.py:364
  13.9 0.0 collective-permute-done.1.refs_1_
  13.9 1.9 %collective-permute-start.6 = (f32[560,128]{1,0:T(8,128)S(1)}, f32[560,128]{1,0:T(8,128)S(1)}, u32[]{:S(2)}, u32[]{:S(2)}) collective-permute-start(f32[560,128]{1,0:T(8,128)S(1)} %get-tuple-element.52), channel_id=1, source_target_pairs={{0,3},{1,0},{2,1},{3,2},{4,7},{5,4},{6,5},{7,6},{8,11},{9,8},{10,9... | collective-permute-start | bytes 860168 | tf_op jit(solution)/shard_map/ppermute | solution.py:364
  15.8 2.9 %collective-permute-done.2.refs_2_ = f32[512,128]{1,0:T(8,128)S(1)} collective-permute-done((f32[512,128]{1,0:T(8,128)S(1)}, f32[512,128]{1,0:T(8,128)S(1)}, u32[]{:S(2)}, u32[]{:S(2)}) %collective-permute-start.2) | collective-permute-done | bytes 262176 | tf_op jit(solution)/shard_map/ppermute | solution.py:364
  18.7 0.0 collective-permute-done.3.refs_3_
  18.7 4.1 %friction_upper.1 = (f32[512,128]{1,0:T(8,128)S(1)}, f32[512,128]{1,0:T(8,128)S(1)}, f32[512,128]{1,0:T(8,128)S(1)}, f32[512,128]{1,0:T(8,128)S(1)}, f32[4,256]{1,0:T(4,128)S(1)}, /*index=5*/f32[4,256]{1,0:T(4,128)S(1)}) custom-call(bf16[128,96]{1,0:T(8,128)(2,1)S(1)} %get-tuple-element.38.forward_ref, bf16[64,256]{1,0:T(8,128)(2,1)S(1)} %get-tuple-element.39.backward_ref, ...), custom_call_target="tpu_custom_call" | custom-call | bytes 12000000 | tf_op jit(solution)/shard_map/friction_upper/pallas_call | solution.py:418
  22.8 1.3 %collective-permute-start.11 = (f32[512,128]{1,0:T(8,128)S(1)}, f32[512,128]{1,0:T(8,128)S(1)}, u32[]{:S(2)}, u32[]{:S(2)}) collective-permute-start(f32[512,128]{1,0:T(8,128)S(1)} %get-tuple-element.62), channel_id=1, source_target_pairs={{0,3},{1,0},{2,1},{3,2},{4,7},{5,4},{6,5},{7,6},{8,11},{9,8},{10,9... | collective-permute-start | bytes 786440 | tf_op jit(solution)/shard_map/ppermute | solution.py:364
  24.1 3.8 %collective-permute-start.7 = (f32[4,256]{1,0:T(4,128)S(1)}, f32[4,256]{1,0:T(4,128)S(1)}, u32[]{:S(2)}, u32[]{:S(2)}) collective-permute-start(f32[4,256]{1,0:T(4,128)S(1)} %get-tuple-element.54), channel_id=1, source_target_pairs={{0,4},{4,8},{8,12},{12,16},{16,20},{20,24},{24,28},{28,32},{32,36}... | collective-permute-start | bytes 12296 | tf_op jit(solution)/shard_map/ppermute | solution.py:428
  28.0 0.0 collective-permute-done.4.refs_1_
  28.0 6.0 %collective-permute-start.8 = (f32[4,256]{1,0:T(4,128)S(1)}, f32[4,256]{1,0:T(4,128)S(1)}, u32[]{:S(2)}, u32[]{:S(2)}) collective-permute-start(f32[4,256]{1,0:T(4,128)S(1)} %get-tuple-element.55), channel_id=1, source_target_pairs={{4,0},{8,4},{12,8},{16,12},{20,16},{24,20},{28,24},{32,28},{36,32}... | collective-permute-start | bytes 12296 | tf_op jit(solution)/shard_map/ppermute | solution.py:427
  34.0 0.0 collective-permute-done.5.refs_2_
  34.0 2.4 %collective-permute-start.12 = (f32[512,128]{1,0:T(8,128)S(1)}, f32[512,128]{1,0:T(8,128)S(1)}, u32[]{:S(2)}, u32[]{:S(2)}) collective-permute-start(f32[512,128]{1,0:T(8,128)S(1)} %get-tuple-element.63), channel_id=1, source_target_pairs={{0,2},{1,3},{2,0},{3,1},{4,6},{5,7},{6,4},{7,5},{8,10},{9,11},{10,... | collective-permute-start | bytes 786440 | tf_op jit(solution)/shard_map/ppermute | solution.py:364
  36.4 0.0 collective-permute-done.6.refs_3_
  36.4 0.8 %collective-permute-start.13 = (f32[512,128]{1,0:T(8,128)S(1)}, f32[512,128]{1,0:T(8,128)S(1)}, u32[]{:S(2)}, u32[]{:S(2)}) collective-permute-start(f32[512,128]{1,0:T(8,128)S(1)} %get-tuple-element.64), channel_id=1, source_target_pairs={{0,1},{1,2},{2,3},{3,0},{4,5},{5,6},{6,7},{7,4},{8,9},{9,10},{10,1... | collective-permute-start | bytes 786440 | tf_op jit(solution)/shard_map/ppermute | solution.py:364
  37.2 0.0 copy-done.3
  37.3 0.0 copy-start.1
  37.3 0.0 copy-start.2
  37.3 3.4 %known.1 = (f32[4,256,256]{2,1,0:T(8,128)S(1)}, f32[4,256,256]{2,1,0:T(8,128)S(1)}, f32[4,256,256]{2,1,0:T(8,128)S(1)}, f32[8,256]{1,0:T(8,128)S(1)}) custom-call(s32[16]{0:T(128)S(1)} %copy-done.4, f32[512,128]{1,0:T(8,128)S(1)} %get-tuple-element.47.behind_ref.refs_0_, f32[12,256]{1,0:T(8,128)S(1)} %collective-permute-done.strip_ref, ...), custom_call_target="tpu_custom_call" | custom-call | bytes 15000000 | tf_op jit(solution)/shard_map/known/pallas_call | solution.py:431
  40.6 4.4 %friction_lower.1 = (f32[512,128]{1,0:T(8,128)S(1)}, f32[512,128]{1,0:T(8,128)S(1)}, f32[512,128]{1,0:T(8,128)S(1)}, f32[512,128]{1,0:T(8,128)S(1)}, f32[24,256]{1,0:T(8,128)S(1)}) custom-call(bf16[128,96]{1,0:T(8,128)(2,1)S(1)} %get-tuple-element.38.forward_ref, bf16[64,256]{1,0:T(8,128)(2,1)S(1)} %get-tuple-element.39.backward_ref, ...), custom_call_target="tpu_custom_call" | custom-call | bytes 12000000 | tf_op jit(solution)/shard_map/friction_lower/pallas_call | solution.py:441
  45.1 0.0 collective-permute-done.7.before_ref
  45.1 2.5 %collective-permute-start.14 = (f32[512,128]{1,0:T(8,128)S(1)}, f32[512,128]{1,0:T(8,128)S(1)}, u32[]{:S(2)}, u32[]{:S(2)}) collective-permute-start(f32[512,128]{1,0:T(8,128)S(1)} %get-tuple-element.68), channel_id=1, source_target_pairs={{0,3},{1,0},{2,1},{3,2},{4,7},{5,4},{6,5},{7,6},{8,11},{9,8},{10,9... | collective-permute-start | bytes 786440 | tf_op jit(solution)/shard_map/ppermute | solution.py:364
  47.6 0.0 collective-permute-done.8.after_ref
  47.6 0.0 collective-permute-start.15
  47.6 0.0 collective-permute-done.11.refs_1_
  47.6 1.1 %collective-permute-start.16 = (f32[512,128]{1,0:T(8,128)S(1)}, f32[512,128]{1,0:T(8,128)S(1)}, u32[]{:S(2)}, u32[]{:S(2)}) collective-permute-start(f32[512,128]{1,0:T(8,128)S(1)} %get-tuple-element.70), channel_id=1, source_target_pairs={{0,1},{1,2},{2,3},{3,0},{4,5},{5,6},{6,7},{7,4},{8,9},{9,10},{10,1... | collective-permute-start | bytes 786440 | tf_op jit(solution)/shard_map/ppermute | solution.py:364
  48.7 0.0 copy-done.1
  48.7 0.0 copy-done.2
  48.8 0.0 collective-permute-done.12.refs_2_
  48.8 1.9 %collective-permute-start.9 = (f32[4,256]{1,0:T(4,128)S(1)}, f32[4,256]{1,0:T(4,128)S(1)}, u32[]{:S(2)}, u32[]{:S(2)}) collective-permute-start(f32[4,256]{1,0:T(4,128)S(1)} %get-tuple-element.57), channel_id=1, source_target_pairs={{0,4},{4,8},{8,12},{12,16},{16,20},{20,24},{24,28},{28,32},{32,36}... | collective-permute-start | bytes 12296 | tf_op jit(solution)/shard_map/ppermute | solution.py:463
  50.7 0.0 collective-permute-done.13.refs_3_
  50.7 6.0 %collective-permute-start.10 = (f32[4,256]{1,0:T(4,128)S(1)}, f32[4,256]{1,0:T(4,128)S(1)}, u32[]{:S(2)}, u32[]{:S(2)}) collective-permute-start(f32[4,256]{1,0:T(4,128)S(1)} %get-tuple-element.58), channel_id=1, source_target_pairs={{4,0},{8,4},{12,8},{16,12},{20,16},{24,20},{28,24},{32,28},{36,32}... | collective-permute-start | bytes 12296 | tf_op jit(solution)/shard_map/ppermute | solution.py:462
  56.7 1.8 %finish_upper.1 = (f32[1,3,4,256,256]{4,3,2,1,0:T(8,128)}, f32[2,4,32,256]{3,2,1,0:T(8,128)S(1)}) custom-call(f32[24,256]{1,0:T(8,128)S(1)} %get-tuple-element.53.extra_ref, f32[1,256,256]{2,1,0:T(8,128)S(1)} %copy-done.1, s32[1,256,256]{2,1,0:T(8,128)S(1)} %copy-done.2, f32[4,256,256]{2,1,0:T(8,128)S(1)} %get-tuple-element.59.east_ref, ...), custom_call_target="tpu_custom_call" | custom-call | bytes 9000000 | tf_op jit(solution)/shard_map/finish_upper/pallas_call | solution.py:466
  58.6 0.0 collective-permute-done.9.before_ref
  58.6 0.0 collective-permute-done.10.after_ref
  58.6 0.0 collective-permute-done.14.refs_1_
  58.6 0.0 collective-permute-done.15.refs_2_
  58.6 1.5 %collective-permute-done.16.refs_3_ = f32[512,128]{1,0:T(8,128)S(1)} collective-permute-done((f32[512,128]{1,0:T(8,128)S(1)}, f32[512,128]{1,0:T(8,128)S(1)}, u32[]{:S(2)}, u32[]{:S(2)}) %collective-permute-start.16) | collective-permute-done | bytes 262176 | tf_op jit(solution)/shard_map/ppermute | solution.py:364
  60.1 2.0 %finish_lower.1 = f32[1,3,4,256,256]{4,3,2,1,0:T(8,128)} custom-call(f32[24,256]{1,0:T(8,128)S(1)} %get-tuple-element.53.extra_ref, f32[8,256]{1,0:T(8,128)S(1)} %get-tuple-element.56.edge_ref, f32[4,256]{1,0:T(4,128)S(1)} %collective-permute-done.9.before_ref, f32[4,256]{1,0:T(4,128)S(1)} %collective-permute-done.10.after_ref, ...), custom_call_target="tpu_custom_call", output_to_operand_aliasing={{}: (10, {})} | custom-call | bytes 9000000 | tf_op jit(solution)/shard_map/finish_lower/pallas_call | solution.py:480
  (1 shorter events, 0.0 us)
Async XLA Ops:
  0.0 7.4 %copy-start = (f32[1,3,4,256,256]{4,3,2,1,0:T(8,128)S(1)}, f32[1,3,4,256,256]{4,3,2,1,0:T(8,128)}, u32[]{:S(2)}) copy-start(f32[1,3,4,256,256]{4,3,2,1,0:T(8,128)} %state_ref.3) | copy-start | bytes 9437188
  0.0 7.4 %copy-start.4 = (s32[16]{0:T(128)S(1)}, s32[16]{0:T(128)}, u32[]{:S(2)}) copy-start(s32[16]{0:T(128)} %freq_ref.3) | copy-start | bytes 196
  0.0 7.4 %copy-start.5 = (s32[256]{0:T(256)S(1)}, s32[256]{0:T(256)}, u32[]{:S(2)}) copy-start(s32[256]{0:T(256)} %param.10) | copy-start | bytes 3076
  1.7 12.3 %collective-permute-start.1 = (f32[512,128]{1,0:T(8,128)S(1)}, f32[512,128]{1,0:T(8,128)S(1)}, u32[]{:S(2)}, u32[]{:S(2)}) collective-permute-start(f32[512,128]{1,0:T(8,128)S(1)} %get-tuple-element.44), channel_id=1, source_target_pairs={{0,1},{1,2},{2,3},{3,0},{4,5},{5,6},{6,7},{7,4},{8,9},{9,10},{10,1... | collective-permute-start | bytes 786440 | tf_op jit(solution)/shard_map/ppermute | solution.py:364
  3.2 15.5 %collective-permute-start.2 = (f32[512,128]{1,0:T(8,128)S(1)}, f32[512,128]{1,0:T(8,128)S(1)}, u32[]{:S(2)}, u32[]{:S(2)}) collective-permute-start(f32[512,128]{1,0:T(8,128)S(1)} %get-tuple-element.45), channel_id=1, source_target_pairs={{0,2},{1,3},{2,0},{3,1},{4,6},{5,7},{6,4},{7,5},{8,10},{9,11},{10,... | collective-permute-start | bytes 786440 | tf_op jit(solution)/shard_map/ppermute | solution.py:364
  6.0 12.8 %collective-permute-start.3 = (f32[512,128]{1,0:T(8,128)S(1)}, f32[512,128]{1,0:T(8,128)S(1)}, u32[]{:S(2)}, u32[]{:S(2)}) collective-permute-start(f32[512,128]{1,0:T(8,128)S(1)} %get-tuple-element.46), channel_id=1, source_target_pairs={{0,3},{1,0},{2,1},{3,2},{4,7},{5,4},{6,5},{7,6},{8,11},{9,8},{10,9... | collective-permute-start | bytes 786440 | tf_op jit(solution)/shard_map/ppermute | solution.py:364
  7.4 29.9 %copy-start.3 = (f32[1,2,4,256,256]{4,3,2,1,0:T(8,128)S(1)}, f32[1,2,4,256,256]{4,3,2,1,0:T(8,128)}, u32[]{:S(2)}) copy-start(f32[1,2,4,256,256]{4,3,2,1,0:T(8,128)} %forcing_ref.1) | copy-start | bytes 6291460
  9.9 2.1 %collective-permute-start = (f32[12,256]{1,0:T(8,128)S(1)}, f32[12,256]{1,0:T(8,128)S(1)}, u32[]{:S(2)}, u32[]{:S(2)}) collective-permute-start(f32[12,256]{1,0:T(8,128)S(1)} %get-tuple-element.40), channel_id=1, source_target_pairs={{0,128},{1,129},{2,130},{3,131},{4,132},{5,133},{6,134},{7,135},{8... | collective-permute-start | bytes 36872 | tf_op jit(solution)/shard_map/ppermute | solution.py:397
  12.4 15.6 %collective-permute-start.4 = (f32[560,128]{1,0:T(8,128)S(1)}, f32[560,128]{1,0:T(8,128)S(1)}, u32[]{:S(2)}, u32[]{:S(2)}) collective-permute-start(f32[560,128]{1,0:T(8,128)S(1)} %get-tuple-element.50), channel_id=1, source_target_pairs={{0,1},{1,2},{2,3},{3,0},{4,5},{5,6},{6,7},{7,4},{8,9},{9,10},{10,1... | collective-permute-start | bytes 860168 | tf_op jit(solution)/shard_map/ppermute | solution.py:364
  13.0 21.0 %collective-permute-start.5 = (f32[560,128]{1,0:T(8,128)S(1)}, f32[560,128]{1,0:T(8,128)S(1)}, u32[]{:S(2)}, u32[]{:S(2)}) collective-permute-start(f32[560,128]{1,0:T(8,128)S(1)} %get-tuple-element.51), channel_id=1, source_target_pairs={{0,2},{1,3},{2,0},{3,1},{4,6},{5,7},{6,4},{7,5},{8,10},{9,11},{10,... | collective-permute-start | bytes 860168 | tf_op jit(solution)/shard_map/ppermute | solution.py:364
  13.9 22.5 %collective-permute-start.6 = (f32[560,128]{1,0:T(8,128)S(1)}, f32[560,128]{1,0:T(8,128)S(1)}, u32[]{:S(2)}, u32[]{:S(2)}) collective-permute-start(f32[560,128]{1,0:T(8,128)S(1)} %get-tuple-element.52), channel_id=1, source_target_pairs={{0,3},{1,0},{2,1},{3,2},{4,7},{5,4},{6,5},{7,6},{8,11},{9,8},{10,9... | collective-permute-start | bytes 860168 | tf_op jit(solution)/shard_map/ppermute | solution.py:364
  22.8 24.8 %collective-permute-start.11 = (f32[512,128]{1,0:T(8,128)S(1)}, f32[512,128]{1,0:T(8,128)S(1)}, u32[]{:S(2)}, u32[]{:S(2)}) collective-permute-start(f32[512,128]{1,0:T(8,128)S(1)} %get-tuple-element.62), channel_id=1, source_target_pairs={{0,3},{1,0},{2,1},{3,2},{4,7},{5,4},{6,5},{7,6},{8,11},{9,8},{10,9... | collective-permute-start | bytes 786440 | tf_op jit(solution)/shard_map/ppermute | solution.py:364
  24.1 20.9 %collective-permute-start.7 = (f32[4,256]{1,0:T(4,128)S(1)}, f32[4,256]{1,0:T(4,128)S(1)}, u32[]{:S(2)}, u32[]{:S(2)}) collective-permute-start(f32[4,256]{1,0:T(4,128)S(1)} %get-tuple-element.54), channel_id=1, source_target_pairs={{0,4},{4,8},{8,12},{12,16},{16,20},{20,24},{24,28},{28,32},{32,36}... | collective-permute-start | bytes 12296 | tf_op jit(solution)/shard_map/ppermute | solution.py:428
  28.0 19.6 %collective-permute-start.8 = (f32[4,256]{1,0:T(4,128)S(1)}, f32[4,256]{1,0:T(4,128)S(1)}, u32[]{:S(2)}, u32[]{:S(2)}) collective-permute-start(f32[4,256]{1,0:T(4,128)S(1)} %get-tuple-element.55), channel_id=1, source_target_pairs={{4,0},{8,4},{12,8},{16,12},{20,16},{24,20},{28,24},{32,28},{36,32}... | collective-permute-start | bytes 12296 | tf_op jit(solution)/shard_map/ppermute | solution.py:427
  34.0 14.7 %collective-permute-start.12 = (f32[512,128]{1,0:T(8,128)S(1)}, f32[512,128]{1,0:T(8,128)S(1)}, u32[]{:S(2)}, u32[]{:S(2)}) collective-permute-start(f32[512,128]{1,0:T(8,128)S(1)} %get-tuple-element.63), channel_id=1, source_target_pairs={{0,2},{1,3},{2,0},{3,1},{4,6},{5,7},{6,4},{7,5},{8,10},{9,11},{10,... | collective-permute-start | bytes 786440 | tf_op jit(solution)/shard_map/ppermute | solution.py:364
  36.4 14.3 %collective-permute-start.13 = (f32[512,128]{1,0:T(8,128)S(1)}, f32[512,128]{1,0:T(8,128)S(1)}, u32[]{:S(2)}, u32[]{:S(2)}) collective-permute-start(f32[512,128]{1,0:T(8,128)S(1)} %get-tuple-element.64), channel_id=1, source_target_pairs={{0,1},{1,2},{2,3},{3,0},{4,5},{5,6},{6,7},{7,4},{8,9},{9,10},{10,1... | collective-permute-start | bytes 786440 | tf_op jit(solution)/shard_map/ppermute | solution.py:364
  37.3 11.5 %copy-start.1 = (f32[1,256,256]{2,1,0:T(8,128)S(1)}, f32[1,256,256]{2,1,0:T(8,128)}, u32[]{:S(2)}) copy-start(f32[1,256,256]{2,1,0:T(8,128)} %depth_ref.5) | copy-start | bytes 786436
  37.3 11.5 %copy-start.2 = (s32[1,256,256]{2,1,0:T(8,128)S(1)}, s32[1,256,256]{2,1,0:T(8,128)}, u32[]{:S(2)}) copy-start(s32[1,256,256]{2,1,0:T(8,128)} %wet_ref.5) | copy-start | bytes 786436
  45.1 13.5 %collective-permute-start.14 = (f32[512,128]{1,0:T(8,128)S(1)}, f32[512,128]{1,0:T(8,128)S(1)}, u32[]{:S(2)}, u32[]{:S(2)}) collective-permute-start(f32[512,128]{1,0:T(8,128)S(1)} %get-tuple-element.68), channel_id=1, source_target_pairs={{0,3},{1,0},{2,1},{3,2},{4,7},{5,4},{6,5},{7,6},{8,11},{9,8},{10,9... | collective-permute-start | bytes 786440 | tf_op jit(solution)/shard_map/ppermute | solution.py:364
  47.6 11.0 %collective-permute-start.15 = (f32[512,128]{1,0:T(8,128)S(1)}, f32[512,128]{1,0:T(8,128)S(1)}, u32[]{:S(2)}, u32[]{:S(2)}) collective-permute-start(f32[512,128]{1,0:T(8,128)S(1)} %get-tuple-element.69), channel_id=1, source_target_pairs={{0,2},{1,3},{2,0},{3,1},{4,6},{5,7},{6,4},{7,5},{8,10},{9,11},{10,... | collective-permute-start | bytes 786440 | tf_op jit(solution)/shard_map/ppermute | solution.py:364
  47.6 12.5 %collective-permute-start.16 = (f32[512,128]{1,0:T(8,128)S(1)}, f32[512,128]{1,0:T(8,128)S(1)}, u32[]{:S(2)}, u32[]{:S(2)}) collective-permute-start(f32[512,128]{1,0:T(8,128)S(1)} %get-tuple-element.70), channel_id=1, source_target_pairs={{0,1},{1,2},{2,3},{3,0},{4,5},{5,6},{6,7},{7,4},{8,9},{9,10},{10,1... | collective-permute-start | bytes 786440 | tf_op jit(solution)/shard_map/ppermute | solution.py:364
  48.8 9.8 %collective-permute-start.9 = (f32[4,256]{1,0:T(4,128)S(1)}, f32[4,256]{1,0:T(4,128)S(1)}, u32[]{:S(2)}, u32[]{:S(2)}) collective-permute-start(f32[4,256]{1,0:T(4,128)S(1)} %get-tuple-element.57), channel_id=1, source_target_pairs={{0,4},{4,8},{8,12},{12,16},{16,20},{20,24},{24,28},{28,32},{32,36}... | collective-permute-start | bytes 12296 | tf_op jit(solution)/shard_map/ppermute | solution.py:463
  50.7 7.9 %collective-permute-start.10 = (f32[4,256]{1,0:T(4,128)S(1)}, f32[4,256]{1,0:T(4,128)S(1)}, u32[]{:S(2)}, u32[]{:S(2)}) collective-permute-start(f32[4,256]{1,0:T(4,128)S(1)} %get-tuple-element.58), channel_id=1, source_target_pairs={{4,0},{8,4},{12,8},{16,12},{20,16},{24,20},{28,24},{32,28},{36,32}... | collective-permute-start | bytes 12296 | tf_op jit(solution)/shard_map/ppermute | solution.py:462

commit v4 on v3

--- a/solution.py
+++ b/solution.py
@@ -172,7 +172,7 @@
                 outs[slot][rows[j], :] = out[8 * slot : 8 * slot + 8, j * LANES : (j + 1) * LANES]
         return carry
 
-    lax.fori_loop(0, size, step, 0, unroll=4)
+    lax.fori_loop(0, size, step, 0, unroll=8)
 
 
 def friction_upper(forward_ref, backward_ref, first_ref, last_ref, *refs):
@@ -209,12 +209,13 @@
 def known(freq_ref, behind_ref, strip_ref, state_ref, forcing_ref, east_ref, north_ref, eta_ref, edge_ref):
     me = lax.axis_index("harm")
     shelf = lax.axis_index("sec") == 1
-    take = jnp.logical_and(iota((CELLS, CELLS), 1) == 0, shelf)
+    take = jnp.logical_and(iota((CELLS, LANES), 1) == 0, shelf)
     columns = jnp.concatenate([strip_ref[...], jnp.zeros((4, CELLS), F32)], 0).T
 
     def field(f, ch):
         k = 4 * f + ch
-        return jnp.where(take, columns[:, k : k + 1], state_ref[0, f, ch])
+        left = jnp.where(take, columns[:, k : k + 1], state_ref[0, f, ch, :, :LANES])
+        return jnp.concatenate([left, state_ref[0, f, ch, :, LANES:]], 1)
 
     for i in range(2):
         omega = omega_step * (freq_ref[2 * me + i] + 1).astype(F32)

time: 62.4 us -> 61.4 us (0.984)
  Pallas kernels: 18.7 us -> 16.6 us
  waiting for transfers between devices: 5.27 us -> 6.42 us
    ppermute x12, waiting for transfers between devices: 4.44 us -> 5.59 us  [around(): lax.ppermute(value, 'harm', [(i, (i + steps) % RING) for i in range(RING)])]
    pallas_call x1, Pallas kernels: 4.43 us -> 3.39 us  [body(): pl.pallas_call(friction_lower, name='friction_lower', in_specs=vmem(2) +...]
    pallas_call x1, Pallas kernels: 4.09 us -> 3.05 us  [body(): pl.pallas_call(friction_upper, name='friction_upper', in_specs=vmem(4 + R...]
  transfers between devices with their start and end apart: 17 -> 17, of which waited for: 3 -> 4; matrix products, arithmetic and copies ran while one was open for 0% -> 0% of each run, Pallas kernels for 27% -> 24%
where the time goes in v4:
time: 61.4 us; the launch traced here: 61.1 us
  starting transfers between devices  36.3 us (59%)
  Pallas kernels  16.6 us (27%)
  waiting for transfers between devices  6.42 us (10%)
  local copies, waits for them, and re-layouts  1.47 us (2%)
    ppermute x12, starting transfers between devices, around(): lax.ppermute(value, 'harm', [(i, (i + steps) % RING) for i in range(RING)])  17.3 us
    ppermute x1, starting transfers between devices, body(): after = lax.ppermute(made[RING], 'tile', to_last)  6.04 us
    ppermute x1, starting transfers between devices, body(): after_flux = lax.ppermute(first, 'tile', to_last)  5.87 us
    ppermute x12, waiting for transfers between devices, around(): lax.ppermute(value, 'harm', [(i, (i + steps) % RING) for i in range(RING)])  5.59 us
    ppermute x1, starting transfers between devices, body(): before = lax.ppermute(made[RING + 1], 'tile', to_next)  3.81 us
    pallas_call x1, Pallas kernels, body(): pl.pallas_call(friction_lower, name='friction_lower', in_specs=vmem(2) +...  3.39 us
    pallas_call x1, Pallas kernels, body(): pl.pallas_call(known, name='known', in_specs=[smem, hbm] + vmem(3), out_s...  3.36 us
    pallas_call x1, Pallas kernels, body(): pl.pallas_call(friction_upper, name='friction_upper', in_specs=vmem(4 + R...  3.05 us
  transfers between devices with their start and end apart: 17, of which 4 were waited for; matrix products, arithmetic and copies ran while one was open for 0% of the time, Pallas kernels for 24%

profile of v4, /device:TPU:24, one launch (start us, length us, event | category | flops | bytes accessed | tf_op | source)
XLA Modules:
  0.0 61.1 jit_solution(11030078612139971780)
XLA Ops:
  0.0 0.0 copy-start
  0.0 0.0 copy-start.4
  0.0 0.0 copy-start.5
  0.0 1.4 %slice.3.state_ref = f32[1,2,4,128,256]{4,3,2,1,0:T(8,128)S(1)} slice(f32[1,3,4,256,256]{4,3,2,1,0:T(8,128)} %state_ref.3), slice={[0:1], [1:3], [0:4], [0:128], [0:256]} | slice | bytes 2097152 | tf_op jit(solution)/shard_map/slice | solution.py:386
  1.5 0.2 pack_upper.1
  1.7 1.6 %collective-permute-start.1 = (f32[512,128]{1,0:T(8,128)S(1)}, f32[512,128]{1,0:T(8,128)S(1)}, u32[]{:S(2)}, u32[]{:S(2)}) collective-permute-start(f32[512,128]{1,0:T(8,128)S(1)} %get-tuple-element.44), channel_id=1, source_target_pairs={{0,1},{1,2},{2,3},{3,0},{4,5},{5,6},{6,7},{7,4},{8,9},{9,10},{10,1... | collective-permute-start | bytes 786440 | tf_op jit(solution)/shard_map/ppermute | solution.py:365
  3.2 2.7 %collective-permute-start.2 = (f32[512,128]{1,0:T(8,128)S(1)}, f32[512,128]{1,0:T(8,128)S(1)}, u32[]{:S(2)}, u32[]{:S(2)}) collective-permute-start(f32[512,128]{1,0:T(8,128)S(1)} %get-tuple-element.45), channel_id=1, source_target_pairs={{0,2},{1,3},{2,0},{3,1},{4,6},{5,7},{6,4},{7,5},{8,10},{9,11},{10,... | collective-permute-start | bytes 786440 | tf_op jit(solution)/shard_map/ppermute | solution.py:365
  6.0 1.4 %collective-permute-start.3 = (f32[512,128]{1,0:T(8,128)S(1)}, f32[512,128]{1,0:T(8,128)S(1)}, u32[]{:S(2)}, u32[]{:S(2)}) collective-permute-start(f32[512,128]{1,0:T(8,128)S(1)} %get-tuple-element.46), channel_id=1, source_target_pairs={{0,3},{1,0},{2,1},{3,2},{4,7},{5,4},{6,5},{7,6},{8,11},{9,8},{10,9... | collective-permute-start | bytes 786440 | tf_op jit(solution)/shard_map/ppermute | solution.py:365
  7.4 0.0 copy-done
  7.4 0.0 copy-done.4
  7.4 0.0 copy-done.5
  7.4 0.0 copy-start.3
  7.4 2.5 %prepare.1 = (f32[12,256]{1,0:T(8,128)S(1)}, bf16[128,96]{1,0:T(8,128)(2,1)S(1)}, bf16[64,256]{1,0:T(8,128)(2,1)S(1)}) custom-call(s32[16]{0:T(128)S(1)} %copy-done.4, s32[1,256]{1,0:T(1,128)S(1)} %bitcast.3, f32[12,256,256]{2,1,0:T(8,128)S(1)} %bitcast.2), custom_call_target="tpu_custom_call" | custom-call | bytes 12000000 | tf_op jit(solution)/shard_map/prepare/pallas_call | solution.py:389
  9.9 1.3 %collective-permute-start = (f32[12,256]{1,0:T(8,128)S(1)}, f32[12,256]{1,0:T(8,128)S(1)}, u32[]{:S(2)}, u32[]{:S(2)}) collective-permute-start(f32[12,256]{1,0:T(8,128)S(1)} %get-tuple-element.40), channel_id=1, source_target_pairs={{0,128},{1,129},{2,130},{3,131},{4,132},{5,133},{6,134},{7,135},{8... | collective-permute-start | bytes 36872 | tf_op jit(solution)/shard_map/ppermute | solution.py:398
  11.2 0.8 %collective-permute-done.strip_ref = f32[12,256]{1,0:T(8,128)S(1)} collective-permute-done((f32[12,256]{1,0:T(8,128)S(1)}, f32[12,256]{1,0:T(8,128)S(1)}, u32[]{:S(2)}, u32[]{:S(2)}) %collective-permute-start) | collective-permute-done | bytes 12320 | tf_op jit(solution)/shard_map/ppermute | solution.py:398
  12.1 0.3 pack_lower.1
  12.4 0.7 %collective-permute-start.4 = (f32[560,128]{1,0:T(8,128)S(1)}, f32[560,128]{1,0:T(8,128)S(1)}, u32[]{:S(2)}, u32[]{:S(2)}) collective-permute-start(f32[560,128]{1,0:T(8,128)S(1)} %get-tuple-element.50), channel_id=1, source_target_pairs={{0,1},{1,2},{2,3},{3,0},{4,5},{5,6},{6,7},{7,4},{8,9},{9,10},{10,1... | collective-permute-start | bytes 860168 | tf_op jit(solution)/shard_map/ppermute | solution.py:365
  13.0 0.9 %collective-permute-start.5 = (f32[560,128]{1,0:T(8,128)S(1)}, f32[560,128]{1,0:T(8,128)S(1)}, u32[]{:S(2)}, u32[]{:S(2)}) collective-permute-start(f32[560,128]{1,0:T(8,128)S(1)} %get-tuple-element.51), channel_id=1, source_target_pairs={{0,2},{1,3},{2,0},{3,1},{4,6},{5,7},{6,4},{7,5},{8,10},{9,11},{10,... | collective-permute-start | bytes 860168 | tf_op jit(solution)/shard_map/ppermute | solution.py:365
  13.9 0.0 collective-permute-done.1.refs_1_
  13.9 1.9 %collective-permute-start.6 = (f32[560,128]{1,0:T(8,128)S(1)}, f32[560,128]{1,0:T(8,128)S(1)}, u32[]{:S(2)}, u32[]{:S(2)}) collective-permute-start(f32[560,128]{1,0:T(8,128)S(1)} %get-tuple-element.52), channel_id=1, source_target_pairs={{0,3},{1,0},{2,1},{3,2},{4,7},{5,4},{6,5},{7,6},{8,11},{9,8},{10,9... | collective-permute-start | bytes 860168 | tf_op jit(solution)/shard_map/ppermute | solution.py:365
  15.8 2.9 %collective-permute-done.2.refs_2_ = f32[512,128]{1,0:T(8,128)S(1)} collective-permute-done((f32[512,128]{1,0:T(8,128)S(1)}, f32[512,128]{1,0:T(8,128)S(1)}, u32[]{:S(2)}, u32[]{:S(2)}) %collective-permute-start.2) | collective-permute-done | bytes 262176 | tf_op jit(solution)/shard_map/ppermute | solution.py:365
  18.7 0.0 collective-permute-done.3.refs_3_
  18.7 3.1 %friction_upper.1 = (f32[512,128]{1,0:T(8,128)S(1)}, f32[512,128]{1,0:T(8,128)S(1)}, f32[512,128]{1,0:T(8,128)S(1)}, f32[512,128]{1,0:T(8,128)S(1)}, f32[4,256]{1,0:T(4,128)S(1)}, /*index=5*/f32[4,256]{1,0:T(4,128)S(1)}) custom-call(bf16[128,96]{1,0:T(8,128)(2,1)S(1)} %get-tuple-element.38.forward_ref, bf16[64,256]{1,0:T(8,128)(2,1)S(1)} %get-tuple-element.39.backward_ref, ...), custom_call_target="tpu_custom_call" | custom-call | bytes 12000000 | tf_op jit(solution)/shard_map/friction_upper/pallas_call | solution.py:419
  21.8 1.3 %collective-permute-start.11 = (f32[512,128]{1,0:T(8,128)S(1)}, f32[512,128]{1,0:T(8,128)S(1)}, u32[]{:S(2)}, u32[]{:S(2)}) collective-permute-start(f32[512,128]{1,0:T(8,128)S(1)} %get-tuple-element.62), channel_id=1, source_target_pairs={{0,3},{1,0},{2,1},{3,2},{4,7},{5,4},{6,5},{7,6},{8,11},{9,8},{10,9... | collective-permute-start | bytes 786440 | tf_op jit(solution)/shard_map/ppermute | solution.py:365
  23.1 3.8 %collective-permute-start.7 = (f32[4,256]{1,0:T(4,128)S(1)}, f32[4,256]{1,0:T(4,128)S(1)}, u32[]{:S(2)}, u32[]{:S(2)}) collective-permute-start(f32[4,256]{1,0:T(4,128)S(1)} %get-tuple-element.54), channel_id=1, source_target_pairs={{0,4},{4,8},{8,12},{12,16},{16,20},{20,24},{24,28},{28,32},{32,36}... | collective-permute-start | bytes 12296 | tf_op jit(solution)/shard_map/ppermute | solution.py:429
  26.9 0.0 collective-permute-done.4.refs_1_
  26.9 6.0 %collective-permute-start.8 = (f32[4,256]{1,0:T(4,128)S(1)}, f32[4,256]{1,0:T(4,128)S(1)}, u32[]{:S(2)}, u32[]{:S(2)}) collective-permute-start(f32[4,256]{1,0:T(4,128)S(1)} %get-tuple-element.55), channel_id=1, source_target_pairs={{4,0},{8,4},{12,8},{16,12},{20,16},{24,20},{28,24},{32,28},{36,32}... | collective-permute-start | bytes 12296 | tf_op jit(solution)/shard_map/ppermute | solution.py:428
  33.0 0.0 collective-permute-done.5.refs_2_
  33.0 2.4 %collective-permute-start.12 = (f32[512,128]{1,0:T(8,128)S(1)}, f32[512,128]{1,0:T(8,128)S(1)}, u32[]{:S(2)}, u32[]{:S(2)}) collective-permute-start(f32[512,128]{1,0:T(8,128)S(1)} %get-tuple-element.63), channel_id=1, source_target_pairs={{0,2},{1,3},{2,0},{3,1},{4,6},{5,7},{6,4},{7,5},{8,10},{9,11},{10,... | collective-permute-start | bytes 786440 | tf_op jit(solution)/shard_map/ppermute | solution.py:365
  35.4 0.0 collective-permute-done.6.refs_3_
  35.4 0.8 %collective-permute-start.13 = (f32[512,128]{1,0:T(8,128)S(1)}, f32[512,128]{1,0:T(8,128)S(1)}, u32[]{:S(2)}, u32[]{:S(2)}) collective-permute-start(f32[512,128]{1,0:T(8,128)S(1)} %get-tuple-element.64), channel_id=1, source_target_pairs={{0,1},{1,2},{2,3},{3,0},{4,5},{5,6},{6,7},{7,4},{8,9},{9,10},{10,1... | collective-permute-start | bytes 786440 | tf_op jit(solution)/shard_map/ppermute | solution.py:365
  36.2 0.0 copy-done.3
  36.2 0.0 copy-start.1
  36.2 0.0 copy-start.2
  36.2 3.4 %known.1 = (f32[4,256,256]{2,1,0:T(8,128)S(1)}, f32[4,256,256]{2,1,0:T(8,128)S(1)}, f32[4,256,256]{2,1,0:T(8,128)S(1)}, f32[8,256]{1,0:T(8,128)S(1)}) custom-call(s32[16]{0:T(128)S(1)} %copy-done.4, f32[512,128]{1,0:T(8,128)S(1)} %get-tuple-element.47.behind_ref.refs_0_, f32[12,256]{1,0:T(8,128)S(1)} %collective-permute-done.strip_ref, ...), custom_call_target="tpu_custom_call" | custom-call | bytes 15000000 | tf_op jit(solution)/shard_map/known/pallas_call | solution.py:432
  39.6 3.4 %friction_lower.1 = (f32[512,128]{1,0:T(8,128)S(1)}, f32[512,128]{1,0:T(8,128)S(1)}, f32[512,128]{1,0:T(8,128)S(1)}, f32[512,128]{1,0:T(8,128)S(1)}, f32[24,256]{1,0:T(8,128)S(1)}) custom-call(bf16[128,96]{1,0:T(8,128)(2,1)S(1)} %get-tuple-element.38.forward_ref, bf16[64,256]{1,0:T(8,128)(2,1)S(1)} %get-tuple-element.39.backward_ref, ...), custom_call_target="tpu_custom_call" | custom-call | bytes 12000000 | tf_op jit(solution)/shard_map/friction_lower/pallas_call | solution.py:442
  43.0 0.0 collective-permute-done.7.before_ref
  43.0 2.7 %collective-permute-start.14 = (f32[512,128]{1,0:T(8,128)S(1)}, f32[512,128]{1,0:T(8,128)S(1)}, u32[]{:S(2)}, u32[]{:S(2)}) collective-permute-start(f32[512,128]{1,0:T(8,128)S(1)} %get-tuple-element.68), channel_id=1, source_target_pairs={{0,3},{1,0},{2,1},{3,2},{4,7},{5,4},{6,5},{7,6},{8,11},{9,8},{10,9... | collective-permute-start | bytes 786440 | tf_op jit(solution)/shard_map/ppermute | solution.py:365
  45.7 0.0 collective-permute-done.8.after_ref
  45.7 0.0 collective-permute-start.15
  45.7 0.0 collective-permute-done.11.refs_1_
  45.7 1.0 %collective-permute-start.16 = (f32[512,128]{1,0:T(8,128)S(1)}, f32[512,128]{1,0:T(8,128)S(1)}, u32[]{:S(2)}, u32[]{:S(2)}) collective-permute-start(f32[512,128]{1,0:T(8,128)S(1)} %get-tuple-element.70), channel_id=1, source_target_pairs={{0,1},{1,2},{2,3},{3,0},{4,5},{5,6},{6,7},{7,4},{8,9},{9,10},{10,1... | collective-permute-start | bytes 786440 | tf_op jit(solution)/shard_map/ppermute | solution.py:365
  46.7 0.0 copy-done.1
  46.7 0.0 copy-done.2
  46.7 0.0 collective-permute-done.12.refs_2_
  46.7 1.9 %collective-permute-start.9 = (f32[4,256]{1,0:T(4,128)S(1)}, f32[4,256]{1,0:T(4,128)S(1)}, u32[]{:S(2)}, u32[]{:S(2)}) collective-permute-start(f32[4,256]{1,0:T(4,128)S(1)} %get-tuple-element.57), channel_id=1, source_target_pairs={{0,4},{4,8},{8,12},{12,16},{16,20},{20,24},{24,28},{28,32},{32,36}... | collective-permute-start | bytes 12296 | tf_op jit(solution)/shard_map/ppermute | solution.py:464
  48.6 0.2 collective-permute-done.13.refs_3_
  48.8 5.9 %collective-permute-start.10 = (f32[4,256]{1,0:T(4,128)S(1)}, f32[4,256]{1,0:T(4,128)S(1)}, u32[]{:S(2)}, u32[]{:S(2)}) collective-permute-start(f32[4,256]{1,0:T(4,128)S(1)} %get-tuple-element.58), channel_id=1, source_target_pairs={{4,0},{8,4},{12,8},{16,12},{20,16},{24,20},{28,24},{32,28},{36,32}... | collective-permute-start | bytes 12296 | tf_op jit(solution)/shard_map/ppermute | solution.py:463
  54.7 1.8 %finish_upper.1 = (f32[1,3,4,256,256]{4,3,2,1,0:T(8,128)}, f32[2,4,32,256]{3,2,1,0:T(8,128)S(1)}) custom-call(f32[24,256]{1,0:T(8,128)S(1)} %get-tuple-element.53.extra_ref, f32[1,256,256]{2,1,0:T(8,128)S(1)} %copy-done.1, s32[1,256,256]{2,1,0:T(8,128)S(1)} %copy-done.2, f32[4,256,256]{2,1,0:T(8,128)S(1)} %get-tuple-element.59.east_ref, ...), custom_call_target="tpu_custom_call" | custom-call | bytes 9000000 | tf_op jit(solution)/shard_map/finish_upper/pallas_call | solution.py:467
  56.5 0.0 collective-permute-done.9.before_ref
  56.5 0.0 collective-permute-done.10.after_ref
  56.5 0.0 collective-permute-done.14.refs_1_
  56.5 0.0 collective-permute-done.15.refs_2_
  56.5 2.5 %collective-permute-done.16.refs_3_ = f32[512,128]{1,0:T(8,128)S(1)} collective-permute-done((f32[512,128]{1,0:T(8,128)S(1)}, f32[512,128]{1,0:T(8,128)S(1)}, u32[]{:S(2)}, u32[]{:S(2)}) %collective-permute-start.16) | collective-permute-done | bytes 262176 | tf_op jit(solution)/shard_map/ppermute | solution.py:365
  59.0 2.0 %finish_lower.1 = f32[1,3,4,256,256]{4,3,2,1,0:T(8,128)} custom-call(f32[24,256]{1,0:T(8,128)S(1)} %get-tuple-element.53.extra_ref, f32[8,256]{1,0:T(8,128)S(1)} %get-tuple-element.56.edge_ref, f32[4,256]{1,0:T(4,128)S(1)} %collective-permute-done.9.before_ref, f32[4,256]{1,0:T(4,128)S(1)} %collective-permute-done.10.after_ref, ...), custom_call_target="tpu_custom_call", output_to_operand_aliasing={{}: (10, {})} | custom-call | bytes 9000000 | tf_op jit(solution)/shard_map/finish_lower/pallas_call | solution.py:481
  (1 shorter events, 0.0 us)
Async XLA Ops:
  0.0 7.4 %copy-start = (f32[1,3,4,256,256]{4,3,2,1,0:T(8,128)S(1)}, f32[1,3,4,256,256]{4,3,2,1,0:T(8,128)}, u32[]{:S(2)}) copy-start(f32[1,3,4,256,256]{4,3,2,1,0:T(8,128)} %state_ref.3) | copy-start | bytes 9437188
  0.0 7.4 %copy-start.4 = (s32[16]{0:T(128)S(1)}, s32[16]{0:T(128)}, u32[]{:S(2)}) copy-start(s32[16]{0:T(128)} %freq_ref.3) | copy-start | bytes 196
  0.0 7.4 %copy-start.5 = (s32[256]{0:T(256)S(1)}, s32[256]{0:T(256)}, u32[]{:S(2)}) copy-start(s32[256]{0:T(256)} %param.10) | copy-start | bytes 3076
  1.7 12.3 %collective-permute-start.1 = (f32[512,128]{1,0:T(8,128)S(1)}, f32[512,128]{1,0:T(8,128)S(1)}, u32[]{:S(2)}, u32[]{:S(2)}) collective-permute-start(f32[512,128]{1,0:T(8,128)S(1)} %get-tuple-element.44), channel_id=1, source_target_pairs={{0,1},{1,2},{2,3},{3,0},{4,5},{5,6},{6,7},{7,4},{8,9},{9,10},{10,1... | collective-permute-start | bytes 786440 | tf_op jit(solution)/shard_map/ppermute | solution.py:365
  3.2 15.5 %collective-permute-start.2 = (f32[512,128]{1,0:T(8,128)S(1)}, f32[512,128]{1,0:T(8,128)S(1)}, u32[]{:S(2)}, u32[]{:S(2)}) collective-permute-start(f32[512,128]{1,0:T(8,128)S(1)} %get-tuple-element.45), channel_id=1, source_target_pairs={{0,2},{1,3},{2,0},{3,1},{4,6},{5,7},{6,4},{7,5},{8,10},{9,11},{10,... | collective-permute-start | bytes 786440 | tf_op jit(solution)/shard_map/ppermute | solution.py:365
  6.0 12.8 %collective-permute-start.3 = (f32[512,128]{1,0:T(8,128)S(1)}, f32[512,128]{1,0:T(8,128)S(1)}, u32[]{:S(2)}, u32[]{:S(2)}) collective-permute-start(f32[512,128]{1,0:T(8,128)S(1)} %get-tuple-element.46), channel_id=1, source_target_pairs={{0,3},{1,0},{2,1},{3,2},{4,7},{5,4},{6,5},{7,6},{8,11},{9,8},{10,9... | collective-permute-start | bytes 786440 | tf_op jit(solution)/shard_map/ppermute | solution.py:365
  7.4 28.8 %copy-start.3 = (f32[1,2,4,256,256]{4,3,2,1,0:T(8,128)S(1)}, f32[1,2,4,256,256]{4,3,2,1,0:T(8,128)}, u32[]{:S(2)}) copy-start(f32[1,2,4,256,256]{4,3,2,1,0:T(8,128)} %forcing_ref.1) | copy-start | bytes 6291460
  9.9 2.1 %collective-permute-start = (f32[12,256]{1,0:T(8,128)S(1)}, f32[12,256]{1,0:T(8,128)S(1)}, u32[]{:S(2)}, u32[]{:S(2)}) collective-permute-start(f32[12,256]{1,0:T(8,128)S(1)} %get-tuple-element.40), channel_id=1, source_target_pairs={{0,128},{1,129},{2,130},{3,131},{4,132},{5,133},{6,134},{7,135},{8... | collective-permute-start | bytes 36872 | tf_op jit(solution)/shard_map/ppermute | solution.py:398
  12.4 14.6 %collective-permute-start.4 = (f32[560,128]{1,0:T(8,128)S(1)}, f32[560,128]{1,0:T(8,128)S(1)}, u32[]{:S(2)}, u32[]{:S(2)}) collective-permute-start(f32[560,128]{1,0:T(8,128)S(1)} %get-tuple-element.50), channel_id=1, source_target_pairs={{0,1},{1,2},{2,3},{3,0},{4,5},{5,6},{6,7},{7,4},{8,9},{9,10},{10,1... | collective-permute-start | bytes 860168 | tf_op jit(solution)/shard_map/ppermute | solution.py:365
  13.0 19.9 %collective-permute-start.5 = (f32[560,128]{1,0:T(8,128)S(1)}, f32[560,128]{1,0:T(8,128)S(1)}, u32[]{:S(2)}, u32[]{:S(2)}) collective-permute-start(f32[560,128]{1,0:T(8,128)S(1)} %get-tuple-element.51), channel_id=1, source_target_pairs={{0,2},{1,3},{2,0},{3,1},{4,6},{5,7},{6,4},{7,5},{8,10},{9,11},{10,... | collective-permute-start | bytes 860168 | tf_op jit(solution)/shard_map/ppermute | solution.py:365
  13.9 21.5 %collective-permute-start.6 = (f32[560,128]{1,0:T(8,128)S(1)}, f32[560,128]{1,0:T(8,128)S(1)}, u32[]{:S(2)}, u32[]{:S(2)}) collective-permute-start(f32[560,128]{1,0:T(8,128)S(1)} %get-tuple-element.52), channel_id=1, source_target_pairs={{0,3},{1,0},{2,1},{3,2},{4,7},{5,4},{6,5},{7,6},{8,11},{9,8},{10,9... | collective-permute-start | bytes 860168 | tf_op jit(solution)/shard_map/ppermute | solution.py:365
  21.8 23.9 %collective-permute-start.11 = (f32[512,128]{1,0:T(8,128)S(1)}, f32[512,128]{1,0:T(8,128)S(1)}, u32[]{:S(2)}, u32[]{:S(2)}) collective-permute-start(f32[512,128]{1,0:T(8,128)S(1)} %get-tuple-element.62), channel_id=1, source_target_pairs={{0,3},{1,0},{2,1},{3,2},{4,7},{5,4},{6,5},{7,6},{8,11},{9,8},{10,9... | collective-permute-start | bytes 786440 | tf_op jit(solution)/shard_map/ppermute | solution.py:365
  23.1 19.9 %collective-permute-start.7 = (f32[4,256]{1,0:T(4,128)S(1)}, f32[4,256]{1,0:T(4,128)S(1)}, u32[]{:S(2)}, u32[]{:S(2)}) collective-permute-start(f32[4,256]{1,0:T(4,128)S(1)} %get-tuple-element.54), channel_id=1, source_target_pairs={{0,4},{4,8},{8,12},{12,16},{16,20},{20,24},{24,28},{28,32},{32,36}... | collective-permute-start | bytes 12296 | tf_op jit(solution)/shard_map/ppermute | solution.py:429
  26.9 18.8 %collective-permute-start.8 = (f32[4,256]{1,0:T(4,128)S(1)}, f32[4,256]{1,0:T(4,128)S(1)}, u32[]{:S(2)}, u32[]{:S(2)}) collective-permute-start(f32[4,256]{1,0:T(4,128)S(1)} %get-tuple-element.55), channel_id=1, source_target_pairs={{4,0},{8,4},{12,8},{16,12},{20,16},{24,20},{28,24},{32,28},{36,32}... | collective-permute-start | bytes 12296 | tf_op jit(solution)/shard_map/ppermute | solution.py:428
  33.0 13.7 %collective-permute-start.12 = (f32[512,128]{1,0:T(8,128)S(1)}, f32[512,128]{1,0:T(8,128)S(1)}, u32[]{:S(2)}, u32[]{:S(2)}) collective-permute-start(f32[512,128]{1,0:T(8,128)S(1)} %get-tuple-element.63), channel_id=1, source_target_pairs={{0,2},{1,3},{2,0},{3,1},{4,6},{5,7},{6,4},{7,5},{8,10},{9,11},{10,... | collective-permute-start | bytes 786440 | tf_op jit(solution)/shard_map/ppermute | solution.py:365
  35.4 13.4 %collective-permute-start.13 = (f32[512,128]{1,0:T(8,128)S(1)}, f32[512,128]{1,0:T(8,128)S(1)}, u32[]{:S(2)}, u32[]{:S(2)}) collective-permute-start(f32[512,128]{1,0:T(8,128)S(1)} %get-tuple-element.64), channel_id=1, source_target_pairs={{0,1},{1,2},{2,3},{3,0},{4,5},{5,6},{6,7},{7,4},{8,9},{9,10},{10,1... | collective-permute-start | bytes 786440 | tf_op jit(solution)/shard_map/ppermute | solution.py:365
  36.2 10.5 %copy-start.1 = (f32[1,256,256]{2,1,0:T(8,128)S(1)}, f32[1,256,256]{2,1,0:T(8,128)}, u32[]{:S(2)}) copy-start(f32[1,256,256]{2,1,0:T(8,128)} %depth_ref.5) | copy-start | bytes 786436
  36.2 10.5 %copy-start.2 = (s32[1,256,256]{2,1,0:T(8,128)S(1)}, s32[1,256,256]{2,1,0:T(8,128)}, u32[]{:S(2)}) copy-start(s32[1,256,256]{2,1,0:T(8,128)} %wet_ref.5) | copy-start | bytes 786436
  43.0 13.5 %collective-permute-start.14 = (f32[512,128]{1,0:T(8,128)S(1)}, f32[512,128]{1,0:T(8,128)S(1)}, u32[]{:S(2)}, u32[]{:S(2)}) collective-permute-start(f32[512,128]{1,0:T(8,128)S(1)} %get-tuple-element.68), channel_id=1, source_target_pairs={{0,3},{1,0},{2,1},{3,2},{4,7},{5,4},{6,5},{7,6},{8,11},{9,8},{10,9... | collective-permute-start | bytes 786440 | tf_op jit(solution)/shard_map/ppermute | solution.py:365
  45.7 10.8 %collective-permute-start.15 = (f32[512,128]{1,0:T(8,128)S(1)}, f32[512,128]{1,0:T(8,128)S(1)}, u32[]{:S(2)}, u32[]{:S(2)}) collective-permute-start(f32[512,128]{1,0:T(8,128)S(1)} %get-tuple-element.69), channel_id=1, source_target_pairs={{0,2},{1,3},{2,0},{3,1},{4,6},{5,7},{6,4},{7,5},{8,10},{9,11},{10,... | collective-permute-start | bytes 786440 | tf_op jit(solution)/shard_map/ppermute | solution.py:365
  45.7 13.3 %collective-permute-start.16 = (f32[512,128]{1,0:T(8,128)S(1)}, f32[512,128]{1,0:T(8,128)S(1)}, u32[]{:S(2)}, u32[]{:S(2)}) collective-permute-start(f32[512,128]{1,0:T(8,128)S(1)} %get-tuple-element.70), channel_id=1, source_target_pairs={{0,1},{1,2},{2,3},{3,0},{4,5},{5,6},{6,7},{7,4},{8,9},{9,10},{10,1... | collective-permute-start | bytes 786440 | tf_op jit(solution)/shard_map/ppermute | solution.py:365
  46.7 9.8 %collective-permute-start.9 = (f32[4,256]{1,0:T(4,128)S(1)}, f32[4,256]{1,0:T(4,128)S(1)}, u32[]{:S(2)}, u32[]{:S(2)}) collective-permute-start(f32[4,256]{1,0:T(4,128)S(1)} %get-tuple-element.57), channel_id=1, source_target_pairs={{0,4},{4,8},{8,12},{12,16},{16,20},{20,24},{24,28},{28,32},{32,36}... | collective-permute-start | bytes 12296 | tf_op jit(solution)/shard_map/ppermute | solution.py:464
  48.8 7.7 %collective-permute-start.10 = (f32[4,256]{1,0:T(4,128)S(1)}, f32[4,256]{1,0:T(4,128)S(1)}, u32[]{:S(2)}, u32[]{:S(2)}) collective-permute-start(f32[4,256]{1,0:T(4,128)S(1)} %get-tuple-element.58), channel_id=1, source_target_pairs={{4,0},{8,4},{12,8},{16,12},{20,16},{24,20},{28,24},{32,28},{36,32}... | collective-permute-start | bytes 12296 | tf_op jit(solution)/shard_map/ppermute | solution.py:463

commit v5 on v4

--- a/solution.py
+++ b/solution.py
@@ -172,7 +172,7 @@
                 outs[slot][rows[j], :] = out[8 * slot : 8 * slot + 8, j * LANES : (j + 1) * LANES]
         return carry
 
-    lax.fori_loop(0, size, step, 0, unroll=8)
+    lax.fori_loop(0, size, step, 0, unroll=16)
 
 
 def friction_upper(forward_ref, backward_ref, first_ref, last_ref, *refs):

time: 61.4 us -> 61.3 us (level)
  waiting for transfers between devices: 6.42 us -> 7.33 us
  starting transfers between devices: 36.3 us -> 35.5 us
    ppermute x12, waiting for transfers between devices: 5.59 us -> 6.49 us  [around(): lax.ppermute(value, 'harm', [(i, (i + steps) % RING) for i in range(RING)])]
  transfers between devices with their start and end apart: 17 -> 17, of which waited for: 4 -> 4; matrix products, arithmetic and copies ran while one was open for 0% -> 0% of each run, Pallas kernels for 24% -> 23%
where the time goes in v5:
time: 61.3 us; the launch traced here: 61 us
  starting transfers between devices  35.5 us (58%)
  Pallas kernels  16.3 us (27%)
  waiting for transfers between devices  7.33 us (12%)
  local copies, waits for them, and re-layouts  1.47 us (2%)
    ppermute x12, starting transfers between devices, around(): lax.ppermute(value, 'harm', [(i, (i + steps) % RING) for i in range(RING)])  17.1 us
    ppermute x12, waiting for transfers between devices, around(): lax.ppermute(value, 'harm', [(i, (i + steps) % RING) for i in range(RING)])  6.49 us
    ppermute x1, starting transfers between devices, body(): after = lax.ppermute(made[RING], 'tile', to_last)  6.13 us
    ppermute x1, starting transfers between devices, body(): after_flux = lax.ppermute(first, 'tile', to_last)  5.32 us
    ppermute x1, starting transfers between devices, body(): before = lax.ppermute(made[RING + 1], 'tile', to_next)  3.81 us
    pallas_call x1, Pallas kernels, body(): pl.pallas_call(known, name='known', in_specs=[smem, hbm] + vmem(3), out_s...  3.36 us
    pallas_call x1, Pallas kernels, body(): pl.pallas_call(friction_lower, name='friction_lower', in_specs=vmem(2) +...  3.24 us
    pallas_call x1, Pallas kernels, body(): pl.pallas_call(friction_upper, name='friction_upper', in_specs=vmem(4 + R...  2.89 us
  transfers between devices with their start and end apart: 17, of which 4 were waited for; matrix products, arithmetic and copies ran while one was open for 0% of the time, Pallas kernels for 23%

profile of v5, /device:TPU:24, one launch (start us, length us, event | category | flops | bytes accessed | tf_op | source)
XLA Modules:
  0.0 61.0 jit_solution(9509885048258860376)
XLA Ops:
  0.0 0.0 copy-start
  0.0 0.0 copy-start.4
  0.0 0.0 copy-start.5
  0.0 1.4 %slice.3.state_ref = f32[1,2,4,128,256]{4,3,2,1,0:T(8,128)S(1)} slice(f32[1,3,4,256,256]{4,3,2,1,0:T(8,128)} %state_ref.3), slice={[0:1], [1:3], [0:4], [0:128], [0:256]} | slice | bytes 2097152 | tf_op jit(solution)/shard_map/slice | solution.py:386
  1.5 0.2 pack_upper.1
  1.7 1.6 %collective-permute-start.1 = (f32[512,128]{1,0:T(8,128)S(1)}, f32[512,128]{1,0:T(8,128)S(1)}, u32[]{:S(2)}, u32[]{:S(2)}) collective-permute-start(f32[512,128]{1,0:T(8,128)S(1)} %get-tuple-element.44), channel_id=1, source_target_pairs={{0,1},{1,2},{2,3},{3,0},{4,5},{5,6},{6,7},{7,4},{8,9},{9,10},{10,1... | collective-permute-start | bytes 786440 | tf_op jit(solution)/shard_map/ppermute | solution.py:365
  3.2 2.7 %collective-permute-start.2 = (f32[512,128]{1,0:T(8,128)S(1)}, f32[512,128]{1,0:T(8,128)S(1)}, u32[]{:S(2)}, u32[]{:S(2)}) collective-permute-start(f32[512,128]{1,0:T(8,128)S(1)} %get-tuple-element.45), channel_id=1, source_target_pairs={{0,2},{1,3},{2,0},{3,1},{4,6},{5,7},{6,4},{7,5},{8,10},{9,11},{10,... | collective-permute-start | bytes 786440 | tf_op jit(solution)/shard_map/ppermute | solution.py:365
  6.0 1.4 %collective-permute-start.3 = (f32[512,128]{1,0:T(8,128)S(1)}, f32[512,128]{1,0:T(8,128)S(1)}, u32[]{:S(2)}, u32[]{:S(2)}) collective-permute-start(f32[512,128]{1,0:T(8,128)S(1)} %get-tuple-element.46), channel_id=1, source_target_pairs={{0,3},{1,0},{2,1},{3,2},{4,7},{5,4},{6,5},{7,6},{8,11},{9,8},{10,9... | collective-permute-start | bytes 786440 | tf_op jit(solution)/shard_map/ppermute | solution.py:365
  7.4 0.0 copy-done
  7.4 0.0 copy-done.4
  7.4 0.0 copy-done.5
  7.4 0.0 copy-start.3
  7.4 2.5 %prepare.1 = (f32[12,256]{1,0:T(8,128)S(1)}, bf16[128,96]{1,0:T(8,128)(2,1)S(1)}, bf16[64,256]{1,0:T(8,128)(2,1)S(1)}) custom-call(s32[16]{0:T(128)S(1)} %copy-done.4, s32[1,256]{1,0:T(1,128)S(1)} %bitcast.3, f32[12,256,256]{2,1,0:T(8,128)S(1)} %bitcast.2), custom_call_target="tpu_custom_call" | custom-call | bytes 12000000 | tf_op jit(solution)/shard_map/prepare/pallas_call | solution.py:389
  9.9 1.3 %collective-permute-start = (f32[12,256]{1,0:T(8,128)S(1)}, f32[12,256]{1,0:T(8,128)S(1)}, u32[]{:S(2)}, u32[]{:S(2)}) collective-permute-start(f32[12,256]{1,0:T(8,128)S(1)} %get-tuple-element.40), channel_id=1, source_target_pairs={{0,128},{1,129},{2,130},{3,131},{4,132},{5,133},{6,134},{7,135},{8... | collective-permute-start | bytes 36872 | tf_op jit(solution)/shard_map/ppermute | solution.py:398
  11.2 0.8 %collective-permute-done.strip_ref = f32[12,256]{1,0:T(8,128)S(1)} collective-permute-done((f32[12,256]{1,0:T(8,128)S(1)}, f32[12,256]{1,0:T(8,128)S(1)}, u32[]{:S(2)}, u32[]{:S(2)}) %collective-permute-start) | collective-permute-done | bytes 12320 | tf_op jit(solution)/shard_map/ppermute | solution.py:398
  12.1 0.3 pack_lower.1
  12.4 0.7 %collective-permute-start.4 = (f32[560,128]{1,0:T(8,128)S(1)}, f32[560,128]{1,0:T(8,128)S(1)}, u32[]{:S(2)}, u32[]{:S(2)}) collective-permute-start(f32[560,128]{1,0:T(8,128)S(1)} %get-tuple-element.50), channel_id=1, source_target_pairs={{0,1},{1,2},{2,3},{3,0},{4,5},{5,6},{6,7},{7,4},{8,9},{9,10},{10,1... | collective-permute-start | bytes 860168 | tf_op jit(solution)/shard_map/ppermute | solution.py:365
  13.0 0.9 %collective-permute-start.5 = (f32[560,128]{1,0:T(8,128)S(1)}, f32[560,128]{1,0:T(8,128)S(1)}, u32[]{:S(2)}, u32[]{:S(2)}) collective-permute-start(f32[560,128]{1,0:T(8,128)S(1)} %get-tuple-element.51), channel_id=1, source_target_pairs={{0,2},{1,3},{2,0},{3,1},{4,6},{5,7},{6,4},{7,5},{8,10},{9,11},{10,... | collective-permute-start | bytes 860168 | tf_op jit(solution)/shard_map/ppermute | solution.py:365
  13.9 0.0 collective-permute-done.1.refs_1_
  13.9 1.9 %collective-permute-start.6 = (f32[560,128]{1,0:T(8,128)S(1)}, f32[560,128]{1,0:T(8,128)S(1)}, u32[]{:S(2)}, u32[]{:S(2)}) collective-permute-start(f32[560,128]{1,0:T(8,128)S(1)} %get-tuple-element.52), channel_id=1, source_target_pairs={{0,3},{1,0},{2,1},{3,2},{4,7},{5,4},{6,5},{7,6},{8,11},{9,8},{10,9... | collective-permute-start | bytes 860168 | tf_op jit(solution)/shard_map/ppermute | solution.py:365
  15.8 2.9 %collective-permute-done.2.refs_2_ = f32[512,128]{1,0:T(8,128)S(1)} collective-permute-done((f32[512,128]{1,0:T(8,128)S(1)}, f32[512,128]{1,0:T(8,128)S(1)}, u32[]{:S(2)}, u32[]{:S(2)}) %collective-permute-start.2) | collective-permute-done | bytes 262176 | tf_op jit(solution)/shard_map/ppermute | solution.py:365
  18.7 0.0 collective-permute-done.3.refs_3_
  18.7 2.9 %friction_upper.1 = (f32[512,128]{1,0:T(8,128)S(1)}, f32[512,128]{1,0:T(8,128)S(1)}, f32[512,128]{1,0:T(8,128)S(1)}, f32[512,128]{1,0:T(8,128)S(1)}, f32[4,256]{1,0:T(4,128)S(1)}, /*index=5*/f32[4,256]{1,0:T(4,128)S(1)}) custom-call(bf16[128,96]{1,0:T(8,128)(2,1)S(1)} %get-tuple-element.38.forward_ref, bf16[64,256]{1,0:T(8,128)(2,1)S(1)} %get-tuple-element.39.backward_ref, ...), custom_call_target="tpu_custom_call" | custom-call | bytes 12000000 | tf_op jit(solution)/shard_map/friction_upper/pallas_call | solution.py:419
  21.6 1.3 %collective-permute-start.11 = (f32[512,128]{1,0:T(8,128)S(1)}, f32[512,128]{1,0:T(8,128)S(1)}, u32[]{:S(2)}, u32[]{:S(2)}) collective-permute-start(f32[512,128]{1,0:T(8,128)S(1)} %get-tuple-element.62), channel_id=1, source_target_pairs={{0,3},{1,0},{2,1},{3,2},{4,7},{5,4},{6,5},{7,6},{8,11},{9,8},{10,9... | collective-permute-start | bytes 786440 | tf_op jit(solution)/shard_map/ppermute | solution.py:365
  22.9 3.8 %collective-permute-start.7 = (f32[4,256]{1,0:T(4,128)S(1)}, f32[4,256]{1,0:T(4,128)S(1)}, u32[]{:S(2)}, u32[]{:S(2)}) collective-permute-start(f32[4,256]{1,0:T(4,128)S(1)} %get-tuple-element.54), channel_id=1, source_target_pairs={{0,4},{4,8},{8,12},{12,16},{16,20},{20,24},{24,28},{28,32},{32,36}... | collective-permute-start | bytes 12296 | tf_op jit(solution)/shard_map/ppermute | solution.py:429
  26.8 0.0 collective-permute-done.4.refs_1_
  26.8 6.1 %collective-permute-start.8 = (f32[4,256]{1,0:T(4,128)S(1)}, f32[4,256]{1,0:T(4,128)S(1)}, u32[]{:S(2)}, u32[]{:S(2)}) collective-permute-start(f32[4,256]{1,0:T(4,128)S(1)} %get-tuple-element.55), channel_id=1, source_target_pairs={{4,0},{8,4},{12,8},{16,12},{20,16},{24,20},{28,24},{32,28},{36,32}... | collective-permute-start | bytes 12296 | tf_op jit(solution)/shard_map/ppermute | solution.py:428
  32.9 0.0 collective-permute-done.5.refs_2_
  32.9 2.3 %collective-permute-start.12 = (f32[512,128]{1,0:T(8,128)S(1)}, f32[512,128]{1,0:T(8,128)S(1)}, u32[]{:S(2)}, u32[]{:S(2)}) collective-permute-start(f32[512,128]{1,0:T(8,128)S(1)} %get-tuple-element.63), channel_id=1, source_target_pairs={{0,2},{1,3},{2,0},{3,1},{4,6},{5,7},{6,4},{7,5},{8,10},{9,11},{10,... | collective-permute-start | bytes 786440 | tf_op jit(solution)/shard_map/ppermute | solution.py:365
  35.2 0.0 collective-permute-done.6.refs_3_
  35.2 0.8 %collective-permute-start.13 = (f32[512,128]{1,0:T(8,128)S(1)}, f32[512,128]{1,0:T(8,128)S(1)}, u32[]{:S(2)}, u32[]{:S(2)}) collective-permute-start(f32[512,128]{1,0:T(8,128)S(1)} %get-tuple-element.64), channel_id=1, source_target_pairs={{0,1},{1,2},{2,3},{3,0},{4,5},{5,6},{6,7},{7,4},{8,9},{9,10},{10,1... | collective-permute-start | bytes 786440 | tf_op jit(solution)/shard_map/ppermute | solution.py:365
  36.0 0.0 copy-done.3
  36.1 0.0 copy-start.1
  36.1 0.0 copy-start.2
  36.1 3.4 %known.1 = (f32[4,256,256]{2,1,0:T(8,128)S(1)}, f32[4,256,256]{2,1,0:T(8,128)S(1)}, f32[4,256,256]{2,1,0:T(8,128)S(1)}, f32[8,256]{1,0:T(8,128)S(1)}) custom-call(s32[16]{0:T(128)S(1)} %copy-done.4, f32[512,128]{1,0:T(8,128)S(1)} %get-tuple-element.47.behind_ref.refs_0_, f32[12,256]{1,0:T(8,128)S(1)} %collective-permute-done.strip_ref, ...), custom_call_target="tpu_custom_call" | custom-call | bytes 15000000 | tf_op jit(solution)/shard_map/known/pallas_call | solution.py:432
  39.4 3.2 %friction_lower.1 = (f32[512,128]{1,0:T(8,128)S(1)}, f32[512,128]{1,0:T(8,128)S(1)}, f32[512,128]{1,0:T(8,128)S(1)}, f32[512,128]{1,0:T(8,128)S(1)}, f32[24,256]{1,0:T(8,128)S(1)}) custom-call(bf16[128,96]{1,0:T(8,128)(2,1)S(1)} %get-tuple-element.38.forward_ref, bf16[64,256]{1,0:T(8,128)(2,1)S(1)} %get-tuple-element.39.backward_ref, ...), custom_call_target="tpu_custom_call" | custom-call | bytes 12000000 | tf_op jit(solution)/shard_map/friction_lower/pallas_call | solution.py:442
  42.7 0.0 collective-permute-done.7.before_ref
  42.7 2.5 %collective-permute-start.14 = (f32[512,128]{1,0:T(8,128)S(1)}, f32[512,128]{1,0:T(8,128)S(1)}, u32[]{:S(2)}, u32[]{:S(2)}) collective-permute-start(f32[512,128]{1,0:T(8,128)S(1)} %get-tuple-element.68), channel_id=1, source_target_pairs={{0,3},{1,0},{2,1},{3,2},{4,7},{5,4},{6,5},{7,6},{8,11},{9,8},{10,9... | collective-permute-start | bytes 786440 | tf_op jit(solution)/shard_map/ppermute | solution.py:365
  45.2 0.0 collective-permute-done.8.after_ref
  45.2 0.1 collective-permute-start.15
  45.3 0.0 collective-permute-done.11.refs_1_
  45.3 0.9 %collective-permute-start.16 = (f32[512,128]{1,0:T(8,128)S(1)}, f32[512,128]{1,0:T(8,128)S(1)}, u32[]{:S(2)}, u32[]{:S(2)}) collective-permute-start(f32[512,128]{1,0:T(8,128)S(1)} %get-tuple-element.70), channel_id=1, source_target_pairs={{0,1},{1,2},{2,3},{3,0},{4,5},{5,6},{6,7},{7,4},{8,9},{9,10},{10,1... | collective-permute-start | bytes 786440 | tf_op jit(solution)/shard_map/ppermute | solution.py:365
  46.2 0.0 copy-done.1
  46.2 0.0 copy-done.2
  46.2 0.0 collective-permute-done.12.refs_2_
  46.2 1.9 %collective-permute-start.9 = (f32[4,256]{1,0:T(4,128)S(1)}, f32[4,256]{1,0:T(4,128)S(1)}, u32[]{:S(2)}, u32[]{:S(2)}) collective-permute-start(f32[4,256]{1,0:T(4,128)S(1)} %get-tuple-element.57), channel_id=1, source_target_pairs={{0,4},{4,8},{8,12},{12,16},{16,20},{20,24},{24,28},{28,32},{32,36}... | collective-permute-start | bytes 12296 | tf_op jit(solution)/shard_map/ppermute | solution.py:464
  48.1 0.7 %collective-permute-done.13.refs_3_ = f32[512,128]{1,0:T(8,128)S(1)} collective-permute-done((f32[512,128]{1,0:T(8,128)S(1)}, f32[512,128]{1,0:T(8,128)S(1)}, u32[]{:S(2)}, u32[]{:S(2)}) %collective-permute-start.13) | collective-permute-done | bytes 262176 | tf_op jit(solution)/shard_map/ppermute | solution.py:365
  48.9 5.3 %collective-permute-start.10 = (f32[4,256]{1,0:T(4,128)S(1)}, f32[4,256]{1,0:T(4,128)S(1)}, u32[]{:S(2)}, u32[]{:S(2)}) collective-permute-start(f32[4,256]{1,0:T(4,128)S(1)} %get-tuple-element.58), channel_id=1, source_target_pairs={{4,0},{8,4},{12,8},{16,12},{20,16},{24,20},{28,24},{32,28},{36,32}... | collective-permute-start | bytes 12296 | tf_op jit(solution)/shard_map/ppermute | solution.py:463
  54.2 1.8 %finish_upper.1 = (f32[1,3,4,256,256]{4,3,2,1,0:T(8,128)}, f32[2,4,32,256]{3,2,1,0:T(8,128)S(1)}) custom-call(f32[24,256]{1,0:T(8,128)S(1)} %get-tuple-element.53.extra_ref, f32[1,256,256]{2,1,0:T(8,128)S(1)} %copy-done.1, s32[1,256,256]{2,1,0:T(8,128)S(1)} %copy-done.2, f32[4,256,256]{2,1,0:T(8,128)S(1)} %get-tuple-element.59.east_ref, ...), custom_call_target="tpu_custom_call" | custom-call | bytes 9000000 | tf_op jit(solution)/shard_map/finish_upper/pallas_call | solution.py:467
  56.0 0.0 collective-permute-done.9.before_ref
  56.0 0.0 collective-permute-done.10.after_ref
  56.0 0.0 collective-permute-done.14.refs_1_
  56.0 0.0 collective-permute-done.15.refs_2_
  56.0 2.8 %collective-permute-done.16.refs_3_ = f32[512,128]{1,0:T(8,128)S(1)} collective-permute-done((f32[512,128]{1,0:T(8,128)S(1)}, f32[512,128]{1,0:T(8,128)S(1)}, u32[]{:S(2)}, u32[]{:S(2)}) %collective-permute-start.16) | collective-permute-done | bytes 262176 | tf_op jit(solution)/shard_map/ppermute | solution.py:365
  58.9 2.0 %finish_lower.1 = f32[1,3,4,256,256]{4,3,2,1,0:T(8,128)} custom-call(f32[24,256]{1,0:T(8,128)S(1)} %get-tuple-element.53.extra_ref, f32[8,256]{1,0:T(8,128)S(1)} %get-tuple-element.56.edge_ref, f32[4,256]{1,0:T(4,128)S(1)} %collective-permute-done.9.before_ref, f32[4,256]{1,0:T(4,128)S(1)} %collective-permute-done.10.after_ref, ...), custom_call_target="tpu_custom_call", output_to_operand_aliasing={{}: (10, {})} | custom-call | bytes 9000000 | tf_op jit(solution)/shard_map/finish_lower/pallas_call | solution.py:481
  (1 shorter events, 0.0 us)
Async XLA Ops:
  0.0 7.4 %copy-start = (f32[1,3,4,256,256]{4,3,2,1,0:T(8,128)S(1)}, f32[1,3,4,256,256]{4,3,2,1,0:T(8,128)}, u32[]{:S(2)}) copy-start(f32[1,3,4,256,256]{4,3,2,1,0:T(8,128)} %state_ref.3) | copy-start | bytes 9437188
  0.0 7.4 %copy-start.4 = (s32[16]{0:T(128)S(1)}, s32[16]{0:T(128)}, u32[]{:S(2)}) copy-start(s32[16]{0:T(128)} %freq_ref.3) | copy-start | bytes 196
  0.0 7.4 %copy-start.5 = (s32[256]{0:T(256)S(1)}, s32[256]{0:T(256)}, u32[]{:S(2)}) copy-start(s32[256]{0:T(256)} %param.10) | copy-start | bytes 3076
  1.7 12.3 %collective-permute-start.1 = (f32[512,128]{1,0:T(8,128)S(1)}, f32[512,128]{1,0:T(8,128)S(1)}, u32[]{:S(2)}, u32[]{:S(2)}) collective-permute-start(f32[512,128]{1,0:T(8,128)S(1)} %get-tuple-element.44), channel_id=1, source_target_pairs={{0,1},{1,2},{2,3},{3,0},{4,5},{5,6},{6,7},{7,4},{8,9},{9,10},{10,1... | collective-permute-start | bytes 786440 | tf_op jit(solution)/shard_map/ppermute | solution.py:365
  3.2 15.5 %collective-permute-start.2 = (f32[512,128]{1,0:T(8,128)S(1)}, f32[512,128]{1,0:T(8,128)S(1)}, u32[]{:S(2)}, u32[]{:S(2)}) collective-permute-start(f32[512,128]{1,0:T(8,128)S(1)} %get-tuple-element.45), channel_id=1, source_target_pairs={{0,2},{1,3},{2,0},{3,1},{4,6},{5,7},{6,4},{7,5},{8,10},{9,11},{10,... | collective-permute-start | bytes 786440 | tf_op jit(solution)/shard_map/ppermute | solution.py:365
  6.0 12.8 %collective-permute-start.3 = (f32[512,128]{1,0:T(8,128)S(1)}, f32[512,128]{1,0:T(8,128)S(1)}, u32[]{:S(2)}, u32[]{:S(2)}) collective-permute-start(f32[512,128]{1,0:T(8,128)S(1)} %get-tuple-element.46), channel_id=1, source_target_pairs={{0,3},{1,0},{2,1},{3,2},{4,7},{5,4},{6,5},{7,6},{8,11},{9,8},{10,9... | collective-permute-start | bytes 786440 | tf_op jit(solution)/shard_map/ppermute | solution.py:365
  7.4 28.7 %copy-start.3 = (f32[1,2,4,256,256]{4,3,2,1,0:T(8,128)S(1)}, f32[1,2,4,256,256]{4,3,2,1,0:T(8,128)}, u32[]{:S(2)}) copy-start(f32[1,2,4,256,256]{4,3,2,1,0:T(8,128)} %forcing_ref.1) | copy-start | bytes 6291460
  9.9 2.1 %collective-permute-start = (f32[12,256]{1,0:T(8,128)S(1)}, f32[12,256]{1,0:T(8,128)S(1)}, u32[]{:S(2)}, u32[]{:S(2)}) collective-permute-start(f32[12,256]{1,0:T(8,128)S(1)} %get-tuple-element.40), channel_id=1, source_target_pairs={{0,128},{1,129},{2,130},{3,131},{4,132},{5,133},{6,134},{7,135},{8... | collective-permute-start | bytes 36872 | tf_op jit(solution)/shard_map/ppermute | solution.py:398
  12.4 14.4 %collective-permute-start.4 = (f32[560,128]{1,0:T(8,128)S(1)}, f32[560,128]{1,0:T(8,128)S(1)}, u32[]{:S(2)}, u32[]{:S(2)}) collective-permute-start(f32[560,128]{1,0:T(8,128)S(1)} %get-tuple-element.50), channel_id=1, source_target_pairs={{0,1},{1,2},{2,3},{3,0},{4,5},{5,6},{6,7},{7,4},{8,9},{9,10},{10,1... | collective-permute-start | bytes 860168 | tf_op jit(solution)/shard_map/ppermute | solution.py:365
  13.0 19.9 %collective-permute-start.5 = (f32[560,128]{1,0:T(8,128)S(1)}, f32[560,128]{1,0:T(8,128)S(1)}, u32[]{:S(2)}, u32[]{:S(2)}) collective-permute-start(f32[560,128]{1,0:T(8,128)S(1)} %get-tuple-element.51), channel_id=1, source_target_pairs={{0,2},{1,3},{2,0},{3,1},{4,6},{5,7},{6,4},{7,5},{8,10},{9,11},{10,... | collective-permute-start | bytes 860168 | tf_op jit(solution)/shard_map/ppermute | solution.py:365
  13.9 21.3 %collective-permute-start.6 = (f32[560,128]{1,0:T(8,128)S(1)}, f32[560,128]{1,0:T(8,128)S(1)}, u32[]{:S(2)}, u32[]{:S(2)}) collective-permute-start(f32[560,128]{1,0:T(8,128)S(1)} %get-tuple-element.52), channel_id=1, source_target_pairs={{0,3},{1,0},{2,1},{3,2},{4,7},{5,4},{6,5},{7,6},{8,11},{9,8},{10,9... | collective-permute-start | bytes 860168 | tf_op jit(solution)/shard_map/ppermute | solution.py:365
  21.6 23.6 %collective-permute-start.11 = (f32[512,128]{1,0:T(8,128)S(1)}, f32[512,128]{1,0:T(8,128)S(1)}, u32[]{:S(2)}, u32[]{:S(2)}) collective-permute-start(f32[512,128]{1,0:T(8,128)S(1)} %get-tuple-element.62), channel_id=1, source_target_pairs={{0,3},{1,0},{2,1},{3,2},{4,7},{5,4},{6,5},{7,6},{8,11},{9,8},{10,9... | collective-permute-start | bytes 786440 | tf_op jit(solution)/shard_map/ppermute | solution.py:365
  22.9 19.7 %collective-permute-start.7 = (f32[4,256]{1,0:T(4,128)S(1)}, f32[4,256]{1,0:T(4,128)S(1)}, u32[]{:S(2)}, u32[]{:S(2)}) collective-permute-start(f32[4,256]{1,0:T(4,128)S(1)} %get-tuple-element.54), channel_id=1, source_target_pairs={{0,4},{4,8},{8,12},{12,16},{16,20},{20,24},{24,28},{28,32},{32,36}... | collective-permute-start | bytes 12296 | tf_op jit(solution)/shard_map/ppermute | solution.py:429
  26.8 18.4 %collective-permute-start.8 = (f32[4,256]{1,0:T(4,128)S(1)}, f32[4,256]{1,0:T(4,128)S(1)}, u32[]{:S(2)}, u32[]{:S(2)}) collective-permute-start(f32[4,256]{1,0:T(4,128)S(1)} %get-tuple-element.55), channel_id=1, source_target_pairs={{4,0},{8,4},{12,8},{16,12},{20,16},{24,20},{28,24},{32,28},{36,32}... | collective-permute-start | bytes 12296 | tf_op jit(solution)/shard_map/ppermute | solution.py:428
  32.9 13.3 %collective-permute-start.12 = (f32[512,128]{1,0:T(8,128)S(1)}, f32[512,128]{1,0:T(8,128)S(1)}, u32[]{:S(2)}, u32[]{:S(2)}) collective-permute-start(f32[512,128]{1,0:T(8,128)S(1)} %get-tuple-element.63), channel_id=1, source_target_pairs={{0,2},{1,3},{2,0},{3,1},{4,6},{5,7},{6,4},{7,5},{8,10},{9,11},{10,... | collective-permute-start | bytes 786440 | tf_op jit(solution)/shard_map/ppermute | solution.py:365
  35.2 13.6 %collective-permute-start.13 = (f32[512,128]{1,0:T(8,128)S(1)}, f32[512,128]{1,0:T(8,128)S(1)}, u32[]{:S(2)}, u32[]{:S(2)}) collective-permute-start(f32[512,128]{1,0:T(8,128)S(1)} %get-tuple-element.64), channel_id=1, source_target_pairs={{0,1},{1,2},{2,3},{3,0},{4,5},{5,6},{6,7},{7,4},{8,9},{9,10},{10,1... | collective-permute-start | bytes 786440 | tf_op jit(solution)/shard_map/ppermute | solution.py:365
  36.1 10.1 %copy-start.1 = (f32[1,256,256]{2,1,0:T(8,128)S(1)}, f32[1,256,256]{2,1,0:T(8,128)}, u32[]{:S(2)}) copy-start(f32[1,256,256]{2,1,0:T(8,128)} %depth_ref.5) | copy-start | bytes 786436
  36.1 10.1 %copy-start.2 = (s32[1,256,256]{2,1,0:T(8,128)S(1)}, s32[1,256,256]{2,1,0:T(8,128)}, u32[]{:S(2)}) copy-start(s32[1,256,256]{2,1,0:T(8,128)} %wet_ref.5) | copy-start | bytes 786436
  42.7 13.3 %collective-permute-start.14 = (f32[512,128]{1,0:T(8,128)S(1)}, f32[512,128]{1,0:T(8,128)S(1)}, u32[]{:S(2)}, u32[]{:S(2)}) collective-permute-start(f32[512,128]{1,0:T(8,128)S(1)} %get-tuple-element.68), channel_id=1, source_target_pairs={{0,3},{1,0},{2,1},{3,2},{4,7},{5,4},{6,5},{7,6},{8,11},{9,8},{10,9... | collective-permute-start | bytes 786440 | tf_op jit(solution)/shard_map/ppermute | solution.py:365
  45.2 10.8 %collective-permute-start.15 = (f32[512,128]{1,0:T(8,128)S(1)}, f32[512,128]{1,0:T(8,128)S(1)}, u32[]{:S(2)}, u32[]{:S(2)}) collective-permute-start(f32[512,128]{1,0:T(8,128)S(1)} %get-tuple-element.69), channel_id=1, source_target_pairs={{0,2},{1,3},{2,0},{3,1},{4,6},{5,7},{6,4},{7,5},{8,10},{9,11},{10,... | collective-permute-start | bytes 786440 | tf_op jit(solution)/shard_map/ppermute | solution.py:365
  45.3 13.6 %collective-permute-start.16 = (f32[512,128]{1,0:T(8,128)S(1)}, f32[512,128]{1,0:T(8,128)S(1)}, u32[]{:S(2)}, u32[]{:S(2)}) collective-permute-start(f32[512,128]{1,0:T(8,128)S(1)} %get-tuple-element.70), channel_id=1, source_target_pairs={{0,1},{1,2},{2,3},{3,0},{4,5},{5,6},{6,7},{7,4},{8,9},{9,10},{10,1... | collective-permute-start | bytes 786440 | tf_op jit(solution)/shard_map/ppermute | solution.py:365
  46.2 9.8 %collective-permute-start.9 = (f32[4,256]{1,0:T(4,128)S(1)}, f32[4,256]{1,0:T(4,128)S(1)}, u32[]{:S(2)}, u32[]{:S(2)}) collective-permute-start(f32[4,256]{1,0:T(4,128)S(1)} %get-tuple-element.57), channel_id=1, source_target_pairs={{0,4},{4,8},{8,12},{12,16},{16,20},{20,24},{24,28},{28,32},{32,36}... | collective-permute-start | bytes 12296 | tf_op jit(solution)/shard_map/ppermute | solution.py:464
  48.9 7.2 %collective-permute-start.10 = (f32[4,256]{1,0:T(4,128)S(1)}, f32[4,256]{1,0:T(4,128)S(1)}, u32[]{:S(2)}, u32[]{:S(2)}) collective-permute-start(f32[4,256]{1,0:T(4,128)S(1)} %get-tuple-element.58), channel_id=1, source_target_pairs={{4,0},{8,4},{12,8},{16,12},{20,16},{24,20},{28,24},{32,28},{36,32}... | collective-permute-start | bytes 12296 | tf_op jit(solution)/shard_map/ppermute | solution.py:463
